TPU v7x, 512 devices: a whole 4x4x16 slice. The times are simulated.
512 devices in a mesh: dp: 64 (over z, x_hi, core), blk: 8 (over x_lo, y).
Axes of the slice: x: 4 (x_hi: 2, x_lo: 2; x = x_hi * 2 + x_lo), y: 4, z: 16, core: 2. Of those that a mesh axis runs over, the one named last changes fastest.
Arguments:
- tokens: bfloat16 [32768, 8192], P('dp', 'blk'), may hold values from -6 to 6
- up_right: bfloat16 [64, 128, 128], P('blk'), may hold values from -0.5 to 0.5
- up_left: bfloat16 [64, 128, 512], P('blk'), may hold values from -0.5 to 0.5
- down_right: bfloat16 [64, 512, 128], P('blk'), may hold values from -0.25 to 0.25
- down_left: bfloat16 [64, 128, 128], P('blk'), may hold values from -0.5 to 0.5
- cotangent: bfloat16 [32768, 8192], P('dp', 'blk'), may hold values from -6 to 6
Outputs:
- layer_out: bfloat16 [32768, 8192], P('dp', 'blk')
- input_grad: bfloat16 [32768, 8192], P('dp', 'blk')
- up_left_grad: float32 [64, 128, 512], P('blk', 'dp')
- down_left_grad: float32 [64, 128, 128], P('blk', 'dp')
All inputs are finite; a program needn't handle non-finite values.
Results may differ from a plain program's by a relative error of at most 0.0068.
Values may be sent and summed in bfloat16 or wider, within the bound.
No kernel may reach another device: no remote copies, remote signals or barrier semaphores. Data moves between devices by JAX's collectives and lax.ppermute only.
A program may use at most 64 MiB of HBM per device.

v0:
```python
import math

import jax
import jax.numpy as jnp
from jax import lax
from jax.sharding import PartitionSpec as P

BIN = 128
BHID = 512
MIX = 2


def on_device(tokens, up_right, up_left, down_right, down_left, cotangent):
    bf16 = jnp.bfloat16
    f32 = jnp.float32
    groups = lax.axis_size("blk")
    shard_rows = tokens.shape[0]
    owned = up_right.shape[0]
    factor = 1.0 / math.sqrt(shard_rows * lax.axis_size("dp"))
    inputs = tokens.reshape(shard_rows, owned, BIN)
    right_split = up_right.reshape(owned, BIN, groups, owned, MIX)
    outbound = jnp.einsum(
        "tki,kinjm->njkmt", inputs, right_split, preferred_element_type=f32
    ).astype(bf16)
    down_split = down_right.reshape(owned, BHID, groups, owned, MIX)
    mixed = lax.all_to_all(outbound, "blk", split_axis=0, concat_axis=2, tiled=True)
    members = mixed.shape[4]
    mixed_in = mixed.reshape(owned, BIN, members)
    before = jnp.einsum("jct,jch->jht", mixed_in, up_left, preferred_element_type=f32)
    hidden = jax.nn.gelu(before).astype(bf16)
    leaving = jnp.einsum("jht,jhnkm->nkjmt", hidden, down_split, preferred_element_type=f32).astype(
        bf16
    )
    mixed, before_saved, leaving = (mixed, before.reshape(1, owned, BHID, 1, members), leaving)
    arrived = lax.all_to_all(leaving, "blk", split_axis=0, concat_axis=2, tiled=True)
    mixed_down = arrived.reshape(owned, BIN, shard_rows)
    layer_out = jnp.einsum("kct,kco->tko", mixed_down, down_left, preferred_element_type=f32)
    layer_out = layer_out.astype(bf16).reshape(shard_rows, owned * BIN)
    upstream = cotangent.reshape(shard_rows, owned, BIN)
    left_split = down_left.reshape(owned, groups, owned, MIX, BIN)
    back_out = jnp.einsum(
        "tko,knjmo->njkmt", upstream, left_split, preferred_element_type=f32
    ).astype(bf16)
    down_part = (
        jnp.einsum("kct,tko->kco", mixed_down, upstream, preferred_element_type=f32) * factor
    )
    back_in = lax.all_to_all(back_out, "blk", split_axis=0, concat_axis=2, tiled=True)
    grad_z = back_in.reshape(owned, BIN, shard_rows)
    before = before_saved.reshape(owned, BHID, shard_rows)
    mixed_in = mixed.reshape(owned, BIN, shard_rows)
    grad_hidden = jnp.einsum("jot,jho->jht", grad_z, down_right, preferred_element_type=f32)
    unused, gelu_back = jax.vjp(jax.nn.gelu, before)
    grad_pre = gelu_back(grad_hidden)[0].astype(bf16)
    up_part = jnp.einsum("jct,jht->jch", mixed_in, grad_pre, preferred_element_type=f32) * factor
    left_back = up_left.reshape(owned, groups, owned, MIX, BHID)
    returning = jnp.einsum(
        "jht,jnkmh->nkjmt", grad_pre, left_back, preferred_element_type=f32
    ).astype(bf16)
    gathered = lax.all_to_all(returning, "blk", split_axis=0, concat_axis=2, tiled=True)
    members = gathered.shape[4]
    grad_u = gathered.reshape(owned, BIN, members)
    grad_in = jnp.einsum("kot,kio->tki", grad_u, up_right, preferred_element_type=f32)
    input_grad = grad_in.astype(bf16).reshape(members, owned * BIN)
    up_grad, down_grad = (
        lax.psum_scatter(up_part, "dp", scatter_dimension=1, tiled=True),
        lax.psum_scatter(down_part, "dp", scatter_dimension=1, tiled=True),
    )
    return (layer_out, input_grad, up_grad, down_grad)


def solution(mesh):
    placed = (
        P("dp", "blk"),
        P("blk", None, None),
        P("blk", None, None),
        P("blk", None, None),
        P("blk", None, None),
        P("dp", "blk"),
    )
    return jax.shard_map(
        on_device,
        mesh=mesh,
        in_specs=placed,
        out_specs=(P("dp", "blk"), P("dp", "blk"), P("blk", "dp", None), P("blk", "dp", None)),
        check_vma=False,
    )
```

profile of v0, /device:TPU:8, one launch (start us, length us, event | category | flops | bytes accessed | tf_op | source)
XLA Modules:
  0.0 503.2 jit_solution(13384082901368557278)
XLA Ops:
  7.2 1.2 copy.49
  8.4 1.5 copy.93
  10.4 1.1 copy.52
  11.4 9.3 %all-to-all-start = ((bf16[8,8,8,2,512]{4,1,3,2,0:T(8,128)(2,1)}), bf16[8,8,8,2,512]{4,1,3,2,0:T(8,128)(2,1)S(1)}, u32[]{:S(2)}, u32[]{:S(2)}) async-start(bf16[8,8,8,2,512]{4,1,3,2,0:T(8,128)(2,1)} %copy.52), calls=%async_computation | async-start | bytes 2097152 | tf_op jit(solution)/shard_map/all_to_all | solution.py:26
  20.7 1.9 copy.54
  22.6 8.3 %all-to-all-done = bf16[8,8,8,2,512]{4,1,3,2,0:T(8,128)(2,1)S(1)} async-done(((bf16[8,8,8,2,512]{4,1,3,2,0:T(8,128)(2,1)}), bf16[8,8,8,2,512]{4,1,3,2,0:T(8,128)(2,1)S(1)}, u32[]{:S(2)}, u32[]{:S(2)}) %all-to-all-start) | async-done | bytes 1048608 | tf_op jit(solution)/shard_map/all_to_all | solution.py:26
  30.9 1.3 fusion.38
  32.2 3.5 fusion.22
  35.7 1.1 copy.57
  36.8 4.8 all-to-all-start.1
  41.6 1.5 copy.94
  43.6 1.0 copy.62
  44.6 9.6 %all-to-all-done.1 = bf16[8,8,8,2,512]{4,1,3,2,0:T(8,128)(2,1)S(1)} async-done(((bf16[8,8,8,2,512]{4,1,3,2,0:T(8,128)(2,1)}), bf16[8,8,8,2,512]{4,1,3,2,0:T(8,128)(2,1)S(1)}, u32[]{:S(2)}, u32[]{:S(2)}) %all-to-all-start.1) | async-done | bytes 1048608 | tf_op jit(solution)/shard_map/all_to_all | solution.py:35
  54.2 5.3 %all-to-all-start.2 = ((bf16[8,8,8,2,512]{4,1,3,2,0:T(8,128)(2,1)}), bf16[8,8,8,2,512]{4,1,3,2,0:T(8,128)(2,1)}, u32[]{:S(2)}, u32[]{:S(2)}) async-start(bf16[8,8,8,2,512]{4,1,3,2,0:T(8,128)(2,1)} %copy.62), calls=%async_computation.2 | async-start | bytes 2097152 | tf_op jit(solution)/shard_map/all_to_all | solution.py:47
  59.5 2.1 convolution_multiply_fusion.1
  61.5 1.1 copy.73
  62.9 10.0 %all-to-all-done.2 = bf16[8,8,8,2,512]{4,1,3,2,0:T(8,128)(2,1)} async-done(((bf16[8,8,8,2,512]{4,1,3,2,0:T(8,128)(2,1)}), bf16[8,8,8,2,512]{4,1,3,2,0:T(8,128)(2,1)}, u32[]{:S(2)}, u32[]{:S(2)}) %all-to-all-start.2) | async-done | bytes 1048608 | tf_op jit(solution)/shard_map/all_to_all | solution.py:47
  72.9 9.1 %fusion.6 = bf16[8,512,512]{1,2,0:T(8,128)(2,1)S(1)} fusion(f32[8,512,512]{2,1,0:T(8,128)} %copy-done.1, bf16[8,512,128]{2,1,0:T(8,128)(2,1)} %param.9, bf16[8,128,512]{2,0,1:T(8,128)(2,1)} %bitcast.20), kind=kOutput, calls=%fused_computation.8 | convolution fusion | flops 578813952 | bytes 14680064 | tf_op jit(solution)/shard_map/jot,jho->jht/dot_general | solution.py:51
  82.0 1.0 convolution_multiply_fusion
  83.0 0.9 copy-done
  83.9 2.5 copy.70
  86.5 1.2 reshape.58
  87.7 4.0 fusion.27
  91.8 18.7 %all_to_all.60 = bf16[8,8,8,2,512]{4,1,3,2,0:T(8,128)(2,1)S(1)} all-to-all(bf16[8,8,8,2,512]{4,1,3,2,0:T(8,128)(2,1)S(1)} %copy.66), channel_id=1, replica_groups=mesh['dp'=64,'blk'=8] {'blk'}, dimensions={0} | all-to-all | bytes 2097152 | tf_op jit(solution)/shard_map/all_to_all | solution.py:59
  110.6 0.8 convolution_convert_fusion
  111.4 1.3 copy.75
  112.7 0.9 convolution_convert_fusion.2
  113.6 1.3 copy.74
  114.9 164.3 %reduce-scatter.5.cloned.1.call-done = f32[8,2,128]{2,0,1:T(8,128)} async-done(((f32[8,128,128]{2,0,1:T(8,128)}), f32[8,2,128]{2,0,1:T(8,128)}) %reduce-scatter.5.cloned.1.call-update) | async-done | bytes 8208 | tf_op jit(solution)/shard_map/reduce_scatter | solution.py:66
  279.2 1.3 copy.77
  280.5 214.5 %reduce-scatter.3.cloned.1.call-done = f32[8,2,512]{2,0,1:T(8,128)} async-done(((f32[8,128,512]{2,0,1:T(8,128)}), f32[8,2,512]{2,0,1:T(8,128)}) %reduce-scatter.3.cloned.1.call-update) | async-done | bytes 32784 | tf_op jit(solution)/shard_map/reduce_scatter | solution.py:65
  495.0 1.4 copy.76
  (16 shorter events, 1.3 us)
Async XLA Ops:
  7.2 23.7 %copy-start.2 = (bf16[8,128,512]{2,1,0:T(8,128)(2,1)S(1)}, bf16[8,128,512]{2,1,0:T(8,128)(2,1)}, u32[]{:S(2)}) copy-start(bf16[8,128,512]{2,1,0:T(8,128)(2,1)} %param.8) | copy-start | bytes 3145732
  11.4 19.5 %all-to-all-start = ((bf16[8,8,8,2,512]{4,1,3,2,0:T(8,128)(2,1)}), bf16[8,8,8,2,512]{4,1,3,2,0:T(8,128)(2,1)S(1)}, u32[]{:S(2)}, u32[]{:S(2)}) async-start(bf16[8,8,8,2,512]{4,1,3,2,0:T(8,128)(2,1)} %copy.52), calls=%async_computation | async-start | bytes 2097152 | tf_op jit(solution)/shard_map/all_to_all | solution.py:26
  32.2 3.5 copy-start.1
  32.2 10.9 %copy-start.3 = (bf16[8,128,128]{2,1,0:T(8,128)(2,1)S(1)}, bf16[8,128,128]{2,1,0:T(8,128)(2,1)}, u32[]{:S(2)}) copy-start(bf16[8,128,128]{2,1,0:T(8,128)(2,1)} %param.10) | copy-start | bytes 786436
  36.8 17.4 %all-to-all-start.1 = ((bf16[8,8,8,2,512]{4,1,3,2,0:T(8,128)(2,1)}), bf16[8,8,8,2,512]{4,1,3,2,0:T(8,128)(2,1)S(1)}, u32[]{:S(2)}, u32[]{:S(2)}) async-start(bf16[8,8,8,2,512]{4,1,3,2,0:T(8,128)(2,1)} %copy.57), calls=%async_computation.1 | async-start | bytes 2097152 | tf_op jit(solution)/shard_map/all_to_all | solution.py:35
  54.2 18.7 %all-to-all-start.2 = ((bf16[8,8,8,2,512]{4,1,3,2,0:T(8,128)(2,1)}), bf16[8,8,8,2,512]{4,1,3,2,0:T(8,128)(2,1)}, u32[]{:S(2)}, u32[]{:S(2)}) async-start(bf16[8,8,8,2,512]{4,1,3,2,0:T(8,128)(2,1)} %copy.62), calls=%async_computation.2 | async-start | bytes 2097152 | tf_op jit(solution)/shard_map/all_to_all | solution.py:47
  59.5 219.7 %reduce-scatter.5.cloned.1.call-start = ((), (), s32[]{:S(2)}) async-start(), calls=%async_computation.7 | async-start | bytes 532480 | tf_op jit(solution)/shard_map/reduce_scatter | solution.py:66
  62.7 432.3 %reduce-scatter.3.cloned.1.call-start = ((), (), s32[]{:S(2)}) async-start(), calls=%async_computation.6 | async-start | bytes 2129920 | tf_op jit(solution)/shard_map/reduce_scatter | solution.py:65
  82.0 2.0 copy-start
  86.5 24.1 %copy-start.4 = (bf16[8,128,128]{2,1,0:T(8,128)(2,1)S(1)}, bf16[8,128,128]{2,1,0:T(8,128)(2,1)}, u32[]{:S(2)}) copy-start(bf16[8,128,128]{2,1,0:T(8,128)(2,1)} %param.7) | copy-start | bytes 786436
Sparse Core Ops, SparseCore 0:
  64.8 214.2 reduce-scatter.4
  283.8 211.1 reduce-scatter.2
where the time goes:
time: 504 us; the launch traced here: 503 us
  waiting for transfers between devices  407 us (81%)
  matrix products  23.6 us (5%)
  local copies, waits for them, and re-layouts  20.5 us (4%)
  starting transfers between devices  19.6 us (4%)
  blocking collectives  18.7 us (4%)
  between operations  14.2 us (3%)
    reduce_scatter x1, waiting for transfers between devices, on_device(): lax.psum_scatter(up_part, 'dp', scatter_dimension=1, tiled=True)  215 us
    reduce_scatter x1, waiting for transfers between devices, on_device(): lax.psum_scatter(down_part, 'dp', scatter_dimension=1, tiled=True)  164 us
    all_to_all x1, blocking collectives, on_device(): lax.all_to_all(returning, 'blk', split_axis=0, concat_axis=2, tiled=True)  18.7 us
    unnamed x18, local copies, waits for them, and re-layouts  12.3 us
  transfers between devices with their start and end apart: 5, of which 5 were waited for; matrix products, arithmetic and copies ran while one was open for 6% of the time, Pallas kernels for 0%

commit v1 on v0

v1 whole, which is shorter than its diff:
```python
import functools
import math

import jax
import jax.numpy as jnp
from jax import lax
from jax.experimental import pallas as pl
from jax.experimental.pallas import tpu as pltpu
from jax.sharding import PartitionSpec as P

GROUPS = 8
OWNED = 8
BIN = 128
BHID = 512
ROWS = 512
PIECE = 16
MIB = 1 << 20
BF16 = jnp.bfloat16
F32 = jnp.float32

NN = (((1,), (0,)), ((), ()))
NT = (((1,), (1,)), ((), ()))
TN = (((0,), (0,)), ((), ()))
TT = (((0,), (1,)), ((), ()))


def dot(a, b, dims):
    return lax.dot_general(a, b, dims, preferred_element_type=F32)


def swap_matrix():
    to = lax.broadcasted_iota(jnp.int32, (BIN, BIN), 0)
    come = lax.broadcasted_iota(jnp.int32, (BIN, BIN), 1)
    wanted = ((to & 14) << 3) | ((to >> 4) << 1) | (to & 1)
    return jnp.where(come == wanted, 1.0, 0.0).astype(BF16)


def shard_matrix(core, xhi):
    to = lax.broadcasted_iota(jnp.int32, (BIN, BIN), 0)
    come = lax.broadcasted_iota(jnp.int32, (BIN, BIN), 1)
    of_core = (1 - (to >> 6)) ^ core
    of_xhi = (1 - ((to >> 5) & 1)) ^ xhi
    wanted = (((to >> 1) & 15) << 3) | (of_xhi << 2) | (of_core << 1) | (to & 1)
    return jnp.where(come == wanted, 1.0, 0.0).astype(BF16)


def scatter_rows(out_ref, block, value):
    at = pl.multiple_of(block * PIECE, PIECE)
    for n in range(GROUPS):
        out_ref[n, pl.ds(at, PIECE), :] = value[n * PIECE : (n + 1) * PIECE, :]


def gather_rows(msg_ref, held_ref):
    swap = swap_matrix()
    for src in range(GROUPS):
        swapped = dot(swap, msg_ref[src], NN).astype(BF16)
        for b in range(OWNED):
            held_ref[b, src * PIECE : (src + 1) * PIECE, :] = swapped[b * PIECE : (b + 1) * PIECE, :]


def right_kernel(dims, x_ref, w_ref, out_ref):
    for k in range(OWNED):
        value = dot(w_ref[k], x_ref[:, k * BIN : (k + 1) * BIN], dims).astype(BF16)
        scatter_rows(out_ref, k, value)


def up_kernel(place_ref, msg_ref, left_ref, down_ref, out_ref, saved_ref, slope_ref, held_ref, shard_ref):
    j = pl.program_id(0)

    @pl.when(j == 0)
    def _():
        gather_rows(msg_ref, held_ref)
        shard_ref[...] = shard_matrix(place_ref[0], place_ref[1])

    v = held_ref[j]
    saved_ref[0] = dot(shard_ref[...], v, NN).astype(BF16)
    s = dot(left_ref[0], v, TN)
    c = math.sqrt(2.0 / math.pi)
    square = s * s
    th = jnp.tanh(s * (c + (c * 0.044715) * square))
    half = 0.5 + 0.5 * th
    hidden = (s * half).astype(BF16)
    slope = half + (0.5 * s) * ((1.0 - th * th) * (c + (3.0 * c * 0.044715) * square))
    slope_ref[0] = slope.astype(BF16)
    z = dot(down_ref[0], hidden, TN).astype(BF16)
    scatter_rows(out_ref, j, z)


def back_kernel(msg_ref, saved_ref, slope_ref, left_ref, down_ref, out_ref, send_ref, keep_ref, held_ref):
    j = pl.program_id(0)

    @pl.when(j == 0)
    def _():
        gather_rows(msg_ref, held_ref)

    grad_hidden = dot(down_ref[0], held_ref[j], NN)
    grad_pre = (grad_hidden * slope_ref[0].astype(F32)).astype(BF16)
    grad_v = dot(left_ref[0], grad_pre, NN).astype(BF16)
    scatter_rows(out_ref, j, grad_v)
    part = dot(saved_ref[0], grad_pre, NT)
    send_ref[...] = part[: BIN // 2].astype(BF16)
    keep_ref[...] = part[BIN // 2 :]


def out_kernel(place_ref, msg_ref, left_ref, cot_ref, out_ref, send_ref, keep_ref, held_ref):
    gather_rows(msg_ref, held_ref)
    shard = shard_matrix(place_ref[0], place_ref[1])
    for k in range(OWNED):
        cols = slice(k * BIN, (k + 1) * BIN)
        w = held_ref[k]
        part = dot(dot(shard, w, NN).astype(BF16), cot_ref[:, cols], NN)
        send_ref[:, cols] = part[: BIN // 2].astype(BF16)
        keep_ref[:, cols] = part[BIN // 2 :]
        out_ref[:, cols] = dot(w, left_ref[k], TN).astype(BF16)


def in_kernel(msg_ref, right_ref, out_ref, held_ref):
    gather_rows(msg_ref, held_ref)
    for k in range(OWNED):
        out_ref[:, k * BIN : (k + 1) * BIN] = dot(held_ref[k], right_ref[k], TT).astype(BF16)


VMEM = pl.BlockSpec(memory_space=pltpu.VMEM)
SMEM = pl.BlockSpec(memory_space=pltpu.SMEM)
MSG = (GROUPS, BIN, ROWS)


def params():
    return pltpu.CompilerParams(vmem_limit_bytes=40 * MIB)


def cost(mflop, mib, trans=0):
    return pl.CostEstimate(flops=mflop * 1000000, bytes_accessed=mib * MIB, transcendentals=trans)


def shape(dims, dtype):
    return jax.ShapeDtypeStruct(dims, dtype)


def right(x, w, dims):
    return pl.pallas_call(
        functools.partial(right_kernel, dims),
        out_shape=shape(MSG, BF16),
        in_specs=[VMEM, VMEM],
        out_specs=VMEM,
        compiler_params=params(),
        cost_estimate=cost(134, 3),
    )(x, w)


def whole(dims):
    return pl.BlockSpec(dims, lambda j: (0,) * len(dims))


def each(dims):
    return pl.BlockSpec((1,) + dims, lambda j: (j, 0, 0))


def up(place, msg, left, down):
    return pl.pallas_call(
        up_kernel,
        grid=(OWNED,),
        out_shape=[shape(MSG, BF16), shape((OWNED, BIN, ROWS), BF16), shape((OWNED, BHID, ROWS), BF16)],
        in_specs=[SMEM, whole(MSG), each((BIN, BHID)), each((BHID, BIN))],
        out_specs=[whole(MSG), each((BIN, ROWS)), each((BHID, ROWS))],
        scratch_shapes=[pltpu.VMEM((OWNED, BIN, ROWS), BF16), pltpu.VMEM((BIN, BIN), BF16)],
        compiler_params=params(),
        cost_estimate=cost(1300, 9, OWNED * BHID * ROWS),
    )(place, msg, left, down)


def back(msg, saved, slope, left, down):
    half = (BIN // 2, OWNED * BHID)
    flat = pl.BlockSpec((BIN // 2, BHID), lambda j: (0, j))
    return pl.pallas_call(
        back_kernel,
        grid=(OWNED,),
        out_shape=[shape(MSG, BF16), shape(half, BF16), shape(half, F32)],
        in_specs=[whole(MSG), each((BIN, ROWS)), each((BHID, ROWS)), each((BIN, BHID)), each((BHID, BIN))],
        out_specs=[whole(MSG), flat, flat],
        scratch_shapes=[pltpu.VMEM((OWNED, BIN, ROWS), BF16)],
        compiler_params=params(),
        cost_estimate=cost(1800, 11),
    )(msg, saved, slope, left, down)


def out(place, msg, left, cot):
    half = (BIN // 2, OWNED * BIN)
    return pl.pallas_call(
        out_kernel,
        out_shape=[shape((ROWS, OWNED * BIN), BF16), shape(half, BF16), shape(half, F32)],
        in_specs=[SMEM, VMEM, VMEM, VMEM],
        out_specs=[VMEM, VMEM, VMEM],
        scratch_shapes=[pltpu.VMEM((OWNED, BIN, ROWS), BF16)],
        compiler_params=params(),
        cost_estimate=cost(500, 4),
    )(place, msg, left, cot)


def into(msg, rightw):
    return pl.pallas_call(
        in_kernel,
        out_shape=shape((ROWS, OWNED * BIN), BF16),
        in_specs=[VMEM, VMEM],
        out_specs=VMEM,
        scratch_shapes=[pltpu.VMEM((OWNED, BIN, ROWS), BF16)],
        compiler_params=params(),
        cost_estimate=cost(300, 3),
    )(msg, rightw)


def exchange(msg):
    return lax.all_to_all(msg, "blk", split_axis=0, concat_axis=0, tiled=True)


def sum_over_dp(send, keep, width, factor):
    count = lax.axis_size("dp")
    depth = count // 4
    rows = keep.shape[0] // 2
    total = keep + lax.ppermute(send, "dp", [(d, d ^ 1) for d in range(count)]).astype(F32)
    far = lax.ppermute(total[:rows].astype(BF16), "dp", [(d, d ^ 2) for d in range(count)])
    total = (total[rows:] + far.astype(F32)).astype(BF16)
    lanes = [[z * 4 + low for z in range(depth)] for low in range(4)]
    pieces = lax.all_to_all(
        total.reshape(depth, rows // depth, -1), "dp", 0, 0, axis_index_groups=lanes, tiled=True
    )
    summed = jnp.sum(pieces.astype(F32), axis=0) * factor
    return summed.reshape(rows // depth, OWNED, width).transpose(1, 0, 2)


def on_device(tokens, up_right, up_left, down_right, down_left, cotangent):
    at = lax.axis_index("dp")
    place = jnp.stack([at & 1, (at >> 1) & 1]).astype(jnp.int32)
    factor = 1.0 / math.sqrt(tokens.shape[0] * lax.axis_size("dp"))
    v = exchange(right(tokens, up_right, TT))
    grad_z = exchange(right(cotangent, down_left, NT))
    z, saved, slope = up(place, v, up_left, down_right)
    w = exchange(z)
    grad_v, up_send, up_keep = back(grad_z, saved, slope, up_left, down_right)
    grad_u = exchange(grad_v)
    up_grad = sum_over_dp(up_send, up_keep, BHID, factor)
    layer_out, down_send, down_keep = out(place, w, down_left, cotangent)
    down_grad = sum_over_dp(down_send, down_keep, BIN, factor)
    input_grad = into(grad_u, up_right)
    return (layer_out, input_grad, up_grad, down_grad)


def solution(mesh):
    placed = (
        P("dp", "blk"),
        P("blk", None, None),
        P("blk", None, None),
        P("blk", None, None),
        P("blk", None, None),
        P("dp", "blk"),
    )
    return jax.shard_map(
        on_device,
        mesh=mesh,
        in_specs=placed,
        out_specs=(P("dp", "blk"), P("dp", "blk"), P("blk", "dp", None), P("blk", "dp", None)),
        check_vma=False,
    )
```

time: 504 us -> 144 us (0.29)
  waiting for transfers between devices: 407 us -> 41.1 us
  starting transfers between devices: 19.6 us -> 56 us
  matrix products: 23.6 us -> 0 us
  Pallas kernels: 0 us -> 23.2 us
  blocking collectives: 18.7 us -> 0 us
  between operations: 14.2 us -> 0.83 us
    reduce_scatter x2 -> x0, waiting for transfers between devices: 379 us -> none  [the longest x1 215 us: on_device(): lax.psum_scatter(up_part, 'dp', scatter_dimension=1, tiled=True)]
    all_to_all x3 -> x6, starting transfers between devices: 19.4 us -> 44.3 us  [the longest x4 25.6 us: exchange(): return lax.all_to_all(msg, 'blk', split_axis=0, concat_axis=0, tiled=True)]
    dot_general x10 -> x0, matrix products: 23.6 us -> none  [the longest x1 9.08 us: on_device(): jnp.einsum('jot,jho->jht', grad_z, down_right, preferred_element_type=f32)]
    pallas_call x0 -> x6, Pallas kernels: none -> 23.2 us  [the longest x1 8.63 us: up(): pl.pallas_call(up_kernel, grid=(OWNED,), out_shape=[shape(MSG, BF16), sha...]
    all_to_all x1 -> x0, blocking collectives: 18.7 us -> none  [on_device(): lax.all_to_all(returning, 'blk', split_axis=0, concat_axis=2, tiled=True)]
    ppermute x0 -> x4, starting transfers between devices: none -> 11.7 us  [the longest x2 7.35 us: sum_over_dp(): lax.ppermute(total[:rows].astype(BF16), 'dp', [(d, d ^ 2) for d in range(...]
    ppermute x0 -> x4, waiting for transfers between devices: none -> 7.48 us  [the longest x2 7.48 us: sum_over_dp(): lax.ppermute(total[:rows].astype(BF16), 'dp', [(d, d ^ 2) for d in range(...]
    all_to_all x3 -> x6, waiting for transfers between devices: 27.9 us -> 33.6 us  [the longest x2 24.8 us: sum_over_dp(): lax.all_to_all(total.reshape(depth, rows // depth, -1), 'dp', 0, 0, axis_...]
  transfers between devices with their start and end apart: 5 -> 10, of which waited for: 5 -> 4; matrix products, arithmetic and copies ran while one was open for 6% -> 3% of each run, Pallas kernels for 0% -> 15%
where the time goes in v1:
time: 144 us; the launch traced here: 143 us
  starting transfers between devices  56 us (39%)
  waiting for transfers between devices  41.1 us (29%)
  Pallas kernels  23.2 us (16%)
  local copies, waits for them, and re-layouts  18.8 us (13%)
  other arithmetic  3.13 us (2%)
    all_to_all x4, starting transfers between devices, exchange(): return lax.all_to_all(msg, 'blk', split_axis=0, concat_axis=0, tiled=True)  25.6 us
    all_to_all x2, waiting for transfers between devices, sum_over_dp(): lax.all_to_all(total.reshape(depth, rows // depth, -1), 'dp', 0, 0, axis_...  24.8 us
    all_to_all x2, starting transfers between devices, sum_over_dp(): lax.all_to_all(total.reshape(depth, rows // depth, -1), 'dp', 0, 0, axis_...  18.7 us
    unnamed x34, local copies, waits for them, and re-layouts  17.3 us
    all_to_all x4, waiting for transfers between devices, exchange(): return lax.all_to_all(msg, 'blk', split_axis=0, concat_axis=0, tiled=True)  8.78 us
    pallas_call x1, Pallas kernels, up(): pl.pallas_call(up_kernel, grid=(OWNED,), out_shape=[shape(MSG, BF16), sha...  8.63 us
    ppermute x2, waiting for transfers between devices, sum_over_dp(): lax.ppermute(total[:rows].astype(BF16), 'dp', [(d, d ^ 2) for d in range(...  7.48 us
    ppermute x2, starting transfers between devices, sum_over_dp(): lax.ppermute(total[:rows].astype(BF16), 'dp', [(d, d ^ 2) for d in range(...  7.35 us
  transfers between devices with their start and end apart: 10, of which 4 were waited for; matrix products, arithmetic and copies ran while one was open for 3% of the time, Pallas kernels for 15%

profile of v1, /device:TPU:8, one launch (start us, length us, event | category | flops | bytes accessed | tf_op | source)
XLA Modules:
  0.0 143.1 jit_solution(1846628929235711661)
XLA Ops:
  0.7 1.0 copy-done.4
  1.7 1.2 copy-done.6
  2.9 1.4 %shard_map.93 = bf16[8,128,512]{2,1,0:T(8,128)(2,1)} custom-call(bf16[512,1024]{1,0:T(8,128)(2,1)S(1)} %copy-done.6, bf16[8,128,128]{2,1,0:T(8,128)(2,1)S(1)} %copy-done.4), custom_call_target="tpu_custom_call" | custom-call | flops 134000000 | bytes 3145728 | tf_op jit(solution)/shard_map/pallas_call | solution.py:141
  4.4 9.3 %all-to-all-start = ((bf16[8,128,512]{2,1,0:T(8,128)(2,1)}), bf16[8,128,512]{2,1,0:T(8,128)(2,1)S(1)}, u32[]{:S(2)}, u32[]{:S(2)}) async-start(bf16[8,128,512]{2,1,0:T(8,128)(2,1)} %shard_map.93), calls=%async_computation | async-start | bytes 2097152 | tf_op jit(solution)/shard_map/all_to_all | solution.py:213
  13.7 1.4 shard_map.96
  15.1 8.8 %all-to-all-done.msg_ref = bf16[8,128,512]{2,1,0:T(8,128)(2,1)S(1)} async-done(((bf16[8,128,512]{2,1,0:T(8,128)(2,1)}), bf16[8,128,512]{2,1,0:T(8,128)(2,1)S(1)}, u32[]{:S(2)}, u32[]{:S(2)}) %all-to-all-start) | async-done | bytes 1048608 | tf_op jit(solution)/shard_map/all_to_all | solution.py:213
  23.9 4.8 %all-to-all-start.2 = ((bf16[8,128,512]{2,1,0:T(8,128)(2,1)}), bf16[8,128,512]{2,1,0:T(8,128)(2,1)S(1)}, u32[]{:S(2)}, u32[]{:S(2)}) async-start(bf16[8,128,512]{2,1,0:T(8,128)(2,1)} %shard_map.96), calls=%async_computation.2 | async-start | bytes 2097152 | tf_op jit(solution)/shard_map/all_to_all | solution.py:213
  28.7 1.2 copy-done.10
  30.0 1.2 copy-done.12
  31.2 8.6 %shard_map.94 = (bf16[8,128,512]{2,1,0:T(8,128)(2,1)S(1)}, bf16[8,128,512]{2,1,0:T(8,128)(2,1)S(1)}, bf16[8,512,512]{2,1,0:T(8,128)(2,1)S(1)}) custom-call(s32[2]{0:T(128)S(1)} %pad_add_fusion.place_ref, bf16[8,128,512]{2,1,0:T(8,128)(2,1)S(1)} %all-to-all-done.msg_ref, bf16[8,128,512]{2,1,0:T(8,128)(2,1)S(1)} %copy-done.10, bf16[8,512,128]{2,1,0:T(8,128)(2,1)S(1)} %copy-done.12), custom_call_target="tpu_custom_call" | custom-call | flops 1300000000 | bytes 9437184 | tf_op jit(solution)/shard_map/pallas_call | solution.py:160
  39.8 1.9 %copy-done.1 = bf16[8,512,512]{2,1,0:T(8,128)(2,1)} copy-done((bf16[8,512,512]{2,1,0:T(8,128)(2,1)}, bf16[8,512,512]{2,1,0:T(8,128)(2,1)S(1)}, u32[]{:S(2)}) %copy-start.1) | copy-done | bytes 4194328
  42.7 1.0 copy-done.14
  43.8 5.7 %all-to-all-start.1 = ((bf16[8,128,512]{2,1,0:T(8,128)(2,1)}), bf16[8,128,512]{2,1,0:T(8,128)(2,1)S(1)}, u32[]{:S(2)}, u32[]{:S(2)}) async-start(bf16[8,128,512]{2,1,0:T(8,128)(2,1)} %copy-done.9), calls=%async_computation.1 | async-start | bytes 2097152 | tf_op jit(solution)/shard_map/all_to_all | solution.py:213
  49.5 2.2 %copy-done.2 = bf16[8,512,512]{2,1,0:T(8,128)(2,1)S(1)} copy-done((bf16[8,512,512]{2,1,0:T(8,128)(2,1)S(1)}, bf16[8,512,512]{2,1,0:T(8,128)(2,1)}, u32[]{:S(2)}) %copy-start.2) | copy-done | bytes 4194328
  51.6 1.2 copy-done.11
  52.9 1.2 copy-done.13
  54.1 1.2 copy-done.15
  55.3 6.2 %shard_map.97 = (bf16[8,128,512]{2,1,0:T(8,128)(2,1)S(1)}, bf16[64,4096]{1,0:T(8,128)(2,1)}, f32[64,4096]{1,0:T(8,128)S(1)}) custom-call(bf16[8,128,512]{2,1,0:T(8,128)(2,1)S(1)} %all-to-all-done.2.msg_ref, bf16[8,128,512]{2,1,0:T(8,128)(2,1)S(1)} %copy-done.15, bf16[8,512,512]{2,1,0:T(8,128)(2,1)S(1)} %copy-done.2, bf16[8,128,512]{2,1,0:T(8,128)(2,1)S(1)} %copy-done.11, ...), custom_call_target="tpu_custom_call" | custom-call | flops 1800000000 | bytes 11534336 | tf_op jit(solution)/shard_map/pallas_call | solution.py:175
  61.5 1.0 copy-done.7
  63.5 1.9 %collective-permute-start = (bf16[64,4096]{1,0:T(8,128)(2,1)}, bf16[64,4096]{1,0:T(8,128)(2,1)S(1)}, u32[]{:S(2)}, u32[]{:S(2)}) collective-permute-start(bf16[64,4096]{1,0:T(8,128)(2,1)} %get-tuple-element.19), channel_id=1, source_target_pairs={{0,8},{8,0},{16,24},{24,16},{32,40},{40,32},{48,56},{56,48},{64,72... | collective-permute-start | bytes 1572872 | tf_op jit(solution)/shard_map/ppermute | solution.py:220
  65.4 3.6 %shard_map.95 = (bf16[512,1024]{1,0:T(8,128)(2,1)}, bf16[64,1024]{1,0:T(8,128)(2,1)S(1)}, f32[64,1024]{1,0:T(8,128)S(1)}) custom-call(s32[2]{0:T(128)S(1)} %pad_add_fusion.place_ref, bf16[8,128,512]{2,1,0:T(8,128)(2,1)S(1)} %all-to-all-done.1.msg_ref, bf16[8,128,128]{2,1,0:T(8,128)(2,1)S(1)} %copy-done.3, bf16[512,1024]{1,0:T(8,128)(2,1)S(1)} %copy-done), custom_call_target="tpu_custom_call" | custom-call | flops 500000000 | bytes 4194304 | tf_op jit(solution)/shard_map/pallas_call | solution.py:189
  69.0 2.4 %collective-permute-start.2 = (bf16[64,1024]{1,0:T(8,128)(2,1)S(1)}, bf16[64,1024]{1,0:T(8,128)(2,1)S(1)}, u32[]{:S(2)}, u32[]{:S(2)}) collective-permute-start(bf16[64,1024]{1,0:T(8,128)(2,1)S(1)} %get-tuple-element.21), channel_id=1, source_target_pairs={{0,8},{8,0},{16,24},{24,16},{32,40},{40,32},{48,56},{56,48},{64,72... | collective-permute-start | bytes 393224 | tf_op jit(solution)/shard_map/ppermute | solution.py:220
  71.5 5.8 %all-to-all-start.3 = ((bf16[8,128,512]{2,1,0:T(8,128)(2,1)}), bf16[8,128,512]{2,1,0:T(8,128)(2,1)S(1)}, u32[]{:S(2)}, u32[]{:S(2)}) async-start(bf16[8,128,512]{2,1,0:T(8,128)(2,1)} %copy-done.7), calls=%async_computation.3 | async-start | bytes 2097152 | tf_op jit(solution)/shard_map/all_to_all | solution.py:213
  77.3 4.6 %collective-permute-start.3 = (bf16[32,1024]{1,0:T(8,128)(2,1)S(1)}, bf16[32,1024]{1,0:T(8,128)(2,1)S(1)}, u32[]{:S(2)}, u32[]{:S(2)}) collective-permute-start(bf16[32,1024]{1,0:T(8,128)(2,1)S(1)} %slice.31), channel_id=1, source_target_pairs={{0,16},{8,24},{16,0},{24,8},{32,48},{40,56},{48,32},{56,40},{64,80... | collective-permute-start | bytes 196616 | tf_op jit(solution)/shard_map/ppermute | solution.py:221
  82.8 1.4 %convert_add_fusion = f32[64,4096]{1,0:T(8,128)S(1)} fusion(f32[64,4096]{1,0:T(8,128)} %copy-done.8, bf16[64,4096]{1,0:T(8,128)(2,1)} %copy-done.16), kind=kLoop, calls=%fused_computation | loop fusion | flops 524288 | bytes 2621440 | tf_op jit(solution)/shard_map/add | solution.py:220
  84.3 2.7 %collective-permute-start.1 = (bf16[32,4096]{1,0:T(8,128)(2,1)S(1)}, bf16[32,4096]{1,0:T(8,128)(2,1)S(1)}, u32[]{:S(2)}, u32[]{:S(2)}) collective-permute-start(bf16[32,4096]{1,0:T(8,128)(2,1)S(1)} %slice.30), channel_id=1, source_target_pairs={{0,16},{8,24},{16,0},{24,8},{32,48},{40,56},{48,32},{56,40},{64,80... | collective-permute-start | bytes 786440 | tf_op jit(solution)/shard_map/ppermute | solution.py:221
  87.0 7.5 %collective-permute-done.3 = bf16[32,1024]{1,0:T(8,128)(2,1)S(1)} collective-permute-done((bf16[32,1024]{1,0:T(8,128)(2,1)S(1)}, bf16[32,1024]{1,0:T(8,128)(2,1)S(1)}, u32[]{:S(2)}, u32[]{:S(2)}) %collective-permute-start.3) | collective-permute-done | bytes 65568 | tf_op jit(solution)/shard_map/ppermute | solution.py:221
  95.2 15.2 %all-to-all-start.5 = ((bf16[16,2,1024]{2,1,0:T(2,128)(2,1)}), bf16[16,2,1024]{2,1,0:T(2,128)(2,1)S(1)}, u32[]{:S(2)}, u32[]{:S(2)}) async-start(bf16[16,2,1024]{2,1,0:T(2,128)(2,1)} %reshape.23), calls=%async_computation.5 | async-start | bytes 131072 | tf_op jit(solution)/shard_map/all_to_all | solution.py:224
  111.3 11.8 %all-to-all-done.5 = bf16[16,2,1024]{2,1,0:T(2,128)(2,1)S(1)} async-done(((bf16[16,2,1024]{2,1,0:T(2,128)(2,1)}), bf16[16,2,1024]{2,1,0:T(2,128)(2,1)S(1)}, u32[]{:S(2)}, u32[]{:S(2)}) %all-to-all-start.5) | async-done | bytes 65568 | tf_op jit(solution)/shard_map/all_to_all | solution.py:224
  123.2 3.5 %all-to-all-start.4 = ((bf16[16,2,4096]{2,1,0:T(2,128)(2,1)}), bf16[16,2,4096]{2,1,0:T(2,128)(2,1)S(1)}, u32[]{:S(2)}, u32[]{:S(2)}) async-start(bf16[16,2,4096]{2,1,0:T(2,128)(2,1)} %reshape.22), calls=%async_computation.4 | async-start | bytes 524288 | tf_op jit(solution)/shard_map/all_to_all | solution.py:224
  126.7 1.8 %shard_map.98 = bf16[512,1024]{1,0:T(8,128)(2,1)} custom-call(bf16[8,128,512]{2,1,0:T(8,128)(2,1)S(1)} %all-to-all-done.3.msg_ref, bf16[8,128,128]{2,1,0:T(8,128)(2,1)S(1)} %copy-done.5), custom_call_target="tpu_custom_call" | custom-call | flops 300000000 | bytes 3145728 | tf_op jit(solution)/shard_map/pallas_call | solution.py:201
  129.2 13.0 %all-to-all-done.4 = bf16[16,2,4096]{2,1,0:T(2,128)(2,1)S(1)} async-done(((bf16[16,2,4096]{2,1,0:T(2,128)(2,1)}), bf16[16,2,4096]{2,1,0:T(2,128)(2,1)S(1)}, u32[]{:S(2)}, u32[]{:S(2)}) %all-to-all-start.4) | async-done | bytes 262176 | tf_op jit(solution)/shard_map/all_to_all | solution.py:224
  (41 shorter events, 6.0 us)
Async XLA Ops:
  0.6 13.0 %copy-start.3 = (bf16[8,128,128]{2,1,0:T(8,128)(2,1)S(1)}, bf16[8,128,128]{2,1,0:T(8,128)(2,1)}, u32[]{:S(2)}) copy-start(bf16[8,128,128]{2,1,0:T(8,128)(2,1)} %w_ref.3) | copy-start | bytes 786436
  0.6 13.0 %copy-start = (bf16[512,1024]{1,0:T(8,128)(2,1)S(1)}, bf16[512,1024]{1,0:T(8,128)(2,1)}, u32[]{:S(2)}) copy-start(bf16[512,1024]{1,0:T(8,128)(2,1)} %x_ref.3) | copy-start | bytes 3145732
  0.7 1.1 copy-start.4
  1.7 1.2 copy-start.6
  4.4 19.5 %all-to-all-start = ((bf16[8,128,512]{2,1,0:T(8,128)(2,1)}), bf16[8,128,512]{2,1,0:T(8,128)(2,1)S(1)}, u32[]{:S(2)}, u32[]{:S(2)}) async-start(bf16[8,128,512]{2,1,0:T(8,128)(2,1)} %shard_map.93), calls=%async_computation | async-start | bytes 2097152 | tf_op jit(solution)/shard_map/all_to_all | solution.py:213
  23.9 19.9 %all-to-all-start.2 = ((bf16[8,128,512]{2,1,0:T(8,128)(2,1)}), bf16[8,128,512]{2,1,0:T(8,128)(2,1)S(1)}, u32[]{:S(2)}, u32[]{:S(2)}) async-start(bf16[8,128,512]{2,1,0:T(8,128)(2,1)} %shard_map.96), calls=%async_computation.2 | async-start | bytes 2097152 | tf_op jit(solution)/shard_map/all_to_all | solution.py:213
  28.7 1.2 copy-start.10
  30.0 1.2 copy-start.12
  39.8 2.0 %copy-start.1 = (bf16[8,512,512]{2,1,0:T(8,128)(2,1)}, bf16[8,512,512]{2,1,0:T(8,128)(2,1)S(1)}, u32[]{:S(2)}) copy-start(bf16[8,512,512]{2,1,0:T(8,128)(2,1)S(1)} %get-tuple-element.16.slope_ref) | copy-start | bytes 12582916
  41.8 1.0 copy-start.9
  42.7 1.0 copy-start.14
  43.8 21.7 %all-to-all-start.1 = ((bf16[8,128,512]{2,1,0:T(8,128)(2,1)}), bf16[8,128,512]{2,1,0:T(8,128)(2,1)S(1)}, u32[]{:S(2)}, u32[]{:S(2)}) async-start(bf16[8,128,512]{2,1,0:T(8,128)(2,1)} %copy-done.9), calls=%async_computation.1 | async-start | bytes 2097152 | tf_op jit(solution)/shard_map/all_to_all | solution.py:213
  49.5 2.2 %copy-start.2 = (bf16[8,512,512]{2,1,0:T(8,128)(2,1)S(1)}, bf16[8,512,512]{2,1,0:T(8,128)(2,1)}, u32[]{:S(2)}) copy-start(bf16[8,512,512]{2,1,0:T(8,128)(2,1)} %copy-done.1) | copy-start | bytes 12582916
  51.6 1.2 copy-start.11
  52.9 1.2 copy-start.13
  54.1 1.2 copy-start.15
  61.5 1.0 copy-start.7
  62.5 1.0 copy-start.8
  63.5 18.5 %collective-permute-start = (bf16[64,4096]{1,0:T(8,128)(2,1)}, bf16[64,4096]{1,0:T(8,128)(2,1)S(1)}, u32[]{:S(2)}, u32[]{:S(2)}) collective-permute-start(bf16[64,4096]{1,0:T(8,128)(2,1)} %get-tuple-element.19), channel_id=1, source_target_pairs={{0,8},{8,0},{16,24},{24,16},{32,40},{40,32},{48,56},{56,48},{64,72... | collective-permute-start | bytes 1572872 | tf_op jit(solution)/shard_map/ppermute | solution.py:220
  69.0 8.2 %collective-permute-start.2 = (bf16[64,1024]{1,0:T(8,128)(2,1)S(1)}, bf16[64,1024]{1,0:T(8,128)(2,1)S(1)}, u32[]{:S(2)}, u32[]{:S(2)}) collective-permute-start(bf16[64,1024]{1,0:T(8,128)(2,1)S(1)} %get-tuple-element.21), channel_id=1, source_target_pairs={{0,8},{8,0},{16,24},{24,16},{32,40},{40,32},{48,56},{56,48},{64,72... | collective-permute-start | bytes 393224 | tf_op jit(solution)/shard_map/ppermute | solution.py:220
  71.4 55.2 %copy-start.5 = (bf16[8,128,128]{2,1,0:T(8,128)(2,1)S(1)}, bf16[8,128,128]{2,1,0:T(8,128)(2,1)}, u32[]{:S(2)}) copy-start(bf16[8,128,128]{2,1,0:T(8,128)(2,1)} %right_ref.1) | copy-start | bytes 786436
  71.5 23.7 %all-to-all-start.3 = ((bf16[8,128,512]{2,1,0:T(8,128)(2,1)}), bf16[8,128,512]{2,1,0:T(8,128)(2,1)S(1)}, u32[]{:S(2)}, u32[]{:S(2)}) async-start(bf16[8,128,512]{2,1,0:T(8,128)(2,1)} %copy-done.7), calls=%async_computation.3 | async-start | bytes 2097152 | tf_op jit(solution)/shard_map/all_to_all | solution.py:213
  77.3 17.1 %collective-permute-start.3 = (bf16[32,1024]{1,0:T(8,128)(2,1)S(1)}, bf16[32,1024]{1,0:T(8,128)(2,1)S(1)}, u32[]{:S(2)}, u32[]{:S(2)}) collective-permute-start(bf16[32,1024]{1,0:T(8,128)(2,1)S(1)} %slice.31), channel_id=1, source_target_pairs={{0,16},{8,24},{16,0},{24,8},{32,48},{40,56},{48,32},{56,40},{64,80... | collective-permute-start | bytes 196616 | tf_op jit(solution)/shard_map/ppermute | solution.py:221
  82.0 0.8 copy-start.16
  84.3 26.1 %collective-permute-start.1 = (bf16[32,4096]{1,0:T(8,128)(2,1)S(1)}, bf16[32,4096]{1,0:T(8,128)(2,1)S(1)}, u32[]{:S(2)}, u32[]{:S(2)}) collective-permute-start(bf16[32,4096]{1,0:T(8,128)(2,1)S(1)} %slice.30), channel_id=1, source_target_pairs={{0,16},{8,24},{16,0},{24,8},{32,48},{40,56},{48,32},{56,40},{64,80... | collective-permute-start | bytes 786440 | tf_op jit(solution)/shard_map/ppermute | solution.py:221
  95.2 28.0 %all-to-all-start.5 = ((bf16[16,2,1024]{2,1,0:T(2,128)(2,1)}), bf16[16,2,1024]{2,1,0:T(2,128)(2,1)S(1)}, u32[]{:S(2)}, u32[]{:S(2)}) async-start(bf16[16,2,1024]{2,1,0:T(2,128)(2,1)} %reshape.23), calls=%async_computation.5 | async-start | bytes 131072 | tf_op jit(solution)/shard_map/all_to_all | solution.py:224
  123.2 19.1 %all-to-all-start.4 = ((bf16[16,2,4096]{2,1,0:T(2,128)(2,1)}), bf16[16,2,4096]{2,1,0:T(2,128)(2,1)S(1)}, u32[]{:S(2)}, u32[]{:S(2)}) async-start(bf16[16,2,4096]{2,1,0:T(2,128)(2,1)} %reshape.22), calls=%async_computation.4 | async-start | bytes 524288 | tf_op jit(solution)/shard_map/all_to_all | solution.py:224

commit v2 on v1

v2 whole, which is shorter than its diff:
```python
import functools
import math

import jax
import jax.numpy as jnp
from jax import lax
from jax.experimental import pallas as pl
from jax.experimental.pallas import tpu as pltpu
from jax.sharding import PartitionSpec as P

GROUPS = 8
OWNED = 8
BIN = 128
BHID = 512
ROWS = 512
PIECE = 16
PAIR = 2
STEPS = (0, 2, 3, 1, 4, 5)
MIB = 1 << 20
BF16 = jnp.bfloat16
F32 = jnp.float32

NN = (((1,), (0,)), ((), ()))
NT = (((1,), (1,)), ((), ()))
TN = (((0,), (0,)), ((), ()))
TT = (((0,), (1,)), ((), ()))


def dot(a, b, dims):
    return lax.dot_general(a, b, dims, preferred_element_type=F32)


def swap_matrix():
    to = lax.broadcasted_iota(jnp.int32, (BIN, BIN), 0)
    come = lax.broadcasted_iota(jnp.int32, (BIN, BIN), 1)
    wanted = ((to & 14) << 3) | ((to >> 4) << 1) | (to & 1)
    return jnp.where(come == wanted, 1.0, 0.0).astype(BF16)


def shard_matrix(place):
    to = lax.broadcasted_iota(jnp.int32, (BIN, BIN), 0)
    come = lax.broadcasted_iota(jnp.int32, (BIN, BIN), 1)
    theirs = jnp.zeros_like(to)
    for step, bit in enumerate(STEPS):
        theirs = theirs | ((1 - ((to >> (len(STEPS) - step)) & 1)) << bit)
    wanted = ((theirs ^ place) << 1) | (to & 1)
    return jnp.where(come == wanted, 1.0, 0.0).astype(BF16)


def scatter_rows(out_ref, slot, value):
    for n in range(GROUPS):
        out_ref[n, slot * PIECE : (slot + 1) * PIECE, :] = value[n * PIECE : (n + 1) * PIECE, :]


def gather_rows(msg_ref, held_ref):
    swap = swap_matrix()
    for src in range(GROUPS):
        swapped = dot(swap, msg_ref[src], NN).astype(BF16)
        for b in range(OWNED):
            held_ref[b, src * PIECE : (src + 1) * PIECE, :] = swapped[b * PIECE : (b + 1) * PIECE, :]


def right_kernel(dims, x_ref, w_ref, out_ref):
    for k in range(PAIR):
        value = dot(w_ref[k], x_ref[:, k * BIN : (k + 1) * BIN], dims).astype(BF16)
        scatter_rows(out_ref, k, value)


def up_kernel(place_ref, msg_ref, left_ref, down_ref, out_ref, saved_ref, slope_ref, held_ref, shard_ref):
    j = pl.program_id(0)

    @pl.when(j == 0)
    def _():
        gather_rows(msg_ref, held_ref)
        shard_ref[...] = shard_matrix(place_ref[0])

    v = held_ref[j]
    saved_ref[0] = dot(shard_ref[...], v, NN).astype(BF16)
    s = dot(left_ref[0], v, TN)
    c = math.sqrt(2.0 / math.pi)
    square = s * s
    th = jnp.tanh(s * (c + (c * 0.044715) * square))
    half = 0.5 + 0.5 * th
    hidden = (s * half).astype(BF16)
    slope = half + (0.5 * s) * ((1.0 - th * th) * (c + (3.0 * c * 0.044715) * square))
    slope_ref[0] = slope.astype(BF16)
    z = dot(down_ref[0], hidden, TN).astype(BF16)
    scatter_rows(out_ref, 0, z)


def back_kernel(msg_ref, saved_ref, slope_ref, left_ref, down_ref, out_ref, send_ref, keep_ref, held_ref):
    j = pl.program_id(0)

    @pl.when(j == 0)
    def _():
        gather_rows(msg_ref, held_ref)

    grad_hidden = dot(down_ref[0], held_ref[j], NN)
    grad_pre = (grad_hidden * slope_ref[0].astype(F32)).astype(BF16)
    grad_v = dot(left_ref[0], grad_pre, NN).astype(BF16)
    scatter_rows(out_ref, 0, grad_v)
    part = dot(saved_ref[0], grad_pre, NT)
    send_ref[...] = part[: BIN // 2].astype(BF16)
    keep_ref[...] = part[BIN // 2 :]


def out_kernel(place_ref, msg_ref, left_ref, cot_ref, out_ref, send_ref, keep_ref, held_ref, shard_ref):
    step = pl.program_id(0)

    @pl.when(step == 0)
    def _():
        gather_rows(msg_ref, held_ref)
        shard_ref[...] = shard_matrix(place_ref[0])

    for k in range(PAIR):
        cols = slice(k * BIN, (k + 1) * BIN)
        w = held_ref[step * PAIR + k]
        part = dot(dot(shard_ref[...], w, NN).astype(BF16), cot_ref[:, cols], NN)
        send_ref[:, cols] = part[: BIN // 2].astype(BF16)
        keep_ref[:, cols] = part[BIN // 2 :]
        out_ref[:, cols] = dot(w, left_ref[k], TN).astype(BF16)


def in_kernel(msg_ref, right_ref, out_ref, held_ref):
    step = pl.program_id(0)

    @pl.when(step == 0)
    def _():
        gather_rows(msg_ref, held_ref)

    for k in range(PAIR):
        w = held_ref[step * PAIR + k]
        out_ref[:, k * BIN : (k + 1) * BIN] = dot(w, right_ref[k], TT).astype(BF16)


VMEM = pl.BlockSpec(memory_space=pltpu.VMEM)
SMEM = pl.BlockSpec(memory_space=pltpu.SMEM)
MSG = (GROUPS, BIN, ROWS)


def params(mib):
    return pltpu.CompilerParams(vmem_limit_bytes=mib * MIB)


def cost(mflop, mib, trans=0):
    return pl.CostEstimate(flops=mflop * 1000000, bytes_accessed=mib * MIB, transcendentals=trans)


def shape(dims, dtype):
    return jax.ShapeDtypeStruct(dims, dtype)


def far(dims, dtype):
    return pltpu.HBM(dims, dtype)


def stay(x):
    return pltpu.with_memory_space_constraint(x, pltpu.HBM)


def each(dims, count=1):
    return pl.BlockSpec((count,) + dims, lambda j: (j, 0, 0))


def pieces(count):
    return pl.BlockSpec((GROUPS, count * PIECE, ROWS), lambda j: (0, j, 0))


def columns(rows, width):
    return pl.BlockSpec((rows, width), lambda j: (0, j))


HELD = pltpu.VMEM((OWNED, BIN, ROWS), BF16)
SHARD = pltpu.VMEM((BIN, BIN), BF16)


def right(x, w, dims):
    return pl.pallas_call(
        functools.partial(right_kernel, dims),
        grid=(OWNED // PAIR,),
        out_shape=far(MSG, BF16),
        in_specs=[columns(ROWS, PAIR * BIN), each((BIN, BIN), PAIR)],
        out_specs=pieces(PAIR),
        compiler_params=params(16),
        cost_estimate=cost(134, 3),
    )(stay(x), stay(w))


def up(place, msg, left, down):
    return pl.pallas_call(
        up_kernel,
        grid=(OWNED,),
        out_shape=[far(MSG, BF16), far((OWNED, BIN, ROWS), BF16), far((OWNED, BHID, ROWS), BF16)],
        in_specs=[SMEM, VMEM, each((BIN, BHID)), each((BHID, BIN))],
        out_specs=[pieces(1), each((BIN, ROWS)), each((BHID, ROWS))],
        scratch_shapes=[HELD, SHARD],
        compiler_params=params(24),
        cost_estimate=cost(1300, 9, OWNED * BHID * ROWS),
    )(place, msg, stay(left), stay(down))


def back(msg, saved, slope, left, down):
    half = (BIN // 2, OWNED * BHID)
    return pl.pallas_call(
        back_kernel,
        grid=(OWNED,),
        out_shape=[far(MSG, BF16), far(half, BF16), far(half, F32)],
        in_specs=[VMEM, each((BIN, ROWS)), each((BHID, ROWS)), each((BIN, BHID)), each((BHID, BIN))],
        out_specs=[pieces(1), columns(BIN // 2, BHID), columns(BIN // 2, BHID)],
        scratch_shapes=[HELD],
        compiler_params=params(24),
        cost_estimate=cost(1800, 11),
    )(msg, stay(saved), stay(slope), stay(left), stay(down))


def out(place, msg, left, cot):
    half = (BIN // 2, OWNED * BIN)
    wide = PAIR * BIN
    return pl.pallas_call(
        out_kernel,
        grid=(OWNED // PAIR,),
        out_shape=[far((ROWS, OWNED * BIN), BF16), shape(half, BF16), shape(half, F32)],
        in_specs=[SMEM, VMEM, each((BIN, BIN), PAIR), columns(ROWS, wide)],
        out_specs=[columns(ROWS, wide), columns(BIN // 2, wide), columns(BIN // 2, wide)],
        scratch_shapes=[HELD, SHARD],
        compiler_params=params(20),
        cost_estimate=cost(500, 4),
    )(place, msg, stay(left), stay(cot))


def into(msg, rightw):
    return pl.pallas_call(
        in_kernel,
        grid=(OWNED // PAIR,),
        out_shape=far((ROWS, OWNED * BIN), BF16),
        in_specs=[VMEM, each((BIN, BIN), PAIR)],
        out_specs=columns(ROWS, PAIR * BIN),
        scratch_shapes=[HELD],
        compiler_params=params(20),
        cost_estimate=cost(300, 3),
    )(msg, stay(rightw))


def exchange(msg):
    return lax.all_to_all(msg, "blk", split_axis=0, concat_axis=0, tiled=True)


def join_kernel(up_keep_ref, up_far_ref, down_keep_ref, down_far_ref, send_ref, keep_ref):
    half = send_ref.shape[0]
    at = 0
    for kept, far in ((up_keep_ref, up_far_ref), (down_keep_ref, down_far_ref)):
        cols = slice(at, at + kept.shape[1])
        at += kept.shape[1]
        total = kept[...] + far[...].astype(F32)
        send_ref[:, cols] = total[:half].astype(BF16)
        keep_ref[:, cols] = total[half:]


def join(up_keep, up_far, down_keep, down_far):
    dims = (up_keep.shape[0] // 2, up_keep.shape[1] + down_keep.shape[1])
    return pl.pallas_call(
        join_kernel,
        out_shape=[shape(dims, BF16), shape(dims, F32)],
        in_specs=[VMEM] * 4,
        out_specs=[VMEM] * 2,
        compiler_params=params(8),
        cost_estimate=cost(1, 3),
    )(up_keep, up_far, down_keep, down_far)


def swap_halves(send, step):
    bit = 1 << STEPS[step]
    return lax.ppermute(send, "dp", [(d, d ^ bit) for d in range(lax.axis_size("dp"))])


def halve(send, keep, step):
    total = keep + swap_halves(send, step).astype(F32)
    rows = total.shape[0] // 2
    return total[:rows].astype(BF16), total[rows:]


def sum_over_dp(up_send, up_keep, down_send, down_keep, grad_u, factor):
    for step in range(2):
        up_send, up_keep = halve(up_send, up_keep, step)
        down_send, down_keep = halve(down_send, down_keep, step)
    up_far, down_far = swap_halves(up_send, 2), swap_halves(down_send, 2)
    send, keep = join(up_keep, up_far, down_keep, down_far)
    send, grad_u = lax.optimization_barrier((send, grad_u))
    for step in range(3, len(STEPS) - 1):
        send, keep = halve(send, keep, step)
    total = (keep + swap_halves(send, len(STEPS) - 1).astype(F32)) * factor
    split = OWNED * BHID
    up_grad = total[:, :split].reshape(-1, OWNED, BHID).transpose(1, 0, 2)
    down_grad = total[:, split:].reshape(-1, OWNED, BIN).transpose(1, 0, 2)
    return up_grad, down_grad, grad_u


def on_device(tokens, up_right, up_left, down_right, down_left, cotangent):
    place = lax.axis_index("dp").reshape(1).astype(jnp.int32)
    factor = 1.0 / math.sqrt(tokens.shape[0] * lax.axis_size("dp"))
    v = exchange(right(tokens, up_right, TT))
    grad_z = exchange(right(cotangent, down_left, NT))
    z, saved, slope = up(place, v, up_left, down_right)
    w = exchange(z)
    grad_v, up_send, up_keep = back(grad_z, saved, slope, up_left, down_right)
    grad_u = exchange(grad_v)
    layer_out, down_send, down_keep = out(place, w, down_left, cotangent)
    up_grad, down_grad, grad_u = sum_over_dp(
        up_send, up_keep, down_send, down_keep, grad_u, factor
    )
    input_grad = into(grad_u, up_right)
    return (layer_out, input_grad, up_grad, down_grad)


def solution(mesh):
    placed = (
        P("dp", "blk"),
        P("blk", None, None),
        P("blk", None, None),
        P("blk", None, None),
        P("blk", None, None),
        P("dp", "blk"),
    )
    return jax.shard_map(
        on_device,
        mesh=mesh,
        in_specs=placed,
        out_specs=(P("dp", "blk"), P("dp", "blk"), P("blk", "dp", None), P("blk", "dp", None)),
        check_vma=False,
    )
```

time: 144 us -> 134 us (0.931)
  the two profiles are of different devices: /device:TPU:8 before, /device:TPU:6 now
where the time goes in v2:
time: 134 us; the launch traced here: 132 us
  starting transfers between devices  62.5 us (47%)
  Pallas kernels  37.2 us (28%)
  waiting for transfers between devices  28.8 us (21%)
  other arithmetic  1.53 us (1%)
    ppermute x9, starting transfers between devices, swap_halves(): lax.ppermute(send, 'dp', [(d, d ^ bit) for d in range(lax.axis_size('dp'))])  44 us
    all_to_all x4, starting transfers between devices, exchange(): return lax.all_to_all(msg, 'blk', split_axis=0, concat_axis=0, tiled=True)  18.5 us
    all_to_all x4, waiting for transfers between devices, exchange(): return lax.all_to_all(msg, 'blk', split_axis=0, concat_axis=0, tiled=True)  16.8 us
    ppermute x9, waiting for transfers between devices, swap_halves(): lax.ppermute(send, 'dp', [(d, d ^ bit) for d in range(lax.axis_size('dp'))])  11.9 us
    pallas_call x1, Pallas kernels, up(): pl.pallas_call(up_kernel, grid=(OWNED,), out_shape=[far(MSG, BF16), far((...  10.9 us
    pallas_call x1, Pallas kernels, back(): pl.pallas_call(back_kernel, grid=(OWNED,), out_shape=[far(MSG, BF16), far...  9.5 us
    pallas_call x2, Pallas kernels, right(): pl.pallas_call(functools.partial(right_kernel, dims), grid=(OWNED // PAIR...  7.73 us
    pallas_call x1, Pallas kernels, out(): pl.pallas_call(out_kernel, grid=(OWNED // PAIR,), out_shape=[far((ROWS, O...  4.99 us
  transfers between devices with their start and end apart: 13, of which 8 were waited for; matrix products, arithmetic and copies ran while one was open for 1% of the time, Pallas kernels for 25%

profile of v2, /device:TPU:6, one launch (start us, length us, event | category | flops | bytes accessed | tf_op | source)
XLA Modules:
  0.0 132.2 jit_solution(9882973411391570213)
XLA Ops:
  0.6 3.8 %shard_map.93 = bf16[8,128,512]{2,1,0:T(8,128)(2,1)} custom-call(bf16[512,1024]{1,0:T(8,128)(2,1)} %x_ref.2, bf16[8,128,128]{2,1,0:T(8,128)(2,1)} %right_ref.1), custom_call_target="tpu_custom_call" | custom-call | flops 134000000 | bytes 3145728 | tf_op jit(solution)/shard_map/pallas_call | solution.py:178
  4.5 5.9 %all-to-all-start = ((bf16[8,128,512]{2,1,0:T(8,128)(2,1)}), bf16[8,128,512]{2,1,0:T(8,128)(2,1)S(1)}, u32[]{:S(2)}, u32[]{:S(2)}) async-start(bf16[8,128,512]{2,1,0:T(8,128)(2,1)} %shard_map.93), calls=%async_computation | async-start | bytes 2097152 | tf_op jit(solution)/shard_map/all_to_all | solution.py:245
  10.4 3.9 %shard_map.96 = bf16[8,128,512]{2,1,0:T(8,128)(2,1)} custom-call(bf16[512,1024]{1,0:T(8,128)(2,1)} %x_ref.3, bf16[8,128,128]{2,1,0:T(8,128)(2,1)} %w_ref.3), custom_call_target="tpu_custom_call" | custom-call | flops 134000000 | bytes 3145728 | tf_op jit(solution)/shard_map/pallas_call | solution.py:178
  14.3 10.3 %all-to-all-done.msg_ref = bf16[8,128,512]{2,1,0:T(8,128)(2,1)S(1)} async-done(((bf16[8,128,512]{2,1,0:T(8,128)(2,1)}), bf16[8,128,512]{2,1,0:T(8,128)(2,1)S(1)}, u32[]{:S(2)}, u32[]{:S(2)}) %all-to-all-start) | async-done | bytes 1048608 | tf_op jit(solution)/shard_map/all_to_all | solution.py:245
  24.6 4.2 %all-to-all-start.2 = ((bf16[8,128,512]{2,1,0:T(8,128)(2,1)}), bf16[8,128,512]{2,1,0:T(8,128)(2,1)S(1)}, u32[]{:S(2)}, u32[]{:S(2)}) async-start(bf16[8,128,512]{2,1,0:T(8,128)(2,1)} %shard_map.96), calls=%async_computation.2 | async-start | bytes 2097152 | tf_op jit(solution)/shard_map/all_to_all | solution.py:245
  28.8 10.9 %shard_map.94 = (bf16[8,128,512]{2,1,0:T(8,128)(2,1)}, bf16[8,128,512]{2,1,0:T(8,128)(2,1)}, bf16[8,512,512]{2,1,0:T(8,128)(2,1)}) custom-call(s32[1]{0:T(128)} %bitcast.place_ref, bf16[8,128,512]{2,1,0:T(8,128)(2,1)S(1)} %all-to-all-done.msg_ref, bf16[8,128,512]{2,1,0:T(8,128)(2,1)} %left_ref.5, bf16[8,512,128]{2,1,0:T(8,128)(2,1)} %down_ref.3), custom_call_target="tpu_custom_call" | custom-call | flops 1300000000 | bytes 9437184 | tf_op jit(solution)/shard_map/pallas_call | solution.py:190
  39.8 3.5 %all-to-all-done.2.msg_ref = bf16[8,128,512]{2,1,0:T(8,128)(2,1)S(1)} async-done(((bf16[8,128,512]{2,1,0:T(8,128)(2,1)}), bf16[8,128,512]{2,1,0:T(8,128)(2,1)S(1)}, u32[]{:S(2)}, u32[]{:S(2)}) %all-to-all-start.2) | async-done | bytes 1048608 | tf_op jit(solution)/shard_map/all_to_all | solution.py:245
  43.3 4.2 %all-to-all-start.1 = ((bf16[8,128,512]{2,1,0:T(8,128)(2,1)}), bf16[8,128,512]{2,1,0:T(8,128)(2,1)S(1)}, u32[]{:S(2)}, u32[]{:S(2)}) async-start(bf16[8,128,512]{2,1,0:T(8,128)(2,1)} %get-tuple-element.17), calls=%async_computation.1 | async-start | bytes 2097152 | tf_op jit(solution)/shard_map/all_to_all | solution.py:245
  47.5 9.5 %shard_map.97 = (bf16[8,128,512]{2,1,0:T(8,128)(2,1)}, bf16[64,4096]{1,0:T(8,128)(2,1)}, f32[64,4096]{1,0:T(8,128)}) custom-call(bf16[8,128,512]{2,1,0:T(8,128)(2,1)S(1)} %all-to-all-done.2.msg_ref, bf16[8,128,512]{2,1,0:T(8,128)(2,1)} %get-tuple-element.19.saved_ref, bf16[8,512,512]{2,1,0:T(8,128)(2,1)} %get-tuple-element.20.slope_ref, ...), custom_call_target="tpu_custom_call" | custom-call | flops 1800000000 | bytes 11534336 | tf_op jit(solution)/shard_map/pallas_call | solution.py:204
  57.0 1.9 %collective-permute-start = (bf16[64,4096]{1,0:T(8,128)(2,1)}, bf16[64,4096]{1,0:T(8,128)(2,1)S(1)}, u32[]{:S(2)}, u32[]{:S(2)}) collective-permute-start(bf16[64,4096]{1,0:T(8,128)(2,1)} %get-tuple-element.22), channel_id=1, source_target_pairs={{0,8},{8,0},{16,24},{24,16},{32,40},{40,32},{48,56},{56,48},{64,72... | collective-permute-start | bytes 1572872 | tf_op jit(solution)/shard_map/ppermute | solution.py:273
  58.9 3.0 %all-to-all-done.1.msg_ref = bf16[8,128,512]{2,1,0:T(8,128)(2,1)S(1)} async-done(((bf16[8,128,512]{2,1,0:T(8,128)(2,1)}), bf16[8,128,512]{2,1,0:T(8,128)(2,1)S(1)}, u32[]{:S(2)}, u32[]{:S(2)}) %all-to-all-start.1) | async-done | bytes 1048608 | tf_op jit(solution)/shard_map/all_to_all | solution.py:245
  61.9 5.0 %shard_map.95 = (bf16[512,1024]{1,0:T(8,128)(2,1)}, bf16[64,1024]{1,0:T(8,128)(2,1)S(1)}, f32[64,1024]{1,0:T(8,128)S(1)}) custom-call(s32[1]{0:T(128)} %bitcast.place_ref, bf16[8,128,512]{2,1,0:T(8,128)(2,1)S(1)} %all-to-all-done.1.msg_ref, bf16[8,128,128]{2,1,0:T(8,128)(2,1)} %w_ref.3, bf16[512,1024]{1,0:T(8,128)(2,1)} %x_ref.3), custom_call_target="tpu_custom_call" | custom-call | flops 500000000 | bytes 4194304 | tf_op jit(solution)/shard_map/pallas_call | solution.py:219
  66.9 1.9 %collective-permute-start.3 = (bf16[64,1024]{1,0:T(8,128)(2,1)S(1)}, bf16[64,1024]{1,0:T(8,128)(2,1)S(1)}, u32[]{:S(2)}, u32[]{:S(2)}) collective-permute-start(bf16[64,1024]{1,0:T(8,128)(2,1)S(1)} %get-tuple-element.24), channel_id=1, source_target_pairs={{0,8},{8,0},{16,24},{24,16},{32,40},{40,32},{48,56},{56,48},{64,72... | collective-permute-start | bytes 393224 | tf_op jit(solution)/shard_map/ppermute | solution.py:273
  68.8 0.0 collective-permute-done
  68.8 1.3 %convert_add_fusion = f32[64,4096]{1,0:T(8,128)S(1)} fusion(f32[64,4096]{1,0:T(8,128)} %get-tuple-element.21, bf16[64,4096]{1,0:T(8,128)(2,1)S(1)} %collective-permute-done), kind=kLoop, calls=%fused_computation | loop fusion | flops 524288 | bytes 2621440 | tf_op jit(solution)/shard_map/add | solution.py:277
  70.2 3.8 %collective-permute-start.1 = (bf16[32,4096]{1,0:T(8,128)(2,1)S(1)}, bf16[32,4096]{1,0:T(8,128)(2,1)S(1)}, u32[]{:S(2)}, u32[]{:S(2)}) collective-permute-start(bf16[32,4096]{1,0:T(8,128)(2,1)S(1)} %slice.89), channel_id=1, source_target_pairs={{0,32},{8,40},{16,48},{24,56},{32,0},{40,8},{48,16},{56,24},{64,96... | collective-permute-start | bytes 786440 | tf_op jit(solution)/shard_map/ppermute | solution.py:273
  74.0 4.2 %all-to-all-start.3 = ((bf16[8,128,512]{2,1,0:T(8,128)(2,1)}), bf16[8,128,512]{2,1,0:T(8,128)(2,1)S(1)}, u32[]{:S(2)}, u32[]{:S(2)}) async-start(bf16[8,128,512]{2,1,0:T(8,128)(2,1)} %get-tuple-element.26), calls=%async_computation.3 | async-start | bytes 2097152 | tf_op jit(solution)/shard_map/all_to_all | solution.py:245
  78.2 0.0 collective-permute-done.3
  78.3 2.0 %collective-permute-start.4 = (bf16[32,1024]{1,0:T(8,128)(2,1)S(1)}, bf16[32,1024]{1,0:T(8,128)(2,1)S(1)}, u32[]{:S(2)}, u32[]{:S(2)}) collective-permute-start(bf16[32,1024]{1,0:T(8,128)(2,1)S(1)} %slice.91), channel_id=1, source_target_pairs={{0,32},{8,40},{16,48},{24,56},{32,0},{40,8},{48,16},{56,24},{64,96... | collective-permute-start | bytes 196616 | tf_op jit(solution)/shard_map/ppermute | solution.py:273
  80.3 0.7 collective-permute-done.1
  81.0 5.2 %collective-permute-start.2 = (bf16[16,4096]{1,0:T(8,128)(2,1)S(1)}, bf16[16,4096]{1,0:T(8,128)(2,1)S(1)}, u32[]{:S(2)}, u32[]{:S(2)}) collective-permute-start(bf16[16,4096]{1,0:T(8,128)(2,1)S(1)} %slice.90), channel_id=1, source_target_pairs={{0,64},{8,72},{16,80},{24,88},{32,96},{40,104},{48,112},{56,120},{... | collective-permute-start | bytes 393224 | tf_op jit(solution)/shard_map/ppermute | solution.py:273
  86.3 3.4 %collective-permute-start.5 = (bf16[16,1024]{1,0:T(8,128)(2,1)S(1)}, bf16[16,1024]{1,0:T(8,128)(2,1)S(1)}, u32[]{:S(2)}, u32[]{:S(2)}) collective-permute-start(bf16[16,1024]{1,0:T(8,128)(2,1)S(1)} %slice.93), channel_id=1, source_target_pairs={{0,64},{8,72},{16,80},{24,88},{32,96},{40,104},{48,112},{56,120},{... | collective-permute-start | bytes 98312 | tf_op jit(solution)/shard_map/ppermute | solution.py:273
  89.7 3.5 %collective-permute-done.2.up_far_ref = bf16[16,4096]{1,0:T(8,128)(2,1)S(1)} collective-permute-done((bf16[16,4096]{1,0:T(8,128)(2,1)S(1)}, bf16[16,4096]{1,0:T(8,128)(2,1)S(1)}, u32[]{:S(2)}, u32[]{:S(2)}) %collective-permute-start.2) | collective-permute-done | bytes 131104 | tf_op jit(solution)/shard_map/ppermute | solution.py:273
  93.2 0.4 collective-permute-done.5.down_far_ref
  93.6 3.3 %collective-permute-start.6 = (bf16[8,5120]{1,0:T(8,128)(2,1)S(1)}, bf16[8,5120]{1,0:T(8,128)(2,1)S(1)}, u32[]{:S(2)}, u32[]{:S(2)}) collective-permute-start(bf16[8,5120]{1,0:T(8,128)(2,1)S(1)} %get-tuple-element.29), channel_id=1, source_target_pairs={{0,16},{8,24},{16,0},{24,8},{32,48},{40,56},{48,32},{56,40},{64,80... | collective-permute-start | bytes 245768 | tf_op jit(solution)/shard_map/ppermute | solution.py:273
  96.9 4.5 %collective-permute-done.6 = bf16[8,5120]{1,0:T(8,128)(2,1)S(1)} collective-permute-done((bf16[8,5120]{1,0:T(8,128)(2,1)S(1)}, bf16[8,5120]{1,0:T(8,128)(2,1)S(1)}, u32[]{:S(2)}, u32[]{:S(2)}) %collective-permute-start.6) | collective-permute-done | bytes 81952 | tf_op jit(solution)/shard_map/ppermute | solution.py:273
  101.5 9.1 %collective-permute-start.7 = (bf16[4,5120]{1,0:T(4,128)(2,1)S(1)}, bf16[4,5120]{1,0:T(4,128)(2,1)S(1)}, u32[]{:S(2)}, u32[]{:S(2)}) collective-permute-start(bf16[4,5120]{1,0:T(4,128)(2,1)S(1)} %slice.92), channel_id=1, source_target_pairs={{0,128},{8,136},{16,144},{24,152},{32,160},{40,168},{48,176},{56,1... | collective-permute-start | bytes 122888 | tf_op jit(solution)/shard_map/ppermute | solution.py:273
  110.6 2.8 %collective-permute-done.7 = bf16[4,5120]{1,0:T(4,128)(2,1)S(1)} collective-permute-done((bf16[4,5120]{1,0:T(4,128)(2,1)S(1)}, bf16[4,5120]{1,0:T(4,128)(2,1)S(1)}, u32[]{:S(2)}, u32[]{:S(2)}) %collective-permute-start.7) | collective-permute-done | bytes 40992 | tf_op jit(solution)/shard_map/ppermute | solution.py:273
  113.5 13.4 %collective-permute-start.8 = (bf16[2,5120]{1,0:T(2,128)(2,1)S(1)}, bf16[2,5120]{1,0:T(2,128)(2,1)S(1)}, u32[]{:S(2)}, u32[]{:S(2)}) collective-permute-start(bf16[2,5120]{1,0:T(2,128)(2,1)S(1)} %slice.94), channel_id=1, source_target_pairs={{0,256},{8,264},{16,272},{24,280},{32,288},{40,296},{48,304},{56,3... | collective-permute-start | bytes 61448 | tf_op jit(solution)/shard_map/ppermute | solution.py:273
  126.9 4.0 %shard_map.99 = bf16[512,1024]{1,0:T(8,128)(2,1)} custom-call(bf16[8,128,512]{2,1,0:T(8,128)(2,1)S(1)} %all-to-all-done.3.msg_ref, bf16[8,128,128]{2,1,0:T(8,128)(2,1)} %right_ref.1), custom_call_target="tpu_custom_call" | custom-call | flops 300000000 | bytes 3145728 | tf_op jit(solution)/shard_map/pallas_call | solution.py:232
  131.0 0.6 slice.74
  131.6 0.6 slice_bitcast_fusion
  (18 shorter events, 0.3 us)
Async XLA Ops:
  4.5 20.2 %all-to-all-start = ((bf16[8,128,512]{2,1,0:T(8,128)(2,1)}), bf16[8,128,512]{2,1,0:T(8,128)(2,1)S(1)}, u32[]{:S(2)}, u32[]{:S(2)}) async-start(bf16[8,128,512]{2,1,0:T(8,128)(2,1)} %shard_map.93), calls=%async_computation | async-start | bytes 2097152 | tf_op jit(solution)/shard_map/all_to_all | solution.py:245
  24.6 18.6 %all-to-all-start.2 = ((bf16[8,128,512]{2,1,0:T(8,128)(2,1)}), bf16[8,128,512]{2,1,0:T(8,128)(2,1)S(1)}, u32[]{:S(2)}, u32[]{:S(2)}) async-start(bf16[8,128,512]{2,1,0:T(8,128)(2,1)} %shard_map.96), calls=%async_computation.2 | async-start | bytes 2097152 | tf_op jit(solution)/shard_map/all_to_all | solution.py:245
  43.3 18.6 %all-to-all-start.1 = ((bf16[8,128,512]{2,1,0:T(8,128)(2,1)}), bf16[8,128,512]{2,1,0:T(8,128)(2,1)S(1)}, u32[]{:S(2)}, u32[]{:S(2)}) async-start(bf16[8,128,512]{2,1,0:T(8,128)(2,1)} %get-tuple-element.17), calls=%async_computation.1 | async-start | bytes 2097152 | tf_op jit(solution)/shard_map/all_to_all | solution.py:245
  57.0 11.8 %collective-permute-start = (bf16[64,4096]{1,0:T(8,128)(2,1)}, bf16[64,4096]{1,0:T(8,128)(2,1)S(1)}, u32[]{:S(2)}, u32[]{:S(2)}) collective-permute-start(bf16[64,4096]{1,0:T(8,128)(2,1)} %get-tuple-element.22), channel_id=1, source_target_pairs={{0,8},{8,0},{16,24},{24,16},{32,40},{40,32},{48,56},{56,48},{64,72... | collective-permute-start | bytes 1572872 | tf_op jit(solution)/shard_map/ppermute | solution.py:273
  66.9 11.4 %collective-permute-start.3 = (bf16[64,1024]{1,0:T(8,128)(2,1)S(1)}, bf16[64,1024]{1,0:T(8,128)(2,1)S(1)}, u32[]{:S(2)}, u32[]{:S(2)}) collective-permute-start(bf16[64,1024]{1,0:T(8,128)(2,1)S(1)} %get-tuple-element.24), channel_id=1, source_target_pairs={{0,8},{8,0},{16,24},{24,16},{32,40},{40,32},{48,56},{56,48},{64,72... | collective-permute-start | bytes 393224 | tf_op jit(solution)/shard_map/ppermute | solution.py:273
  70.2 10.8 %collective-permute-start.1 = (bf16[32,4096]{1,0:T(8,128)(2,1)S(1)}, bf16[32,4096]{1,0:T(8,128)(2,1)S(1)}, u32[]{:S(2)}, u32[]{:S(2)}) collective-permute-start(bf16[32,4096]{1,0:T(8,128)(2,1)S(1)} %slice.89), channel_id=1, source_target_pairs={{0,32},{8,40},{16,48},{24,56},{32,0},{40,8},{48,16},{56,24},{64,96... | collective-permute-start | bytes 786440 | tf_op jit(solution)/shard_map/ppermute | solution.py:273
  74.0 19.6 %all-to-all-start.3 = ((bf16[8,128,512]{2,1,0:T(8,128)(2,1)}), bf16[8,128,512]{2,1,0:T(8,128)(2,1)S(1)}, u32[]{:S(2)}, u32[]{:S(2)}) async-start(bf16[8,128,512]{2,1,0:T(8,128)(2,1)} %get-tuple-element.26), calls=%async_computation.3 | async-start | bytes 2097152 | tf_op jit(solution)/shard_map/all_to_all | solution.py:245
  78.3 8.0 %collective-permute-start.4 = (bf16[32,1024]{1,0:T(8,128)(2,1)S(1)}, bf16[32,1024]{1,0:T(8,128)(2,1)S(1)}, u32[]{:S(2)}, u32[]{:S(2)}) collective-permute-start(bf16[32,1024]{1,0:T(8,128)(2,1)S(1)} %slice.91), channel_id=1, source_target_pairs={{0,32},{8,40},{16,48},{24,56},{32,0},{40,8},{48,16},{56,24},{64,96... | collective-permute-start | bytes 196616 | tf_op jit(solution)/shard_map/ppermute | solution.py:273
  81.0 12.2 %collective-permute-start.2 = (bf16[16,4096]{1,0:T(8,128)(2,1)S(1)}, bf16[16,4096]{1,0:T(8,128)(2,1)S(1)}, u32[]{:S(2)}, u32[]{:S(2)}) collective-permute-start(bf16[16,4096]{1,0:T(8,128)(2,1)S(1)} %slice.90), channel_id=1, source_target_pairs={{0,64},{8,72},{16,80},{24,88},{32,96},{40,104},{48,112},{56,120},{... | collective-permute-start | bytes 393224 | tf_op jit(solution)/shard_map/ppermute | solution.py:273
  86.3 7.3 %collective-permute-start.5 = (bf16[16,1024]{1,0:T(8,128)(2,1)S(1)}, bf16[16,1024]{1,0:T(8,128)(2,1)S(1)}, u32[]{:S(2)}, u32[]{:S(2)}) collective-permute-start(bf16[16,1024]{1,0:T(8,128)(2,1)S(1)} %slice.93), channel_id=1, source_target_pairs={{0,64},{8,72},{16,80},{24,88},{32,96},{40,104},{48,112},{56,120},{... | collective-permute-start | bytes 98312 | tf_op jit(solution)/shard_map/ppermute | solution.py:273
  93.6 7.8 %collective-permute-start.6 = (bf16[8,5120]{1,0:T(8,128)(2,1)S(1)}, bf16[8,5120]{1,0:T(8,128)(2,1)S(1)}, u32[]{:S(2)}, u32[]{:S(2)}) collective-permute-start(bf16[8,5120]{1,0:T(8,128)(2,1)S(1)} %get-tuple-element.29), channel_id=1, source_target_pairs={{0,16},{8,24},{16,0},{24,8},{32,48},{40,56},{48,32},{56,40},{64,80... | collective-permute-start | bytes 245768 | tf_op jit(solution)/shard_map/ppermute | solution.py:273
  101.5 11.9 %collective-permute-start.7 = (bf16[4,5120]{1,0:T(4,128)(2,1)S(1)}, bf16[4,5120]{1,0:T(4,128)(2,1)S(1)}, u32[]{:S(2)}, u32[]{:S(2)}) collective-permute-start(bf16[4,5120]{1,0:T(4,128)(2,1)S(1)} %slice.92), channel_id=1, source_target_pairs={{0,128},{8,136},{16,144},{24,152},{32,160},{40,168},{48,176},{56,1... | collective-permute-start | bytes 122888 | tf_op jit(solution)/shard_map/ppermute | solution.py:273
  113.5 17.5 %collective-permute-start.8 = (bf16[2,5120]{1,0:T(2,128)(2,1)S(1)}, bf16[2,5120]{1,0:T(2,128)(2,1)S(1)}, u32[]{:S(2)}, u32[]{:S(2)}) collective-permute-start(bf16[2,5120]{1,0:T(2,128)(2,1)S(1)} %slice.94), channel_id=1, source_target_pairs={{0,256},{8,264},{16,272},{24,280},{32,288},{40,296},{48,304},{56,3... | collective-permute-start | bytes 61448 | tf_op jit(solution)/shard_map/ppermute | solution.py:273

commit v3 on v2

--- a/solution.py
+++ b/solution.py
@@ -15,7 +15,8 @@
 ROWS = 512
 PIECE = 16
 PAIR = 2
-STEPS = (0, 2, 3, 1, 4, 5)
+STEPS = (0, 2, 3)
+SHARED = (5, 4, 1)
 MIB = 1 << 20
 BF16 = jnp.bfloat16
 F32 = jnp.float32
@@ -40,11 +41,13 @@
 def shard_matrix(place):
     to = lax.broadcasted_iota(jnp.int32, (BIN, BIN), 0)
     come = lax.broadcasted_iota(jnp.int32, (BIN, BIN), 1)
-    theirs = jnp.zeros_like(to)
-    for step, bit in enumerate(STEPS):
-        theirs = theirs | ((1 - ((to >> (len(STEPS) - step)) & 1)) << bit)
-    wanted = ((theirs ^ place) << 1) | (to & 1)
-    return jnp.where(come == wanted, 1.0, 0.0).astype(BF16)
+    owner = jnp.zeros_like(to)
+    for at, bit in enumerate(STEPS + SHARED):
+        here = (to >> (len(STEPS + SHARED) - at)) & 1
+        if bit in STEPS:
+            here = (1 - here) ^ ((place >> bit) & 1)
+        owner = owner | (here << bit)
+    return jnp.where(come == ((owner << 1) | (to & 1)), 1.0, 0.0).astype(BF16)
 
 
 def scatter_rows(out_ref, slot, value):
@@ -60,10 +63,30 @@
             held_ref[b, src * PIECE : (src + 1) * PIECE, :] = swapped[b * PIECE : (b + 1) * PIECE, :]
 
 
-def right_kernel(dims, x_ref, w_ref, out_ref):
-    for k in range(PAIR):
-        value = dot(w_ref[k], x_ref[:, k * BIN : (k + 1) * BIN], dims).astype(BF16)
-        scatter_rows(out_ref, k, value)
+def fetch(src, dst, sem):
+    copy = pltpu.make_async_copy(src, dst, sem)
+    copy.start()
+    return copy
+
+
+def right_kernel(dims, x_hbm, w_hbm, out_hbm, x_ref, w_ref, out_ref, w_sem, in_sem, out_sem):
+    w_copy = fetch(w_hbm, w_ref, w_sem)
+    wide = PAIR * BIN
+    x_copies = []
+    for p in range(OWNED // PAIR):
+        cols = pl.ds(p * wide, wide)
+        x_copies.append(fetch(x_hbm.at[:, cols], x_ref.at[:, cols], in_sem.at[p]))
+    w_copy.wait()
+    out_copies = []
+    for p in range(OWNED // PAIR):
+        x_copies[p].wait()
+        for k in range(p * PAIR, (p + 1) * PAIR):
+            value = dot(w_ref[k], x_ref[:, k * BIN : (k + 1) * BIN], dims).astype(BF16)
+            scatter_rows(out_ref, k, value)
+        rows = pl.ds(p * PAIR * PIECE, PAIR * PIECE)
+        out_copies.append(fetch(out_ref.at[:, rows, :], out_hbm.at[:, rows, :], out_sem.at[p]))
+    for copy in out_copies:
+        copy.wait()
 
 
 def up_kernel(place_ref, msg_ref, left_ref, down_ref, out_ref, saved_ref, slope_ref, held_ref, shard_ref):
@@ -104,33 +127,48 @@
     keep_ref[...] = part[BIN // 2 :]
 
 
-def out_kernel(place_ref, msg_ref, left_ref, cot_ref, out_ref, send_ref, keep_ref, held_ref, shard_ref):
-    step = pl.program_id(0)
-
-    @pl.when(step == 0)
-    def _():
-        gather_rows(msg_ref, held_ref)
-        shard_ref[...] = shard_matrix(place_ref[0])
-
-    for k in range(PAIR):
-        cols = slice(k * BIN, (k + 1) * BIN)
-        w = held_ref[step * PAIR + k]
-        part = dot(dot(shard_ref[...], w, NN).astype(BF16), cot_ref[:, cols], NN)
-        send_ref[:, cols] = part[: BIN // 2].astype(BF16)
-        keep_ref[:, cols] = part[BIN // 2 :]
-        out_ref[:, cols] = dot(w, left_ref[k], TN).astype(BF16)
-
-
-def in_kernel(msg_ref, right_ref, out_ref, held_ref):
-    step = pl.program_id(0)
-
-    @pl.when(step == 0)
-    def _():
-        gather_rows(msg_ref, held_ref)
-
-    for k in range(PAIR):
-        w = held_ref[step * PAIR + k]
-        out_ref[:, k * BIN : (k + 1) * BIN] = dot(w, right_ref[k], TT).astype(BF16)
+def out_kernel(
+    place_ref, msg_ref, left_hbm, cot_hbm, out_hbm, send_ref, keep_ref,
+    held_ref, left_ref, cot_ref, out_ref, left_sem, in_sem, out_sem,
+):
+    wide = PAIR * BIN
+    left_copy = fetch(left_hbm, left_ref, left_sem)
+    cot_copies = []
+    for p in range(OWNED // PAIR):
+        cols = pl.ds(p * wide, wide)
+        cot_copies.append(fetch(cot_hbm.at[:, cols], cot_ref.at[:, cols], in_sem.at[p]))
+    gather_rows(msg_ref, held_ref)
+    shard = shard_matrix(place_ref[0])
+    left_copy.wait()
+    out_copies = []
+    for p in range(OWNED // PAIR):
+        cot_copies[p].wait()
+        for k in range(p * PAIR, (p + 1) * PAIR):
+            cols = slice(k * BIN, (k + 1) * BIN)
+            w = held_ref[k]
+            part = dot(dot(shard, w, NN).astype(BF16), cot_ref[:, cols], NN)
+            send_ref[:, cols] = part[: BIN // 2].astype(BF16)
+            keep_ref[:, cols] = part[BIN // 2 :]
+            out_ref[:, cols] = dot(w, left_ref[k], TN).astype(BF16)
+        cols = pl.ds(p * wide, wide)
+        out_copies.append(fetch(out_ref.at[:, cols], out_hbm.at[:, cols], out_sem.at[p]))
+    for copy in out_copies:
+        copy.wait()
+
+
+def in_kernel(msg_ref, right_hbm, out_hbm, held_ref, right_ref, out_ref, right_sem, out_sem):
+    wide = PAIR * BIN
+    right_copy = fetch(right_hbm, right_ref, right_sem)
+    gather_rows(msg_ref, held_ref)
+    right_copy.wait()
+    out_copies = []
+    for p in range(OWNED // PAIR):
+        for k in range(p * PAIR, (p + 1) * PAIR):
+            out_ref[:, k * BIN : (k + 1) * BIN] = dot(held_ref[k], right_ref[k], TT).astype(BF16)
+        cols = pl.ds(p * wide, wide)
+        out_copies.append(fetch(out_ref.at[:, cols], out_hbm.at[:, cols], out_sem.at[p]))
+    for copy in out_copies:
+        copy.wait()
 
 
 VMEM = pl.BlockSpec(memory_space=pltpu.VMEM)
@@ -174,13 +212,20 @@
 SHARD = pltpu.VMEM((BIN, BIN), BF16)
 
 
+ANY = pl.BlockSpec(memory_space=pl.ANY)
+SQUARES = pltpu.VMEM((OWNED, BIN, BIN), BF16)
+FLAT = pltpu.VMEM((ROWS, OWNED * BIN), BF16)
+ONE = pltpu.SemaphoreType.DMA
+SEMS = pltpu.SemaphoreType.DMA((OWNED // PAIR,))
+
+
 def right(x, w, dims):
     return pl.pallas_call(
         functools.partial(right_kernel, dims),
-        grid=(OWNED // PAIR,),
         out_shape=far(MSG, BF16),
-        in_specs=[columns(ROWS, PAIR * BIN), each((BIN, BIN), PAIR)],
-        out_specs=pieces(PAIR),
+        in_specs=[ANY, ANY],
+        out_specs=ANY,
+        scratch_shapes=[FLAT, SQUARES, pltpu.VMEM(MSG, BF16), ONE, SEMS, SEMS],
         compiler_params=params(16),
         cost_estimate=cost(134, 3),
     )(stay(x), stay(w))
@@ -215,27 +260,24 @@
 
 def out(place, msg, left, cot):
     half = (BIN // 2, OWNED * BIN)
-    wide = PAIR * BIN
     return pl.pallas_call(
         out_kernel,
-        grid=(OWNED // PAIR,),
-        out_shape=[far((ROWS, OWNED * BIN), BF16), shape(half, BF16), shape(half, F32)],
-        in_specs=[SMEM, VMEM, each((BIN, BIN), PAIR), columns(ROWS, wide)],
-        out_specs=[columns(ROWS, wide), columns(BIN // 2, wide), columns(BIN // 2, wide)],
-        scratch_shapes=[HELD, SHARD],
+        out_shape=[far((ROWS, OWNED * BIN), BF16), far(half, BF16), far(half, F32)],
+        in_specs=[SMEM, VMEM, ANY, ANY],
+        out_specs=[ANY, VMEM, VMEM],
+        scratch_shapes=[HELD, SQUARES, FLAT, FLAT, ONE, SEMS, SEMS],
         compiler_params=params(20),
-        cost_estimate=cost(500, 4),
+        cost_estimate=cost(3000, 16),
     )(place, msg, stay(left), stay(cot))
 
 
 def into(msg, rightw):
     return pl.pallas_call(
         in_kernel,
-        grid=(OWNED // PAIR,),
         out_shape=far((ROWS, OWNED * BIN), BF16),
-        in_specs=[VMEM, each((BIN, BIN), PAIR)],
-        out_specs=columns(ROWS, PAIR * BIN),
-        scratch_shapes=[HELD],
+        in_specs=[VMEM, ANY],
+        out_specs=ANY,
+        scratch_shapes=[HELD, SQUARES, FLAT, ONE, SEMS],
         compiler_params=params(20),
         cost_estimate=cost(300, 3),
     )(msg, stay(rightw))
@@ -245,26 +287,25 @@
     return lax.all_to_all(msg, "blk", split_axis=0, concat_axis=0, tiled=True)
 
 
-def join_kernel(up_keep_ref, up_far_ref, down_keep_ref, down_far_ref, send_ref, keep_ref):
-    half = send_ref.shape[0]
+def join_kernel(up_keep_ref, up_far_ref, down_keep_ref, down_far_ref, out_ref):
     at = 0
-    for kept, far in ((up_keep_ref, up_far_ref), (down_keep_ref, down_far_ref)):
+    for kept, far_ref in ((up_keep_ref, up_far_ref), (down_keep_ref, down_far_ref)):
         cols = slice(at, at + kept.shape[1])
         at += kept.shape[1]
-        total = kept[...] + far[...].astype(F32)
-        send_ref[:, cols] = total[:half].astype(BF16)
-        keep_ref[:, cols] = total[half:]
+        total = (kept[...] + far_ref[...].astype(F32)).astype(BF16)
+        for n in range(out_ref.shape[0]):
+            out_ref[n, :, cols] = total[2 * n : 2 * n + 2]
 
 
 def join(up_keep, up_far, down_keep, down_far):
-    dims = (up_keep.shape[0] // 2, up_keep.shape[1] + down_keep.shape[1])
+    dims = (up_keep.shape[0] // 2, 2, up_keep.shape[1] + down_keep.shape[1])
     return pl.pallas_call(
         join_kernel,
-        out_shape=[shape(dims, BF16), shape(dims, F32)],
+        out_shape=shape(dims, BF16),
         in_specs=[VMEM] * 4,
-        out_specs=[VMEM] * 2,
+        out_specs=VMEM,
         compiler_params=params(8),
-        cost_estimate=cost(1, 3),
+        cost_estimate=cost(1, 1),
     )(up_keep, up_far, down_keep, down_far)
 
 
@@ -280,15 +321,24 @@
 
 
 def sum_over_dp(up_send, up_keep, down_send, down_keep, grad_u, factor):
-    for step in range(2):
+    for step in range(len(STEPS) - 1):
         up_send, up_keep = halve(up_send, up_keep, step)
         down_send, down_keep = halve(down_send, down_keep, step)
-    up_far, down_far = swap_halves(up_send, 2), swap_halves(down_send, 2)
-    send, keep = join(up_keep, up_far, down_keep, down_far)
-    send, grad_u = lax.optimization_barrier((send, grad_u))
-    for step in range(3, len(STEPS) - 1):
-        send, keep = halve(send, keep, step)
-    total = (keep + swap_halves(send, len(STEPS) - 1).astype(F32)) * factor
+    last = len(STEPS) - 1
+    up_far, down_far = swap_halves(up_send, last), swap_halves(down_send, last)
+    total = join(up_keep, up_far, down_keep, down_far)
+    total, grad_u = lax.optimization_barrier((total, grad_u))
+    count = lax.axis_size("dp")
+    mask = sum(1 << bit for bit in SHARED)
+    groups = []
+    for first in range(count):
+        if first & mask == 0:
+            members = [0]
+            for bit in SHARED:
+                members = [m | (b << bit) for m in members for b in (0, 1)]
+            groups.append([first | m for m in members])
+    total = lax.all_to_all(total, "dp", 0, 0, axis_index_groups=groups, tiled=True)
+    total = jnp.sum(total.astype(F32), axis=0) * factor
     split = OWNED * BHID
     up_grad = total[:, :split].reshape(-1, OWNED, BHID).transpose(1, 0, 2)
     down_grad = total[:, split:].reshape(-1, OWNED, BIN).transpose(1, 0, 2)

time: 134 us -> 127 us (0.948)
  the two profiles are of different devices: /device:TPU:6 before, /device:TPU:4 now
where the time goes in v3:
time: 127 us; the launch traced here: 126 us
  starting transfers between devices  51.5 us (41%)
  waiting for transfers between devices  37.4 us (29%)
  Pallas kernels  34.5 us (27%)
  local copies, waits for them, and re-layouts  1.31 us (1%)
    all_to_all x4, waiting for transfers between devices, exchange(): return lax.all_to_all(msg, 'blk', split_axis=0, concat_axis=0, tiled=True)  19.4 us
    ppermute x6, starting transfers between devices, swap_halves(): lax.ppermute(send, 'dp', [(d, d ^ bit) for d in range(lax.axis_size('dp'))])  18 us
    all_to_all x1, starting transfers between devices, sum_over_dp(): lax.all_to_all(total, 'dp', 0, 0, axis_index_groups=groups, tiled=True)  17.5 us
    all_to_all x4, starting transfers between devices, exchange(): return lax.all_to_all(msg, 'blk', split_axis=0, concat_axis=0, tiled=True)  16 us
    all_to_all x1, waiting for transfers between devices, sum_over_dp(): lax.all_to_all(total, 'dp', 0, 0, axis_index_groups=groups, tiled=True)  12.4 us
    pallas_call x1, Pallas kernels, up(): pl.pallas_call(up_kernel, grid=(OWNED,), out_shape=[far(MSG, BF16), far((...  10.9 us
    pallas_call x1, Pallas kernels, back(): pl.pallas_call(back_kernel, grid=(OWNED,), out_shape=[far(MSG, BF16), far...  9.49 us
    pallas_call x2, Pallas kernels, right(): pl.pallas_call(functools.partial(right_kernel, dims), out_shape=far(MSG,...  5.9 us
  transfers between devices with their start and end apart: 11, of which 7 were waited for; matrix products, arithmetic and copies ran while one was open for 0% of the time, Pallas kernels for 25%

profile of v3, /device:TPU:4, one launch (start us, length us, event | category | flops | bytes accessed | tf_op | source)
XLA Modules:
  0.0 125.9 jit_solution(8133171832618958567)
XLA Ops:
  0.6 3.0 %shard_map.93 = bf16[8,128,512]{2,1,0:T(8,128)(2,1)} custom-call(bf16[512,1024]{1,0:T(8,128)(2,1)} %x_hbm.2, bf16[8,128,128]{2,1,0:T(8,128)(2,1)} %right_hbm.1), custom_call_target="tpu_custom_call" | custom-call | flops 134000000 | bytes 3145728 | tf_op jit(solution)/shard_map/pallas_call | solution.py:223
  3.6 5.1 %all-to-all-start = ((bf16[8,128,512]{2,1,0:T(8,128)(2,1)}), bf16[8,128,512]{2,1,0:T(8,128)(2,1)S(1)}, u32[]{:S(2)}, u32[]{:S(2)}) async-start(bf16[8,128,512]{2,1,0:T(8,128)(2,1)} %shard_map.93), calls=%async_computation | async-start | bytes 2097152 | tf_op jit(solution)/shard_map/all_to_all | solution.py:287
  8.7 2.9 %shard_map.96 = bf16[8,128,512]{2,1,0:T(8,128)(2,1)} custom-call(bf16[512,1024]{1,0:T(8,128)(2,1)} %x_hbm.3, bf16[8,128,128]{2,1,0:T(8,128)(2,1)} %w_hbm.3), custom_call_target="tpu_custom_call" | custom-call | flops 134000000 | bytes 3145728 | tf_op jit(solution)/shard_map/pallas_call | solution.py:223
  11.7 11.9 %all-to-all-done.msg_ref = bf16[8,128,512]{2,1,0:T(8,128)(2,1)S(1)} async-done(((bf16[8,128,512]{2,1,0:T(8,128)(2,1)}), bf16[8,128,512]{2,1,0:T(8,128)(2,1)S(1)}, u32[]{:S(2)}, u32[]{:S(2)}) %all-to-all-start) | async-done | bytes 1048608 | tf_op jit(solution)/shard_map/all_to_all | solution.py:287
  23.5 3.6 %all-to-all-start.2 = ((bf16[8,128,512]{2,1,0:T(8,128)(2,1)}), bf16[8,128,512]{2,1,0:T(8,128)(2,1)S(1)}, u32[]{:S(2)}, u32[]{:S(2)}) async-start(bf16[8,128,512]{2,1,0:T(8,128)(2,1)} %shard_map.96), calls=%async_computation.2 | async-start | bytes 2097152 | tf_op jit(solution)/shard_map/all_to_all | solution.py:287
  27.2 10.9 %shard_map.94 = (bf16[8,128,512]{2,1,0:T(8,128)(2,1)}, bf16[8,128,512]{2,1,0:T(8,128)(2,1)}, bf16[8,512,512]{2,1,0:T(8,128)(2,1)}) custom-call(s32[1]{0:T(128)} %bitcast.place_ref, bf16[8,128,512]{2,1,0:T(8,128)(2,1)S(1)} %all-to-all-done.msg_ref, bf16[8,128,512]{2,1,0:T(8,128)(2,1)} %left_ref.3, bf16[8,512,128]{2,1,0:T(8,128)(2,1)} %down_ref.3), custom_call_target="tpu_custom_call" | custom-call | flops 1300000000 | bytes 9437184 | tf_op jit(solution)/shard_map/pallas_call | solution.py:235
  38.1 4.0 %all-to-all-done.2.msg_ref = bf16[8,128,512]{2,1,0:T(8,128)(2,1)S(1)} async-done(((bf16[8,128,512]{2,1,0:T(8,128)(2,1)}), bf16[8,128,512]{2,1,0:T(8,128)(2,1)S(1)}, u32[]{:S(2)}, u32[]{:S(2)}) %all-to-all-start.2) | async-done | bytes 1048608 | tf_op jit(solution)/shard_map/all_to_all | solution.py:287
  42.2 3.6 %all-to-all-start.1 = ((bf16[8,128,512]{2,1,0:T(8,128)(2,1)}), bf16[8,128,512]{2,1,0:T(8,128)(2,1)S(1)}, u32[]{:S(2)}, u32[]{:S(2)}) async-start(bf16[8,128,512]{2,1,0:T(8,128)(2,1)} %get-tuple-element.15), calls=%async_computation.1 | async-start | bytes 2097152 | tf_op jit(solution)/shard_map/all_to_all | solution.py:287
  45.8 9.5 %shard_map.97 = (bf16[8,128,512]{2,1,0:T(8,128)(2,1)}, bf16[64,4096]{1,0:T(8,128)(2,1)}, f32[64,4096]{1,0:T(8,128)}) custom-call(bf16[8,128,512]{2,1,0:T(8,128)(2,1)S(1)} %all-to-all-done.2.msg_ref, bf16[8,128,512]{2,1,0:T(8,128)(2,1)} %get-tuple-element.17.saved_ref, bf16[8,512,512]{2,1,0:T(8,128)(2,1)} %get-tuple-element.18.slope_ref, ...), custom_call_target="tpu_custom_call" | custom-call | flops 1800000000 | bytes 11534336 | tf_op jit(solution)/shard_map/pallas_call | solution.py:249
  55.3 2.0 %collective-permute-start = (bf16[64,4096]{1,0:T(8,128)(2,1)}, bf16[64,4096]{1,0:T(8,128)(2,1)S(1)}, u32[]{:S(2)}, u32[]{:S(2)}) collective-permute-start(bf16[64,4096]{1,0:T(8,128)(2,1)} %get-tuple-element.20), channel_id=1, source_target_pairs={{0,8},{8,0},{16,24},{24,16},{32,40},{40,32},{48,56},{56,48},{64,72... | collective-permute-start | bytes 1572872 | tf_op jit(solution)/shard_map/ppermute | solution.py:314
  57.3 3.4 %all-to-all-done.1.msg_ref = bf16[8,128,512]{2,1,0:T(8,128)(2,1)S(1)} async-done(((bf16[8,128,512]{2,1,0:T(8,128)(2,1)}), bf16[8,128,512]{2,1,0:T(8,128)(2,1)S(1)}, u32[]{:S(2)}, u32[]{:S(2)}) %all-to-all-start.1) | async-done | bytes 1048608 | tf_op jit(solution)/shard_map/all_to_all | solution.py:287
  60.8 5.0 %shard_map.95 = (bf16[512,1024]{1,0:T(8,128)(2,1)}, bf16[64,1024]{1,0:T(8,128)(2,1)}, f32[64,1024]{1,0:T(8,128)}) custom-call(s32[1]{0:T(128)} %bitcast.place_ref, bf16[8,128,512]{2,1,0:T(8,128)(2,1)S(1)} %all-to-all-done.1.msg_ref, bf16[8,128,128]{2,1,0:T(8,128)(2,1)} %w_hbm.3, bf16[512,1024]{1,0:T(8,128)(2,1)} %x_hbm.3), custom_call_target="tpu_custom_call" | custom-call | flops 3000000000 | bytes 16777216 | tf_op jit(solution)/shard_map/pallas_call | solution.py:263
  65.8 0.0 copy-start.1
  65.8 2.1 %collective-permute-start.3 = (bf16[64,1024]{1,0:T(8,128)(2,1)}, bf16[64,1024]{1,0:T(8,128)(2,1)S(1)}, u32[]{:S(2)}, u32[]{:S(2)}) collective-permute-start(bf16[64,1024]{1,0:T(8,128)(2,1)} %get-tuple-element.22), channel_id=1, source_target_pairs={{0,8},{8,0},{16,24},{24,16},{32,40},{40,32},{48,56},{56,48},{64,72... | collective-permute-start | bytes 393224 | tf_op jit(solution)/shard_map/ppermute | solution.py:314
  67.9 0.0 collective-permute-done
  67.9 0.1 convert_add_fusion
  68.0 3.8 %collective-permute-start.1 = (bf16[32,4096]{1,0:T(8,128)(2,1)S(1)}, bf16[32,4096]{1,0:T(8,128)(2,1)S(1)}, u32[]{:S(2)}, u32[]{:S(2)}) collective-permute-start(bf16[32,4096]{1,0:T(8,128)(2,1)S(1)} %slice.61), channel_id=1, source_target_pairs={{0,32},{8,40},{16,48},{24,56},{32,0},{40,8},{48,16},{56,24},{64,96... | collective-permute-start | bytes 786440 | tf_op jit(solution)/shard_map/ppermute | solution.py:314
  71.8 3.7 %all-to-all-start.3 = ((bf16[8,128,512]{2,1,0:T(8,128)(2,1)}), bf16[8,128,512]{2,1,0:T(8,128)(2,1)S(1)}, u32[]{:S(2)}, u32[]{:S(2)}) async-start(bf16[8,128,512]{2,1,0:T(8,128)(2,1)} %get-tuple-element.23), calls=%async_computation.3 | async-start | bytes 2097152 | tf_op jit(solution)/shard_map/all_to_all | solution.py:287
  75.5 0.0 collective-permute-done.3
  75.6 2.1 %collective-permute-start.4 = (bf16[32,1024]{1,0:T(8,128)(2,1)S(1)}, bf16[32,1024]{1,0:T(8,128)(2,1)S(1)}, u32[]{:S(2)}, u32[]{:S(2)}) collective-permute-start(bf16[32,1024]{1,0:T(8,128)(2,1)S(1)} %slice.63), channel_id=1, source_target_pairs={{0,32},{8,40},{16,48},{24,56},{32,0},{40,8},{48,16},{56,24},{64,96... | collective-permute-start | bytes 196616 | tf_op jit(solution)/shard_map/ppermute | solution.py:314
  77.6 1.2 collective-permute-done.1
  78.9 5.2 %collective-permute-start.2 = (bf16[16,4096]{1,0:T(8,128)(2,1)S(1)}, bf16[16,4096]{1,0:T(8,128)(2,1)S(1)}, u32[]{:S(2)}, u32[]{:S(2)}) collective-permute-start(bf16[16,4096]{1,0:T(8,128)(2,1)S(1)} %slice.62), channel_id=1, source_target_pairs={{0,64},{8,72},{16,80},{24,88},{32,96},{40,104},{48,112},{56,120},{... | collective-permute-start | bytes 393224 | tf_op jit(solution)/shard_map/ppermute | solution.py:314
  84.1 2.8 %collective-permute-start.5 = (bf16[16,1024]{1,0:T(8,128)(2,1)S(1)}, bf16[16,1024]{1,0:T(8,128)(2,1)S(1)}, u32[]{:S(2)}, u32[]{:S(2)}) collective-permute-start(bf16[16,1024]{1,0:T(8,128)(2,1)S(1)} %slice.64), channel_id=1, source_target_pairs={{0,64},{8,72},{16,80},{24,88},{32,96},{40,104},{48,112},{56,120},{... | collective-permute-start | bytes 98312 | tf_op jit(solution)/shard_map/ppermute | solution.py:314
  87.0 4.1 %collective-permute-done.2.up_far_ref = bf16[16,4096]{1,0:T(8,128)(2,1)S(1)} collective-permute-done((bf16[16,4096]{1,0:T(8,128)(2,1)S(1)}, bf16[16,4096]{1,0:T(8,128)(2,1)S(1)}, u32[]{:S(2)}, u32[]{:S(2)}) %collective-permute-start.2) | collective-permute-done | bytes 131104 | tf_op jit(solution)/shard_map/ppermute | solution.py:314
  91.0 0.4 collective-permute-done.5.down_far_ref
  91.4 0.7 shard_map.98
  92.1 17.5 %all-to-all-start.4 = ((bf16[8,2,5120]{2,1,0:T(2,128)(2,1)}), bf16[8,2,5120]{2,1,0:T(2,128)(2,1)S(1)}, u32[]{:S(2)}, u32[]{:S(2)}) async-start(bf16[8,2,5120]{2,1,0:T(2,128)(2,1)} %shard_map.98), calls=%async_computation.4 | async-start | bytes 327680 | tf_op jit(solution)/shard_map/all_to_all | solution.py:340
  109.6 2.5 %shard_map.99 = bf16[512,1024]{1,0:T(8,128)(2,1)} custom-call(bf16[8,128,512]{2,1,0:T(8,128)(2,1)S(1)} %all-to-all-done.3.msg_ref, bf16[8,128,128]{2,1,0:T(8,128)(2,1)} %right_hbm.1), custom_call_target="tpu_custom_call" | custom-call | flops 300000000 | bytes 3145728 | tf_op jit(solution)/shard_map/pallas_call | solution.py:275
  112.1 12.4 %all-to-all-done.4 = bf16[8,2,5120]{2,1,0:T(2,128)(2,1)S(1)} async-done(((bf16[8,2,5120]{2,1,0:T(2,128)(2,1)}), bf16[8,2,5120]{2,1,0:T(2,128)(2,1)S(1)}, u32[]{:S(2)}, u32[]{:S(2)}) %all-to-all-start.4) | async-done | bytes 163872 | tf_op jit(solution)/shard_map/all_to_all | solution.py:340
  124.5 0.1 convert_reduce_fusion
  124.7 0.6 slice.52
  125.3 0.6 slice_bitcast_fusion
  (15 shorter events, 0.2 us)
Async XLA Ops:
  3.6 19.9 %all-to-all-start = ((bf16[8,128,512]{2,1,0:T(8,128)(2,1)}), bf16[8,128,512]{2,1,0:T(8,128)(2,1)S(1)}, u32[]{:S(2)}, u32[]{:S(2)}) async-start(bf16[8,128,512]{2,1,0:T(8,128)(2,1)} %shard_map.93), calls=%async_computation | async-start | bytes 2097152 | tf_op jit(solution)/shard_map/all_to_all | solution.py:287
  23.5 18.6 %all-to-all-start.2 = ((bf16[8,128,512]{2,1,0:T(8,128)(2,1)}), bf16[8,128,512]{2,1,0:T(8,128)(2,1)S(1)}, u32[]{:S(2)}, u32[]{:S(2)}) async-start(bf16[8,128,512]{2,1,0:T(8,128)(2,1)} %shard_map.96), calls=%async_computation.2 | async-start | bytes 2097152 | tf_op jit(solution)/shard_map/all_to_all | solution.py:287
  42.2 18.6 %all-to-all-start.1 = ((bf16[8,128,512]{2,1,0:T(8,128)(2,1)}), bf16[8,128,512]{2,1,0:T(8,128)(2,1)S(1)}, u32[]{:S(2)}, u32[]{:S(2)}) async-start(bf16[8,128,512]{2,1,0:T(8,128)(2,1)} %get-tuple-element.15), calls=%async_computation.1 | async-start | bytes 2097152 | tf_op jit(solution)/shard_map/all_to_all | solution.py:287
  55.3 12.6 %copy-start = (f32[64,4096]{1,0:T(8,128)S(1)}, f32[64,4096]{1,0:T(8,128)}, u32[]{:S(2)}) copy-start(f32[64,4096]{1,0:T(8,128)} %get-tuple-element.19) | copy-start | bytes 3145732
  55.3 12.6 %collective-permute-start = (bf16[64,4096]{1,0:T(8,128)(2,1)}, bf16[64,4096]{1,0:T(8,128)(2,1)S(1)}, u32[]{:S(2)}, u32[]{:S(2)}) collective-permute-start(bf16[64,4096]{1,0:T(8,128)(2,1)} %get-tuple-element.20), channel_id=1, source_target_pairs={{0,8},{8,0},{16,24},{24,16},{32,40},{40,32},{48,56},{56,48},{64,72... | collective-permute-start | bytes 1572872 | tf_op jit(solution)/shard_map/ppermute | solution.py:314
  65.8 9.7 %copy-start.1 = (f32[64,1024]{1,0:T(8,128)S(1)}, f32[64,1024]{1,0:T(8,128)}, u32[]{:S(2)}) copy-start(f32[64,1024]{1,0:T(8,128)} %get-tuple-element.21) | copy-start | bytes 786436
  65.8 9.7 %collective-permute-start.3 = (bf16[64,1024]{1,0:T(8,128)(2,1)}, bf16[64,1024]{1,0:T(8,128)(2,1)S(1)}, u32[]{:S(2)}, u32[]{:S(2)}) collective-permute-start(bf16[64,1024]{1,0:T(8,128)(2,1)} %get-tuple-element.22), channel_id=1, source_target_pairs={{0,8},{8,0},{16,24},{24,16},{32,40},{40,32},{48,56},{56,48},{64,72... | collective-permute-start | bytes 393224 | tf_op jit(solution)/shard_map/ppermute | solution.py:314
  68.0 10.8 %collective-permute-start.1 = (bf16[32,4096]{1,0:T(8,128)(2,1)S(1)}, bf16[32,4096]{1,0:T(8,128)(2,1)S(1)}, u32[]{:S(2)}, u32[]{:S(2)}) collective-permute-start(bf16[32,4096]{1,0:T(8,128)(2,1)S(1)} %slice.61), channel_id=1, source_target_pairs={{0,32},{8,40},{16,48},{24,56},{32,0},{40,8},{48,16},{56,24},{64,96... | collective-permute-start | bytes 786440 | tf_op jit(solution)/shard_map/ppermute | solution.py:314
  71.8 20.3 %all-to-all-start.3 = ((bf16[8,128,512]{2,1,0:T(8,128)(2,1)}), bf16[8,128,512]{2,1,0:T(8,128)(2,1)S(1)}, u32[]{:S(2)}, u32[]{:S(2)}) async-start(bf16[8,128,512]{2,1,0:T(8,128)(2,1)} %get-tuple-element.23), calls=%async_computation.3 | async-start | bytes 2097152 | tf_op jit(solution)/shard_map/all_to_all | solution.py:287
  75.6 8.5 %collective-permute-start.4 = (bf16[32,1024]{1,0:T(8,128)(2,1)S(1)}, bf16[32,1024]{1,0:T(8,128)(2,1)S(1)}, u32[]{:S(2)}, u32[]{:S(2)}) collective-permute-start(bf16[32,1024]{1,0:T(8,128)(2,1)S(1)} %slice.63), channel_id=1, source_target_pairs={{0,32},{8,40},{16,48},{24,56},{32,0},{40,8},{48,16},{56,24},{64,96... | collective-permute-start | bytes 196616 | tf_op jit(solution)/shard_map/ppermute | solution.py:314
  78.9 12.2 %collective-permute-start.2 = (bf16[16,4096]{1,0:T(8,128)(2,1)S(1)}, bf16[16,4096]{1,0:T(8,128)(2,1)S(1)}, u32[]{:S(2)}, u32[]{:S(2)}) collective-permute-start(bf16[16,4096]{1,0:T(8,128)(2,1)S(1)} %slice.62), channel_id=1, source_target_pairs={{0,64},{8,72},{16,80},{24,88},{32,96},{40,104},{48,112},{56,120},{... | collective-permute-start | bytes 393224 | tf_op jit(solution)/shard_map/ppermute | solution.py:314
  84.1 7.3 %collective-permute-start.5 = (bf16[16,1024]{1,0:T(8,128)(2,1)S(1)}, bf16[16,1024]{1,0:T(8,128)(2,1)S(1)}, u32[]{:S(2)}, u32[]{:S(2)}) collective-permute-start(bf16[16,1024]{1,0:T(8,128)(2,1)S(1)} %slice.64), channel_id=1, source_target_pairs={{0,64},{8,72},{16,80},{24,88},{32,96},{40,104},{48,112},{56,120},{... | collective-permute-start | bytes 98312 | tf_op jit(solution)/shard_map/ppermute | solution.py:314
  92.1 32.4 %all-to-all-start.4 = ((bf16[8,2,5120]{2,1,0:T(2,128)(2,1)}), bf16[8,2,5120]{2,1,0:T(2,128)(2,1)S(1)}, u32[]{:S(2)}, u32[]{:S(2)}) async-start(bf16[8,2,5120]{2,1,0:T(2,128)(2,1)} %shard_map.98), calls=%async_computation.4 | async-start | bytes 327680 | tf_op jit(solution)/shard_map/all_to_all | solution.py:340

commit v4 on v3

--- a/solution.py
+++ b/solution.py
@@ -15,8 +15,9 @@
 ROWS = 512
 PIECE = 16
 PAIR = 2
-STEPS = (0, 2, 3)
-SHARED = (5, 4, 1)
+STEPS = (0, 2)
+SHARED = (5, 4, 3, 1)
+DP = ("z8", "z4", "z2", "z1", "far", "core")
 MIB = 1 << 20
 BF16 = jnp.bfloat16
 F32 = jnp.float32
@@ -132,24 +133,21 @@
     held_ref, left_ref, cot_ref, out_ref, left_sem, in_sem, out_sem,
 ):
     wide = PAIR * BIN
+    cot_copy = fetch(cot_hbm, cot_ref, in_sem)
     left_copy = fetch(left_hbm, left_ref, left_sem)
-    cot_copies = []
-    for p in range(OWNED // PAIR):
-        cols = pl.ds(p * wide, wide)
-        cot_copies.append(fetch(cot_hbm.at[:, cols], cot_ref.at[:, cols], in_sem.at[p]))
+    shard = shard_matrix(place_ref[0])
     gather_rows(msg_ref, held_ref)
-    shard = shard_matrix(place_ref[0])
     left_copy.wait()
+    cot_copy.wait()
     out_copies = []
     for p in range(OWNED // PAIR):
-        cot_copies[p].wait()
         for k in range(p * PAIR, (p + 1) * PAIR):
             cols = slice(k * BIN, (k + 1) * BIN)
             w = held_ref[k]
+            out_ref[:, cols] = dot(w, left_ref[k], TN).astype(BF16)
             part = dot(dot(shard, w, NN).astype(BF16), cot_ref[:, cols], NN)
             send_ref[:, cols] = part[: BIN // 2].astype(BF16)
             keep_ref[:, cols] = part[BIN // 2 :]
-            out_ref[:, cols] = dot(w, left_ref[k], TN).astype(BF16)
         cols = pl.ds(p * wide, wide)
         out_copies.append(fetch(out_ref.at[:, cols], out_hbm.at[:, cols], out_sem.at[p]))
     for copy in out_copies:
@@ -265,7 +263,7 @@
         out_shape=[far((ROWS, OWNED * BIN), BF16), far(half, BF16), far(half, F32)],
         in_specs=[SMEM, VMEM, ANY, ANY],
         out_specs=[ANY, VMEM, VMEM],
-        scratch_shapes=[HELD, SQUARES, FLAT, FLAT, ONE, SEMS, SEMS],
+        scratch_shapes=[HELD, SQUARES, FLAT, FLAT, ONE, ONE, SEMS],
         compiler_params=params(20),
         cost_estimate=cost(3000, 16),
     )(place, msg, stay(left), stay(cot))
@@ -309,9 +307,12 @@
     )(up_keep, up_far, down_keep, down_far)
 
 
+def axis_of(bit):
+    return DP[len(DP) - 1 - bit]
+
+
 def swap_halves(send, step):
-    bit = 1 << STEPS[step]
-    return lax.ppermute(send, "dp", [(d, d ^ bit) for d in range(lax.axis_size("dp"))])
+    return lax.ppermute(send, axis_of(STEPS[step]), [(0, 1), (1, 0)])
 
 
 def halve(send, keep, step):
@@ -320,34 +321,44 @@
     return total[:rows].astype(BF16), total[rows:]
 
 
-def sum_over_dp(up_send, up_keep, down_send, down_keep, grad_u, factor):
+def finish_kernel(factor, in_ref, up_ref, down_ref):
+    total = in_ref[0].astype(F32)
+    for n in range(1, in_ref.shape[0]):
+        total = total + in_ref[n].astype(F32)
+    total = total * factor
+    at = 0
+    for ref in (up_ref, down_ref):
+        for k in range(OWNED):
+            ref[k] = total[:, at : at + ref.shape[2]]
+            at += ref.shape[2]
+
+
+def finish(pieces_in, factor):
+    rows = pieces_in.shape[1]
+    return pl.pallas_call(
+        functools.partial(finish_kernel, factor),
+        out_shape=[shape((OWNED, rows, BHID), F32), shape((OWNED, rows, BIN), F32)],
+        in_specs=[VMEM],
+        out_specs=[VMEM] * 2,
+        compiler_params=params(8),
+        cost_estimate=cost(1, 1),
+    )(pieces_in)
+
+
+def sum_over_dp(up_half, down_half, grad_u, factor):
     for step in range(len(STEPS) - 1):
-        up_send, up_keep = halve(up_send, up_keep, step)
-        down_send, down_keep = halve(down_send, down_keep, step)
+        up_half = halve(*up_half, step)
+        down_half = halve(*down_half, step)
     last = len(STEPS) - 1
-    up_far, down_far = swap_halves(up_send, last), swap_halves(down_send, last)
-    total = join(up_keep, up_far, down_keep, down_far)
+    total = join(up_half[1], swap_halves(up_half[0], last), down_half[1], swap_halves(down_half[0], last))
     total, grad_u = lax.optimization_barrier((total, grad_u))
-    count = lax.axis_size("dp")
-    mask = sum(1 << bit for bit in SHARED)
-    groups = []
-    for first in range(count):
-        if first & mask == 0:
-            members = [0]
-            for bit in SHARED:
-                members = [m | (b << bit) for m in members for b in (0, 1)]
-            groups.append([first | m for m in members])
-    total = lax.all_to_all(total, "dp", 0, 0, axis_index_groups=groups, tiled=True)
-    total = jnp.sum(total.astype(F32), axis=0) * factor
-    split = OWNED * BHID
-    up_grad = total[:, :split].reshape(-1, OWNED, BHID).transpose(1, 0, 2)
-    down_grad = total[:, split:].reshape(-1, OWNED, BIN).transpose(1, 0, 2)
-    return up_grad, down_grad, grad_u
+    total = lax.all_to_all(total, tuple(axis_of(bit) for bit in SHARED), 0, 0, tiled=True)
+    return (*finish(total, factor), grad_u)
 
 
 def on_device(tokens, up_right, up_left, down_right, down_left, cotangent):
-    place = lax.axis_index("dp").reshape(1).astype(jnp.int32)
-    factor = 1.0 / math.sqrt(tokens.shape[0] * lax.axis_size("dp"))
+    place = lax.axis_index(DP).reshape(1).astype(jnp.int32)
+    factor = 1.0 / math.sqrt(tokens.shape[0] * lax.axis_size(DP))
     v = exchange(right(tokens, up_right, TT))
     grad_z = exchange(right(cotangent, down_left, NT))
     z, saved, slope = up(place, v, up_left, down_right)
@@ -355,26 +366,25 @@
     grad_v, up_send, up_keep = back(grad_z, saved, slope, up_left, down_right)
     grad_u = exchange(grad_v)
     layer_out, down_send, down_keep = out(place, w, down_left, cotangent)
-    up_grad, down_grad, grad_u = sum_over_dp(
-        up_send, up_keep, down_send, down_keep, grad_u, factor
-    )
+    up_grad, down_grad, grad_u = sum_over_dp((up_send, up_keep), (down_send, down_keep), grad_u, factor)
     input_grad = into(grad_u, up_right)
     return (layer_out, input_grad, up_grad, down_grad)
 
 
 def solution(mesh):
+    fine = jax.sharding.Mesh(mesh.devices.reshape((2,) * len(DP) + (GROUPS,)), DP + ("blk",))
     placed = (
-        P("dp", "blk"),
+        P(DP, "blk"),
         P("blk", None, None),
         P("blk", None, None),
         P("blk", None, None),
         P("blk", None, None),
-        P("dp", "blk"),
+        P(DP, "blk"),
     )
     return jax.shard_map(
         on_device,
-        mesh=mesh,
+        mesh=fine,
         in_specs=placed,
-        out_specs=(P("dp", "blk"), P("dp", "blk"), P("blk", "dp", None), P("blk", "dp", None)),
+        out_specs=(P(DP, "blk"), P(DP, "blk"), P("blk", DP, None), P("blk", DP, None)),
         check_vma=False,
     )

time: 127 us -> 128 us (level)
  the two profiles are of different devices: /device:TPU:4 before, /device:TPU:8 now
where the time goes in v4:
time: 128 us; the launch traced here: 127 us
  starting transfers between devices  51.7 us (40%)
  waiting for transfers between devices  38.2 us (30%)
  Pallas kernels  35 us (27%)
    all_to_all x4, starting transfers between devices, exchange(): return lax.all_to_all(msg, 'blk', split_axis=0, concat_axis=0, tiled=True)  23.7 us
    all_to_all x1, waiting for transfers between devices, sum_over_dp(): lax.all_to_all(total, tuple((axis_of(bit) for bit in SHARED)), 0, 0, tile...  21.5 us
    all_to_all x1, starting transfers between devices, sum_over_dp(): lax.all_to_all(total, tuple((axis_of(bit) for bit in SHARED)), 0, 0, tile...  17.2 us
    all_to_all x4, waiting for transfers between devices, exchange(): return lax.all_to_all(msg, 'blk', split_axis=0, concat_axis=0, tiled=True)  11.3 us
    pallas_call x1, Pallas kernels, up(): pl.pallas_call(up_kernel, grid=(OWNED,), out_shape=[far(MSG, BF16), far((...  10.9 us
    ppermute x4, starting transfers between devices, swap_halves(): return lax.ppermute(send, axis_of(STEPS[step]), [(0, 1), (1, 0)])  10.8 us
    pallas_call x1, Pallas kernels, back(): pl.pallas_call(back_kernel, grid=(OWNED,), out_shape=[far(MSG, BF16), far...  9.5 us
    pallas_call x2, Pallas kernels, right(): pl.pallas_call(functools.partial(right_kernel, dims), out_shape=far(MSG,...  5.9 us
  transfers between devices with their start and end apart: 9, of which 6 were waited for; matrix products, arithmetic and copies ran while one was open for 1% of the time, Pallas kernels for 25%

profile of v4, /device:TPU:8, one launch (start us, length us, event | category | flops | bytes accessed | tf_op | source)
XLA Modules:
  0.0 126.8 jit_solution(15710266037466630338)
XLA Ops:
  0.6 3.0 %shard_map.93 = bf16[8,128,512]{2,1,0:T(8,128)(2,1)} custom-call(bf16[512,1024]{1,0:T(8,128)(2,1)} %x_hbm.2, bf16[8,128,128]{2,1,0:T(8,128)(2,1)} %right_hbm.1), custom_call_target="tpu_custom_call" | custom-call | flops 134000000 | bytes 3145728 | tf_op jit(solution)/shard_map/pallas_call | solution.py:221
  3.6 9.3 %all-to-all-start = ((bf16[8,128,512]{2,1,0:T(8,128)(2,1)}), bf16[8,128,512]{2,1,0:T(8,128)(2,1)S(1)}, u32[]{:S(2)}, u32[]{:S(2)}) async-start(bf16[8,128,512]{2,1,0:T(8,128)(2,1)} %shard_map.93), calls=%async_computation | async-start | bytes 2097152 | tf_op jit(solution)/shard_map/all_to_all | solution.py:285
  12.9 2.9 %shard_map.96 = bf16[8,128,512]{2,1,0:T(8,128)(2,1)} custom-call(bf16[512,1024]{1,0:T(8,128)(2,1)} %x_hbm.3, bf16[8,128,128]{2,1,0:T(8,128)(2,1)} %w_hbm.3), custom_call_target="tpu_custom_call" | custom-call | flops 134000000 | bytes 3145728 | tf_op jit(solution)/shard_map/pallas_call | solution.py:221
  15.8 7.3 %all-to-all-done.msg_ref = bf16[8,128,512]{2,1,0:T(8,128)(2,1)S(1)} async-done(((bf16[8,128,512]{2,1,0:T(8,128)(2,1)}), bf16[8,128,512]{2,1,0:T(8,128)(2,1)S(1)}, u32[]{:S(2)}, u32[]{:S(2)}) %all-to-all-start) | async-done | bytes 1048608 | tf_op jit(solution)/shard_map/all_to_all | solution.py:285
  23.1 4.8 %all-to-all-start.2 = ((bf16[8,128,512]{2,1,0:T(8,128)(2,1)}), bf16[8,128,512]{2,1,0:T(8,128)(2,1)S(1)}, u32[]{:S(2)}, u32[]{:S(2)}) async-start(bf16[8,128,512]{2,1,0:T(8,128)(2,1)} %shard_map.96), calls=%async_computation.2 | async-start | bytes 2097152 | tf_op jit(solution)/shard_map/all_to_all | solution.py:285
  27.9 10.9 %shard_map.94 = (bf16[8,128,512]{2,1,0:T(8,128)(2,1)}, bf16[8,128,512]{2,1,0:T(8,128)(2,1)}, bf16[8,512,512]{2,1,0:T(8,128)(2,1)}) custom-call(s32[1]{0:T(128)} %bitcast.place_ref, bf16[8,128,512]{2,1,0:T(8,128)(2,1)S(1)} %all-to-all-done.msg_ref, bf16[8,128,512]{2,1,0:T(8,128)(2,1)} %left_ref.3, bf16[8,512,128]{2,1,0:T(8,128)(2,1)} %down_ref.3), custom_call_target="tpu_custom_call" | custom-call | flops 1300000000 | bytes 9437184 | tf_op jit(solution)/shard_map/pallas_call | solution.py:233
  38.8 1.7 %all-to-all-done.2.msg_ref = bf16[8,128,512]{2,1,0:T(8,128)(2,1)S(1)} async-done(((bf16[8,128,512]{2,1,0:T(8,128)(2,1)}), bf16[8,128,512]{2,1,0:T(8,128)(2,1)S(1)}, u32[]{:S(2)}, u32[]{:S(2)}) %all-to-all-start.2) | async-done | bytes 1048608 | tf_op jit(solution)/shard_map/all_to_all | solution.py:285
  40.5 4.8 %all-to-all-start.1 = ((bf16[8,128,512]{2,1,0:T(8,128)(2,1)}), bf16[8,128,512]{2,1,0:T(8,128)(2,1)S(1)}, u32[]{:S(2)}, u32[]{:S(2)}) async-start(bf16[8,128,512]{2,1,0:T(8,128)(2,1)} %get-tuple-element.17), calls=%async_computation.1 | async-start | bytes 2097152 | tf_op jit(solution)/shard_map/all_to_all | solution.py:285
  45.3 9.5 %shard_map.97 = (bf16[8,128,512]{2,1,0:T(8,128)(2,1)}, bf16[64,4096]{1,0:T(8,128)(2,1)}, f32[64,4096]{1,0:T(8,128)}) custom-call(bf16[8,128,512]{2,1,0:T(8,128)(2,1)S(1)} %all-to-all-done.2.msg_ref, bf16[8,128,512]{2,1,0:T(8,128)(2,1)} %get-tuple-element.19.saved_ref, bf16[8,512,512]{2,1,0:T(8,128)(2,1)} %get-tuple-element.20.slope_ref, ...), custom_call_target="tpu_custom_call" | custom-call | flops 1800000000 | bytes 11534336 | tf_op jit(solution)/shard_map/pallas_call | solution.py:247
  54.8 1.9 %collective-permute-start = (bf16[64,4096]{1,0:T(8,128)(2,1)}, bf16[64,4096]{1,0:T(8,128)(2,1)S(1)}, u32[]{:S(2)}, u32[]{:S(2)}) collective-permute-start(bf16[64,4096]{1,0:T(8,128)(2,1)} %get-tuple-element.22), channel_id=1, source_target_pairs={{0,8},{8,0},{1,9},{9,1},{2,10},{10,2},{3,11},{11,3},{4,12},{12,4},... | collective-permute-start | bytes 1572872 | tf_op jit(solution)/shard_map/ppermute | solution.py:315
  56.7 2.4 %all-to-all-done.1.msg_ref = bf16[8,128,512]{2,1,0:T(8,128)(2,1)S(1)} async-done(((bf16[8,128,512]{2,1,0:T(8,128)(2,1)}), bf16[8,128,512]{2,1,0:T(8,128)(2,1)S(1)}, u32[]{:S(2)}, u32[]{:S(2)}) %all-to-all-start.1) | async-done | bytes 1048608 | tf_op jit(solution)/shard_map/all_to_all | solution.py:285
  59.1 4.8 %all-to-all-start.3 = ((bf16[8,128,512]{2,1,0:T(8,128)(2,1)}), bf16[8,128,512]{2,1,0:T(8,128)(2,1)S(1)}, u32[]{:S(2)}, u32[]{:S(2)}) async-start(bf16[8,128,512]{2,1,0:T(8,128)(2,1)} %get-tuple-element.25), calls=%async_computation.3 | async-start | bytes 2097152 | tf_op jit(solution)/shard_map/all_to_all | solution.py:285
  63.9 0.0 copy-start
  63.9 4.7 %shard_map.95 = (bf16[512,1024]{1,0:T(8,128)(2,1)}, bf16[64,1024]{1,0:T(8,128)(2,1)}, f32[64,1024]{1,0:T(8,128)}) custom-call(s32[1]{0:T(128)} %bitcast.place_ref, bf16[8,128,512]{2,1,0:T(8,128)(2,1)S(1)} %all-to-all-done.1.msg_ref, bf16[8,128,128]{2,1,0:T(8,128)(2,1)} %w_hbm.3, bf16[512,1024]{1,0:T(8,128)(2,1)} %x_hbm.3), custom_call_target="tpu_custom_call" | custom-call | flops 3000000000 | bytes 16777216 | tf_op jit(solution)/shard_map/pallas_call | solution.py:261
  68.6 1.9 %collective-permute-start.2 = (bf16[64,1024]{1,0:T(8,128)(2,1)}, bf16[64,1024]{1,0:T(8,128)(2,1)S(1)}, u32[]{:S(2)}, u32[]{:S(2)}) collective-permute-start(bf16[64,1024]{1,0:T(8,128)(2,1)} %get-tuple-element.24), channel_id=1, source_target_pairs={{0,8},{8,0},{1,9},{9,1},{2,10},{10,2},{3,11},{11,3},{4,12},{12,4},... | collective-permute-start | bytes 393224 | tf_op jit(solution)/shard_map/ppermute | solution.py:315
  70.5 0.0 collective-permute-done
  70.5 0.0 copy-done
  70.6 0.1 convert_add_fusion
  70.7 5.1 %collective-permute-start.1 = (bf16[32,4096]{1,0:T(8,128)(2,1)S(1)}, bf16[32,4096]{1,0:T(8,128)(2,1)S(1)}, u32[]{:S(2)}, u32[]{:S(2)}) collective-permute-start(bf16[32,4096]{1,0:T(8,128)(2,1)S(1)} %slice.24), channel_id=1, source_target_pairs={{0,32},{32,0},{1,33},{33,1},{2,34},{34,2},{3,35},{35,3},{4,36},{36... | collective-permute-start | bytes 786440 | tf_op jit(solution)/shard_map/ppermute | solution.py:315
  75.8 0.0 collective-permute-done.2
  75.8 1.0 convert_add_fusion.1
  76.8 1.9 %collective-permute-start.3 = (bf16[32,1024]{1,0:T(8,128)(2,1)S(1)}, bf16[32,1024]{1,0:T(8,128)(2,1)S(1)}, u32[]{:S(2)}, u32[]{:S(2)}) collective-permute-start(bf16[32,1024]{1,0:T(8,128)(2,1)S(1)} %slice.25), channel_id=1, source_target_pairs={{0,32},{32,0},{1,33},{33,1},{2,34},{34,2},{3,35},{35,3},{4,36},{36... | collective-permute-start | bytes 196616 | tf_op jit(solution)/shard_map/ppermute | solution.py:315
  78.8 4.1 %collective-permute-done.1.up_far_ref = bf16[32,4096]{1,0:T(8,128)(2,1)S(1)} collective-permute-done((bf16[32,4096]{1,0:T(8,128)(2,1)S(1)}, bf16[32,4096]{1,0:T(8,128)(2,1)S(1)}, u32[]{:S(2)}, u32[]{:S(2)}) %collective-permute-start.1) | collective-permute-done | bytes 262176 | tf_op jit(solution)/shard_map/ppermute | solution.py:315
  82.9 1.2 collective-permute-done.3.down_far_ref
  84.1 0.8 shard_map.98
  84.9 0.0 all-to-all-done.3.msg_ref
  84.9 17.2 %all-to-all-start.4 = ((bf16[16,2,5120]{2,1,0:T(2,128)(2,1)}), bf16[16,2,5120]{2,1,0:T(2,128)(2,1)S(1)}, u32[]{:S(2)}, u32[]{:S(2)}) async-start(bf16[16,2,5120]{2,1,0:T(2,128)(2,1)} %shard_map.98), calls=%async_computation.4 | async-start | bytes 655360 | tf_op jit(solution)/shard_map/all_to_all | solution.py:355
  102.1 2.5 %shard_map.99 = bf16[512,1024]{1,0:T(8,128)(2,1)} custom-call(bf16[8,128,512]{2,1,0:T(8,128)(2,1)S(1)} %all-to-all-done.3.msg_ref, bf16[8,128,128]{2,1,0:T(8,128)(2,1)} %right_hbm.1), custom_call_target="tpu_custom_call" | custom-call | flops 300000000 | bytes 3145728 | tf_op jit(solution)/shard_map/pallas_call | solution.py:273
  104.6 21.5 %all-to-all-done.4.in_ref = bf16[16,2,5120]{2,1,0:T(2,128)(2,1)S(1)} async-done(((bf16[16,2,5120]{2,1,0:T(2,128)(2,1)}), bf16[16,2,5120]{2,1,0:T(2,128)(2,1)S(1)}, u32[]{:S(2)}, u32[]{:S(2)}) %all-to-all-start.4) | async-done | bytes 327712 | tf_op jit(solution)/shard_map/all_to_all | solution.py:355
  126.2 0.7 shard_map.100
  (4 shorter events, 0.1 us)
Async XLA Ops:
  3.6 19.5 %all-to-all-start = ((bf16[8,128,512]{2,1,0:T(8,128)(2,1)}), bf16[8,128,512]{2,1,0:T(8,128)(2,1)S(1)}, u32[]{:S(2)}, u32[]{:S(2)}) async-start(bf16[8,128,512]{2,1,0:T(8,128)(2,1)} %shard_map.93), calls=%async_computation | async-start | bytes 2097152 | tf_op jit(solution)/shard_map/all_to_all | solution.py:285
  23.1 17.4 %all-to-all-start.2 = ((bf16[8,128,512]{2,1,0:T(8,128)(2,1)}), bf16[8,128,512]{2,1,0:T(8,128)(2,1)S(1)}, u32[]{:S(2)}, u32[]{:S(2)}) async-start(bf16[8,128,512]{2,1,0:T(8,128)(2,1)} %shard_map.96), calls=%async_computation.2 | async-start | bytes 2097152 | tf_op jit(solution)/shard_map/all_to_all | solution.py:285
  40.5 18.6 %all-to-all-start.1 = ((bf16[8,128,512]{2,1,0:T(8,128)(2,1)}), bf16[8,128,512]{2,1,0:T(8,128)(2,1)S(1)}, u32[]{:S(2)}, u32[]{:S(2)}) async-start(bf16[8,128,512]{2,1,0:T(8,128)(2,1)} %get-tuple-element.17), calls=%async_computation.1 | async-start | bytes 2097152 | tf_op jit(solution)/shard_map/all_to_all | solution.py:285
  54.8 15.7 %collective-permute-start = (bf16[64,4096]{1,0:T(8,128)(2,1)}, bf16[64,4096]{1,0:T(8,128)(2,1)S(1)}, u32[]{:S(2)}, u32[]{:S(2)}) collective-permute-start(bf16[64,4096]{1,0:T(8,128)(2,1)} %get-tuple-element.22), channel_id=1, source_target_pairs={{0,8},{8,0},{1,9},{9,1},{2,10},{10,2},{3,11},{11,3},{4,12},{12,4},... | collective-permute-start | bytes 1572872 | tf_op jit(solution)/shard_map/ppermute | solution.py:315
  59.1 25.8 %all-to-all-start.3 = ((bf16[8,128,512]{2,1,0:T(8,128)(2,1)}), bf16[8,128,512]{2,1,0:T(8,128)(2,1)S(1)}, u32[]{:S(2)}, u32[]{:S(2)}) async-start(bf16[8,128,512]{2,1,0:T(8,128)(2,1)} %get-tuple-element.25), calls=%async_computation.3 | async-start | bytes 2097152 | tf_op jit(solution)/shard_map/all_to_all | solution.py:285
  63.9 6.6 %copy-start = (f32[64,4096]{1,0:T(8,128)S(1)}, f32[64,4096]{1,0:T(8,128)}, u32[]{:S(2)}) copy-start(f32[64,4096]{1,0:T(8,128)} %get-tuple-element.21) | copy-start | bytes 3145732
  68.6 7.2 %collective-permute-start.2 = (bf16[64,1024]{1,0:T(8,128)(2,1)}, bf16[64,1024]{1,0:T(8,128)(2,1)S(1)}, u32[]{:S(2)}, u32[]{:S(2)}) collective-permute-start(bf16[64,1024]{1,0:T(8,128)(2,1)} %get-tuple-element.24), channel_id=1, source_target_pairs={{0,8},{8,0},{1,9},{9,1},{2,10},{10,2},{3,11},{11,3},{4,12},{12,4},... | collective-permute-start | bytes 393224 | tf_op jit(solution)/shard_map/ppermute | solution.py:315
  70.7 12.2 %collective-permute-start.1 = (bf16[32,4096]{1,0:T(8,128)(2,1)S(1)}, bf16[32,4096]{1,0:T(8,128)(2,1)S(1)}, u32[]{:S(2)}, u32[]{:S(2)}) collective-permute-start(bf16[32,4096]{1,0:T(8,128)(2,1)S(1)} %slice.24), channel_id=1, source_target_pairs={{0,32},{32,0},{1,33},{33,1},{2,34},{34,2},{3,35},{35,3},{4,36},{36... | collective-permute-start | bytes 786440 | tf_op jit(solution)/shard_map/ppermute | solution.py:315
  76.8 7.3 %collective-permute-start.3 = (bf16[32,1024]{1,0:T(8,128)(2,1)S(1)}, bf16[32,1024]{1,0:T(8,128)(2,1)S(1)}, u32[]{:S(2)}, u32[]{:S(2)}) collective-permute-start(bf16[32,1024]{1,0:T(8,128)(2,1)S(1)} %slice.25), channel_id=1, source_target_pairs={{0,32},{32,0},{1,33},{33,1},{2,34},{34,2},{3,35},{35,3},{4,36},{36... | collective-permute-start | bytes 196616 | tf_op jit(solution)/shard_map/ppermute | solution.py:315
  84.9 41.2 %all-to-all-start.4 = ((bf16[16,2,5120]{2,1,0:T(2,128)(2,1)}), bf16[16,2,5120]{2,1,0:T(2,128)(2,1)S(1)}, u32[]{:S(2)}, u32[]{:S(2)}) async-start(bf16[16,2,5120]{2,1,0:T(2,128)(2,1)} %shard_map.98), calls=%async_computation.4 | async-start | bytes 655360 | tf_op jit(solution)/shard_map/all_to_all | solution.py:355

commit v5 on v4

--- a/solution.py
+++ b/solution.py
@@ -15,8 +15,9 @@
 ROWS = 512
 PIECE = 16
 PAIR = 2
-STEPS = (0, 2)
-SHARED = (5, 4, 3, 1)
+UP_STEPS = (2, 0, 3)
+DOWN_STEPS = (0, 2, 3)
+SHARED = (5, 4, 1)
 DP = ("z8", "z4", "z2", "z1", "far", "core")
 MIB = 1 << 20
 BF16 = jnp.bfloat16
@@ -39,13 +40,13 @@
     return jnp.where(come == wanted, 1.0, 0.0).astype(BF16)
 
 
-def shard_matrix(place):
+def shard_matrix(steps, place):
     to = lax.broadcasted_iota(jnp.int32, (BIN, BIN), 0)
     come = lax.broadcasted_iota(jnp.int32, (BIN, BIN), 1)
     owner = jnp.zeros_like(to)
-    for at, bit in enumerate(STEPS + SHARED):
-        here = (to >> (len(STEPS + SHARED) - at)) & 1
-        if bit in STEPS:
+    for at, bit in enumerate(steps + SHARED):
+        here = (to >> (len(steps + SHARED) - at)) & 1
+        if bit in steps:
             here = (1 - here) ^ ((place >> bit) & 1)
         owner = owner | (here << bit)
     return jnp.where(come == ((owner << 1) | (to & 1)), 1.0, 0.0).astype(BF16)
@@ -96,7 +97,7 @@
     @pl.when(j == 0)
     def _():
         gather_rows(msg_ref, held_ref)
-        shard_ref[...] = shard_matrix(place_ref[0])
+        shard_ref[...] = shard_matrix(UP_STEPS, place_ref[0])
 
     v = held_ref[j]
     saved_ref[0] = dot(shard_ref[...], v, NN).astype(BF16)
@@ -135,7 +136,7 @@
     wide = PAIR * BIN
     cot_copy = fetch(cot_hbm, cot_ref, in_sem)
     left_copy = fetch(left_hbm, left_ref, left_sem)
-    shard = shard_matrix(place_ref[0])
+    shard = shard_matrix(DOWN_STEPS, place_ref[0])
     gather_rows(msg_ref, held_ref)
     left_copy.wait()
     cot_copy.wait()
@@ -260,7 +261,7 @@
     half = (BIN // 2, OWNED * BIN)
     return pl.pallas_call(
         out_kernel,
-        out_shape=[far((ROWS, OWNED * BIN), BF16), far(half, BF16), far(half, F32)],
+        out_shape=[far((ROWS, OWNED * BIN), BF16), shape(half, BF16), shape(half, F32)],
         in_specs=[SMEM, VMEM, ANY, ANY],
         out_specs=[ANY, VMEM, VMEM],
         scratch_shapes=[HELD, SQUARES, FLAT, FLAT, ONE, ONE, SEMS],
@@ -311,12 +312,12 @@
     return DP[len(DP) - 1 - bit]
 
 
-def swap_halves(send, step):
-    return lax.ppermute(send, axis_of(STEPS[step]), [(0, 1), (1, 0)])
-
-
-def halve(send, keep, step):
-    total = keep + swap_halves(send, step).astype(F32)
+def swap_halves(send, bit):
+    return lax.ppermute(send, axis_of(bit), [(0, 1), (1, 0)])
+
+
+def halve(send, keep, bit):
+    total = keep + swap_halves(send, bit).astype(F32)
     rows = total.shape[0] // 2
     return total[:rows].astype(BF16), total[rows:]
 
@@ -346,12 +347,15 @@
 
 
 def sum_over_dp(up_half, down_half, grad_u, factor):
-    for step in range(len(STEPS) - 1):
-        up_half = halve(*up_half, step)
-        down_half = halve(*down_half, step)
-    last = len(STEPS) - 1
-    total = join(up_half[1], swap_halves(up_half[0], last), down_half[1], swap_halves(down_half[0], last))
-    total, grad_u = lax.optimization_barrier((total, grad_u))
+    for bit in UP_STEPS[:-1]:
+        up_half = halve(*up_half, bit)
+    for bit in DOWN_STEPS[:-1]:
+        down_half = halve(*down_half, bit)
+    up_send, up_keep = up_half
+    down_send, down_keep = down_half
+    down_send, grad_u = lax.optimization_barrier((down_send, grad_u))
+    up_far, down_far = swap_halves(up_send, UP_STEPS[-1]), swap_halves(down_send, DOWN_STEPS[-1])
+    total = join(up_keep, up_far, down_keep, down_far)
     total = lax.all_to_all(total, tuple(axis_of(bit) for bit in SHARED), 0, 0, tiled=True)
     return (*finish(total, factor), grad_u)
 

time: 128 us -> 137 us (1.070)
  the two profiles are of different devices: /device:TPU:8 before, /device:TPU:32 now
where the time goes in v5:
time: 137 us; the launch traced here: 136 us
  starting transfers between devices  52.5 us (38%)
  waiting for transfers between devices  48.2 us (35%)
  Pallas kernels  34.2 us (25%)
    all_to_all x4, waiting for transfers between devices, exchange(): return lax.all_to_all(msg, 'blk', split_axis=0, concat_axis=0, tiled=True)  27.1 us
    ppermute x6, starting transfers between devices, swap_halves(): return lax.ppermute(send, axis_of(bit), [(0, 1), (1, 0)])  18.4 us
    all_to_all x4, starting transfers between devices, exchange(): return lax.all_to_all(msg, 'blk', split_axis=0, concat_axis=0, tiled=True)  18.1 us
    all_to_all x1, starting transfers between devices, sum_over_dp(): lax.all_to_all(total, tuple((axis_of(bit) for bit in SHARED)), 0, 0, tile...  16 us
    all_to_all x1, waiting for transfers between devices, sum_over_dp(): lax.all_to_all(total, tuple((axis_of(bit) for bit in SHARED)), 0, 0, tile...  14.7 us
    pallas_call x1, Pallas kernels, up(): pl.pallas_call(up_kernel, grid=(OWNED,), out_shape=[far(MSG, BF16), far((...  10.9 us
    pallas_call x1, Pallas kernels, back(): pl.pallas_call(back_kernel, grid=(OWNED,), out_shape=[far(MSG, BF16), far...  9.5 us
    ppermute x6, waiting for transfers between devices, swap_halves(): return lax.ppermute(send, axis_of(bit), [(0, 1), (1, 0)])  6.29 us
  transfers between devices with their start and end apart: 11, of which 7 were waited for; matrix products, arithmetic and copies ran while one was open for 0% of the time, Pallas kernels for 22%

profile of v5, /device:TPU:32, one launch (start us, length us, event | category | flops | bytes accessed | tf_op | source)
XLA Modules:
  0.0 136.0 jit_solution(13430769738723465649)
XLA Ops:
  0.6 3.0 %shard_map.93 = bf16[8,128,512]{2,1,0:T(8,128)(2,1)} custom-call(bf16[512,1024]{1,0:T(8,128)(2,1)} %x_hbm.2, bf16[8,128,128]{2,1,0:T(8,128)(2,1)} %right_hbm.1), custom_call_target="tpu_custom_call" | custom-call | flops 134000000 | bytes 3145728 | tf_op jit(solution)/shard_map/pallas_call | solution.py:222
  3.6 5.4 %all-to-all-start = ((bf16[8,128,512]{2,1,0:T(8,128)(2,1)}), bf16[8,128,512]{2,1,0:T(8,128)(2,1)S(1)}, u32[]{:S(2)}, u32[]{:S(2)}) async-start(bf16[8,128,512]{2,1,0:T(8,128)(2,1)} %shard_map.93), calls=%async_computation | async-start | bytes 2097152 | tf_op jit(solution)/shard_map/all_to_all | solution.py:286
  9.0 3.0 %shard_map.96 = bf16[8,128,512]{2,1,0:T(8,128)(2,1)} custom-call(bf16[512,1024]{1,0:T(8,128)(2,1)} %x_hbm.3, bf16[8,128,128]{2,1,0:T(8,128)(2,1)} %w_hbm.3), custom_call_target="tpu_custom_call" | custom-call | flops 134000000 | bytes 3145728 | tf_op jit(solution)/shard_map/pallas_call | solution.py:222
  12.0 11.8 %all-to-all-done.msg_ref = bf16[8,128,512]{2,1,0:T(8,128)(2,1)S(1)} async-done(((bf16[8,128,512]{2,1,0:T(8,128)(2,1)}), bf16[8,128,512]{2,1,0:T(8,128)(2,1)S(1)}, u32[]{:S(2)}, u32[]{:S(2)}) %all-to-all-start) | async-done | bytes 1048608 | tf_op jit(solution)/shard_map/all_to_all | solution.py:286
  23.8 3.6 %all-to-all-start.2 = ((bf16[8,128,512]{2,1,0:T(8,128)(2,1)}), bf16[8,128,512]{2,1,0:T(8,128)(2,1)S(1)}, u32[]{:S(2)}, u32[]{:S(2)}) async-start(bf16[8,128,512]{2,1,0:T(8,128)(2,1)} %shard_map.96), calls=%async_computation.2 | async-start | bytes 2097152 | tf_op jit(solution)/shard_map/all_to_all | solution.py:286
  27.5 10.9 %shard_map.94 = (bf16[8,128,512]{2,1,0:T(8,128)(2,1)}, bf16[8,128,512]{2,1,0:T(8,128)(2,1)}, bf16[8,512,512]{2,1,0:T(8,128)(2,1)}) custom-call(s32[1]{0:T(128)} %bitcast.place_ref, bf16[8,128,512]{2,1,0:T(8,128)(2,1)S(1)} %all-to-all-done.msg_ref, bf16[8,128,512]{2,1,0:T(8,128)(2,1)} %left_ref.3, bf16[8,512,128]{2,1,0:T(8,128)(2,1)} %down_ref.3), custom_call_target="tpu_custom_call" | custom-call | flops 1300000000 | bytes 9437184 | tf_op jit(solution)/shard_map/pallas_call | solution.py:234
  38.4 4.0 %all-to-all-done.2.msg_ref = bf16[8,128,512]{2,1,0:T(8,128)(2,1)S(1)} async-done(((bf16[8,128,512]{2,1,0:T(8,128)(2,1)}), bf16[8,128,512]{2,1,0:T(8,128)(2,1)S(1)}, u32[]{:S(2)}, u32[]{:S(2)}) %all-to-all-start.2) | async-done | bytes 1048608 | tf_op jit(solution)/shard_map/all_to_all | solution.py:286
  42.5 3.6 %all-to-all-start.1 = ((bf16[8,128,512]{2,1,0:T(8,128)(2,1)}), bf16[8,128,512]{2,1,0:T(8,128)(2,1)S(1)}, u32[]{:S(2)}, u32[]{:S(2)}) async-start(bf16[8,128,512]{2,1,0:T(8,128)(2,1)} %get-tuple-element.17), calls=%async_computation.1 | async-start | bytes 2097152 | tf_op jit(solution)/shard_map/all_to_all | solution.py:286
  46.1 9.5 %shard_map.97 = (bf16[8,128,512]{2,1,0:T(8,128)(2,1)}, bf16[64,4096]{1,0:T(8,128)(2,1)}, f32[64,4096]{1,0:T(8,128)}) custom-call(bf16[8,128,512]{2,1,0:T(8,128)(2,1)S(1)} %all-to-all-done.2.msg_ref, bf16[8,128,512]{2,1,0:T(8,128)(2,1)} %get-tuple-element.21.saved_ref, bf16[8,512,512]{2,1,0:T(8,128)(2,1)} %get-tuple-element.22.slope_ref, ...), custom_call_target="tpu_custom_call" | custom-call | flops 1800000000 | bytes 11534336 | tf_op jit(solution)/shard_map/pallas_call | solution.py:248
  55.6 2.0 %collective-permute-start.2 = (bf16[64,4096]{1,0:T(8,128)(2,1)}, bf16[64,4096]{1,0:T(8,128)(2,1)S(1)}, u32[]{:S(2)}, u32[]{:S(2)}) collective-permute-start(bf16[64,4096]{1,0:T(8,128)(2,1)} %get-tuple-element.26), channel_id=1, source_target_pairs={{0,32},{32,0},{1,33},{33,1},{2,34},{34,2},{3,35},{35,3},{4,36},{36... | collective-permute-start | bytes 1572872 | tf_op jit(solution)/shard_map/ppermute | solution.py:316
  57.6 3.4 %all-to-all-done.1.msg_ref = bf16[8,128,512]{2,1,0:T(8,128)(2,1)S(1)} async-done(((bf16[8,128,512]{2,1,0:T(8,128)(2,1)}), bf16[8,128,512]{2,1,0:T(8,128)(2,1)S(1)}, u32[]{:S(2)}, u32[]{:S(2)}) %all-to-all-start.1) | async-done | bytes 1048608 | tf_op jit(solution)/shard_map/all_to_all | solution.py:286
  61.1 3.9 %shard_map.95 = (bf16[512,1024]{1,0:T(8,128)(2,1)}, bf16[64,1024]{1,0:T(8,128)(2,1)S(1)}, f32[64,1024]{1,0:T(8,128)S(1)}) custom-call(s32[1]{0:T(128)} %bitcast.place_ref, bf16[8,128,512]{2,1,0:T(8,128)(2,1)S(1)} %all-to-all-done.1.msg_ref, bf16[8,128,128]{2,1,0:T(8,128)(2,1)} %w_hbm.3, bf16[512,1024]{1,0:T(8,128)(2,1)} %x_hbm.3), custom_call_target="tpu_custom_call" | custom-call | flops 3000000000 | bytes 16777216 | tf_op jit(solution)/shard_map/pallas_call | solution.py:262
  65.0 1.9 %collective-permute-start = (bf16[64,1024]{1,0:T(8,128)(2,1)S(1)}, bf16[64,1024]{1,0:T(8,128)(2,1)S(1)}, u32[]{:S(2)}, u32[]{:S(2)}) collective-permute-start(bf16[64,1024]{1,0:T(8,128)(2,1)S(1)} %get-tuple-element.20), channel_id=1, source_target_pairs={{0,8},{8,0},{1,9},{9,1},{2,10},{10,2},{3,11},{11,3},{4,12},{12,4},... | collective-permute-start | bytes 393224 | tf_op jit(solution)/shard_map/ppermute | solution.py:316
  66.9 4.5 %collective-permute-done.2 = bf16[64,4096]{1,0:T(8,128)(2,1)S(1)} collective-permute-done((bf16[64,4096]{1,0:T(8,128)(2,1)}, bf16[64,4096]{1,0:T(8,128)(2,1)S(1)}, u32[]{:S(2)}, u32[]{:S(2)}) %collective-permute-start.2) | collective-permute-done | bytes 524320 | tf_op jit(solution)/shard_map/ppermute | solution.py:316
  71.4 0.0 copy-done
  71.4 0.1 convert_add_fusion
  71.5 1.9 %collective-permute-start.3 = (bf16[32,4096]{1,0:T(8,128)(2,1)S(1)}, bf16[32,4096]{1,0:T(8,128)(2,1)S(1)}, u32[]{:S(2)}, u32[]{:S(2)}) collective-permute-start(bf16[32,4096]{1,0:T(8,128)(2,1)S(1)} %slice.50), channel_id=1, source_target_pairs={{0,8},{8,0},{1,9},{9,1},{2,10},{10,2},{3,11},{11,3},{4,12},{12,4},... | collective-permute-start | bytes 786440 | tf_op jit(solution)/shard_map/ppermute | solution.py:316
  73.5 5.4 %all-to-all-start.3 = ((bf16[8,128,512]{2,1,0:T(8,128)(2,1)}), bf16[8,128,512]{2,1,0:T(8,128)(2,1)S(1)}, u32[]{:S(2)}, u32[]{:S(2)}) async-start(bf16[8,128,512]{2,1,0:T(8,128)(2,1)} %get-tuple-element.23), calls=%async_computation.3 | async-start | bytes 2097152 | tf_op jit(solution)/shard_map/all_to_all | solution.py:286
  78.9 0.0 collective-permute-done
  79.0 2.2 %collective-permute-start.1 = (bf16[32,1024]{1,0:T(8,128)(2,1)S(1)}, bf16[32,1024]{1,0:T(8,128)(2,1)S(1)}, u32[]{:S(2)}, u32[]{:S(2)}) collective-permute-start(bf16[32,1024]{1,0:T(8,128)(2,1)S(1)} %slice.52), channel_id=1, source_target_pairs={{0,32},{32,0},{1,33},{33,1},{2,34},{34,2},{3,35},{35,3},{4,36},{36... | collective-permute-start | bytes 196616 | tf_op jit(solution)/shard_map/ppermute | solution.py:316
  81.2 0.0 collective-permute-done.3
  81.3 5.2 %collective-permute-start.4 = (bf16[16,4096]{1,0:T(8,128)(2,1)S(1)}, bf16[16,4096]{1,0:T(8,128)(2,1)S(1)}, u32[]{:S(2)}, u32[]{:S(2)}) collective-permute-start(bf16[16,4096]{1,0:T(8,128)(2,1)S(1)} %slice.51), channel_id=1, source_target_pairs={{0,64},{64,0},{1,65},{65,1},{2,66},{66,2},{3,67},{67,3},{4,68},{68... | collective-permute-start | bytes 393224 | tf_op jit(solution)/shard_map/ppermute | solution.py:316
  86.4 0.0 collective-permute-done.1
  86.5 7.9 %all-to-all-done.3.msg_ref = bf16[8,128,512]{2,1,0:T(8,128)(2,1)S(1)} async-done(((bf16[8,128,512]{2,1,0:T(8,128)(2,1)}), bf16[8,128,512]{2,1,0:T(8,128)(2,1)S(1)}, u32[]{:S(2)}, u32[]{:S(2)}) %all-to-all-start.3) | async-done | bytes 1048608 | tf_op jit(solution)/shard_map/all_to_all | solution.py:286
  94.4 5.2 %collective-permute-start.5 = (bf16[16,1024]{1,0:T(8,128)(2,1)S(1)}, bf16[16,1024]{1,0:T(8,128)(2,1)S(1)}, u32[]{:S(2)}, u32[]{:S(2)}) collective-permute-start(bf16[16,1024]{1,0:T(8,128)(2,1)S(1)} %slice.53), channel_id=1, source_target_pairs={{0,64},{64,0},{1,65},{65,1},{2,66},{66,2},{3,67},{67,3},{4,68},{68... | collective-permute-start | bytes 98312 | tf_op jit(solution)/shard_map/ppermute | solution.py:316
  99.6 0.0 collective-permute-done.4.up_far_ref
  99.6 1.8 %collective-permute-done.5.down_far_ref = bf16[16,1024]{1,0:T(8,128)(2,1)S(1)} collective-permute-done((bf16[16,1024]{1,0:T(8,128)(2,1)S(1)}, bf16[16,1024]{1,0:T(8,128)(2,1)S(1)}, u32[]{:S(2)}, u32[]{:S(2)}) %collective-permute-start.5) | collective-permute-done | bytes 32800 | tf_op jit(solution)/shard_map/ppermute | solution.py:316
  101.4 0.7 shard_map.99
  102.1 16.0 %all-to-all-start.4 = ((bf16[8,2,5120]{2,1,0:T(2,128)(2,1)}), bf16[8,2,5120]{2,1,0:T(2,128)(2,1)S(1)}, u32[]{:S(2)}, u32[]{:S(2)}) async-start(bf16[8,2,5120]{2,1,0:T(2,128)(2,1)} %shard_map.99), calls=%async_computation.4 | async-start | bytes 327680 | tf_op jit(solution)/shard_map/all_to_all | solution.py:359
  118.1 2.5 %shard_map.98 = bf16[512,1024]{1,0:T(8,128)(2,1)} custom-call(bf16[8,128,512]{2,1,0:T(8,128)(2,1)S(1)} %all-to-all-done.3.msg_ref, bf16[8,128,128]{2,1,0:T(8,128)(2,1)} %right_hbm.1), custom_call_target="tpu_custom_call" | custom-call | flops 300000000 | bytes 3145728 | tf_op jit(solution)/shard_map/pallas_call | solution.py:274
  120.6 14.7 %all-to-all-done.4.in_ref = bf16[8,2,5120]{2,1,0:T(2,128)(2,1)S(1)} async-done(((bf16[8,2,5120]{2,1,0:T(2,128)(2,1)}), bf16[8,2,5120]{2,1,0:T(2,128)(2,1)S(1)}, u32[]{:S(2)}, u32[]{:S(2)}) %all-to-all-start.4) | async-done | bytes 163872 | tf_op jit(solution)/shard_map/all_to_all | solution.py:359
  135.4 0.6 shard_map.100
  (10 shorter events, 0.2 us)
Async XLA Ops:
  3.6 20.2 %all-to-all-start = ((bf16[8,128,512]{2,1,0:T(8,128)(2,1)}), bf16[8,128,512]{2,1,0:T(8,128)(2,1)S(1)}, u32[]{:S(2)}, u32[]{:S(2)}) async-start(bf16[8,128,512]{2,1,0:T(8,128)(2,1)} %shard_map.93), calls=%async_computation | async-start | bytes 2097152 | tf_op jit(solution)/shard_map/all_to_all | solution.py:286
  23.8 18.6 %all-to-all-start.2 = ((bf16[8,128,512]{2,1,0:T(8,128)(2,1)}), bf16[8,128,512]{2,1,0:T(8,128)(2,1)S(1)}, u32[]{:S(2)}, u32[]{:S(2)}) async-start(bf16[8,128,512]{2,1,0:T(8,128)(2,1)} %shard_map.96), calls=%async_computation.2 | async-start | bytes 2097152 | tf_op jit(solution)/shard_map/all_to_all | solution.py:286
  42.5 18.6 %all-to-all-start.1 = ((bf16[8,128,512]{2,1,0:T(8,128)(2,1)}), bf16[8,128,512]{2,1,0:T(8,128)(2,1)S(1)}, u32[]{:S(2)}, u32[]{:S(2)}) async-start(bf16[8,128,512]{2,1,0:T(8,128)(2,1)} %get-tuple-element.17), calls=%async_computation.1 | async-start | bytes 2097152 | tf_op jit(solution)/shard_map/all_to_all | solution.py:286
  55.6 15.8 %copy-start = (f32[64,4096]{1,0:T(8,128)S(1)}, f32[64,4096]{1,0:T(8,128)}, u32[]{:S(2)}) copy-start(f32[64,4096]{1,0:T(8,128)} %get-tuple-element.25) | copy-start | bytes 3145732
  55.6 15.8 %collective-permute-start.2 = (bf16[64,4096]{1,0:T(8,128)(2,1)}, bf16[64,4096]{1,0:T(8,128)(2,1)S(1)}, u32[]{:S(2)}, u32[]{:S(2)}) collective-permute-start(bf16[64,4096]{1,0:T(8,128)(2,1)} %get-tuple-element.26), channel_id=1, source_target_pairs={{0,32},{32,0},{1,33},{33,1},{2,34},{34,2},{3,35},{35,3},{4,36},{36... | collective-permute-start | bytes 1572872 | tf_op jit(solution)/shard_map/ppermute | solution.py:316
  65.0 13.9 %collective-permute-start = (bf16[64,1024]{1,0:T(8,128)(2,1)S(1)}, bf16[64,1024]{1,0:T(8,128)(2,1)S(1)}, u32[]{:S(2)}, u32[]{:S(2)}) collective-permute-start(bf16[64,1024]{1,0:T(8,128)(2,1)S(1)} %get-tuple-element.20), channel_id=1, source_target_pairs={{0,8},{8,0},{1,9},{9,1},{2,10},{10,2},{3,11},{11,3},{4,12},{12,4},... | collective-permute-start | bytes 393224 | tf_op jit(solution)/shard_map/ppermute | solution.py:316
  71.5 9.6 %collective-permute-start.3 = (bf16[32,4096]{1,0:T(8,128)(2,1)S(1)}, bf16[32,4096]{1,0:T(8,128)(2,1)S(1)}, u32[]{:S(2)}, u32[]{:S(2)}) collective-permute-start(bf16[32,4096]{1,0:T(8,128)(2,1)S(1)} %slice.50), channel_id=1, source_target_pairs={{0,8},{8,0},{1,9},{9,1},{2,10},{10,2},{3,11},{11,3},{4,12},{12,4},... | collective-permute-start | bytes 786440 | tf_op jit(solution)/shard_map/ppermute | solution.py:316
  73.5 20.9 %all-to-all-start.3 = ((bf16[8,128,512]{2,1,0:T(8,128)(2,1)}), bf16[8,128,512]{2,1,0:T(8,128)(2,1)S(1)}, u32[]{:S(2)}, u32[]{:S(2)}) async-start(bf16[8,128,512]{2,1,0:T(8,128)(2,1)} %get-tuple-element.23), calls=%async_computation.3 | async-start | bytes 2097152 | tf_op jit(solution)/shard_map/all_to_all | solution.py:286
  79.0 7.5 %collective-permute-start.1 = (bf16[32,1024]{1,0:T(8,128)(2,1)S(1)}, bf16[32,1024]{1,0:T(8,128)(2,1)S(1)}, u32[]{:S(2)}, u32[]{:S(2)}) collective-permute-start(bf16[32,1024]{1,0:T(8,128)(2,1)S(1)} %slice.52), channel_id=1, source_target_pairs={{0,32},{32,0},{1,33},{33,1},{2,34},{34,2},{3,35},{35,3},{4,36},{36... | collective-permute-start | bytes 196616 | tf_op jit(solution)/shard_map/ppermute | solution.py:316
  81.3 18.3 %collective-permute-start.4 = (bf16[16,4096]{1,0:T(8,128)(2,1)S(1)}, bf16[16,4096]{1,0:T(8,128)(2,1)S(1)}, u32[]{:S(2)}, u32[]{:S(2)}) collective-permute-start(bf16[16,4096]{1,0:T(8,128)(2,1)S(1)} %slice.51), channel_id=1, source_target_pairs={{0,64},{64,0},{1,65},{65,1},{2,66},{66,2},{3,67},{67,3},{4,68},{68... | collective-permute-start | bytes 393224 | tf_op jit(solution)/shard_map/ppermute | solution.py:316
  94.4 7.1 %collective-permute-start.5 = (bf16[16,1024]{1,0:T(8,128)(2,1)S(1)}, bf16[16,1024]{1,0:T(8,128)(2,1)S(1)}, u32[]{:S(2)}, u32[]{:S(2)}) collective-permute-start(bf16[16,1024]{1,0:T(8,128)(2,1)S(1)} %slice.53), channel_id=1, source_target_pairs={{0,64},{64,0},{1,65},{65,1},{2,66},{66,2},{3,67},{67,3},{4,68},{68... | collective-permute-start | bytes 98312 | tf_op jit(solution)/shard_map/ppermute | solution.py:316
  102.1 33.2 %all-to-all-start.4 = ((bf16[8,2,5120]{2,1,0:T(2,128)(2,1)}), bf16[8,2,5120]{2,1,0:T(2,128)(2,1)S(1)}, u32[]{:S(2)}, u32[]{:S(2)}) async-start(bf16[8,2,5120]{2,1,0:T(2,128)(2,1)} %shard_map.99), calls=%async_computation.4 | async-start | bytes 327680 | tf_op jit(solution)/shard_map/all_to_all | solution.py:359

commit v6 on v5

--- a/solution.py
+++ b/solution.py
@@ -15,9 +15,9 @@
 ROWS = 512
 PIECE = 16
 PAIR = 2
-UP_STEPS = (2, 0, 3)
-DOWN_STEPS = (0, 2, 3)
-SHARED = (5, 4, 1)
+UP_STEPS = (2, 0)
+DOWN_STEPS = (0, 2)
+SHARED = (5, 4, 3, 1)
 DP = ("z8", "z4", "z2", "z1", "far", "core")
 MIB = 1 << 20
 BF16 = jnp.bfloat16
@@ -353,9 +353,9 @@
         down_half = halve(*down_half, bit)
     up_send, up_keep = up_half
     down_send, down_keep = down_half
-    down_send, grad_u = lax.optimization_barrier((down_send, grad_u))
     up_far, down_far = swap_halves(up_send, UP_STEPS[-1]), swap_halves(down_send, DOWN_STEPS[-1])
     total = join(up_keep, up_far, down_keep, down_far)
+    total, grad_u = lax.optimization_barrier((total, grad_u))
     total = lax.all_to_all(total, tuple(axis_of(bit) for bit in SHARED), 0, 0, tiled=True)
     return (*finish(total, factor), grad_u)
 

time: 137 us -> 124 us (0.905)
  the two profiles are of different devices: /device:TPU:32 before, /device:TPU:8 now
where the time goes in v6:
time: 124 us; the launch traced here: 123 us
  starting transfers between devices  54.3 us (44%)
  Pallas kernels  34.3 us (28%)
  waiting for transfers between devices  33.1 us (27%)
    all_to_all x4, starting transfers between devices, exchange(): return lax.all_to_all(msg, 'blk', split_axis=0, concat_axis=0, tiled=True)  24.6 us
    all_to_all x1, waiting for transfers between devices, sum_over_dp(): lax.all_to_all(total, tuple((axis_of(bit) for bit in SHARED)), 0, 0, tile...  21.4 us
    all_to_all x1, starting transfers between devices, sum_over_dp(): lax.all_to_all(total, tuple((axis_of(bit) for bit in SHARED)), 0, 0, tile...  17 us
    ppermute x4, starting transfers between devices, swap_halves(): return lax.ppermute(send, axis_of(bit), [(0, 1), (1, 0)])  12.7 us
    pallas_call x1, Pallas kernels, up(): pl.pallas_call(up_kernel, grid=(OWNED,), out_shape=[far(MSG, BF16), far((...  10.9 us
    pallas_call x1, Pallas kernels, back(): pl.pallas_call(back_kernel, grid=(OWNED,), out_shape=[far(MSG, BF16), far...  9.5 us
    all_to_all x4, waiting for transfers between devices, exchange(): return lax.all_to_all(msg, 'blk', split_axis=0, concat_axis=0, tiled=True)  8.91 us
    pallas_call x2, Pallas kernels, right(): pl.pallas_call(functools.partial(right_kernel, dims), out_shape=far(MSG,...  5.9 us
  transfers between devices with their start and end apart: 9, of which 5 were waited for; matrix products, arithmetic and copies ran while one was open for 0% of the time, Pallas kernels for 25%

profile of v6, /device:TPU:8, one launch (start us, length us, event | category | flops | bytes accessed | tf_op | source)
XLA Modules:
  0.0 122.7 jit_solution(18136929583321171532)
XLA Ops:
  0.6 3.0 %shard_map.93 = bf16[8,128,512]{2,1,0:T(8,128)(2,1)} custom-call(bf16[512,1024]{1,0:T(8,128)(2,1)} %x_hbm.2, bf16[8,128,128]{2,1,0:T(8,128)(2,1)} %right_hbm.1), custom_call_target="tpu_custom_call" | custom-call | flops 134000000 | bytes 3145728 | tf_op jit(solution)/shard_map/pallas_call | solution.py:222
  3.6 9.3 %all-to-all-start = ((bf16[8,128,512]{2,1,0:T(8,128)(2,1)}), bf16[8,128,512]{2,1,0:T(8,128)(2,1)S(1)}, u32[]{:S(2)}, u32[]{:S(2)}) async-start(bf16[8,128,512]{2,1,0:T(8,128)(2,1)} %shard_map.93), calls=%async_computation | async-start | bytes 2097152 | tf_op jit(solution)/shard_map/all_to_all | solution.py:286
  12.9 2.9 %shard_map.96 = bf16[8,128,512]{2,1,0:T(8,128)(2,1)} custom-call(bf16[512,1024]{1,0:T(8,128)(2,1)} %x_hbm.3, bf16[8,128,128]{2,1,0:T(8,128)(2,1)} %w_hbm.3), custom_call_target="tpu_custom_call" | custom-call | flops 134000000 | bytes 3145728 | tf_op jit(solution)/shard_map/pallas_call | solution.py:222
  15.8 7.3 %all-to-all-done.msg_ref = bf16[8,128,512]{2,1,0:T(8,128)(2,1)S(1)} async-done(((bf16[8,128,512]{2,1,0:T(8,128)(2,1)}), bf16[8,128,512]{2,1,0:T(8,128)(2,1)S(1)}, u32[]{:S(2)}, u32[]{:S(2)}) %all-to-all-start) | async-done | bytes 1048608 | tf_op jit(solution)/shard_map/all_to_all | solution.py:286
  23.1 4.8 %all-to-all-start.2 = ((bf16[8,128,512]{2,1,0:T(8,128)(2,1)}), bf16[8,128,512]{2,1,0:T(8,128)(2,1)S(1)}, u32[]{:S(2)}, u32[]{:S(2)}) async-start(bf16[8,128,512]{2,1,0:T(8,128)(2,1)} %shard_map.96), calls=%async_computation.2 | async-start | bytes 2097152 | tf_op jit(solution)/shard_map/all_to_all | solution.py:286
  27.9 10.9 %shard_map.94 = (bf16[8,128,512]{2,1,0:T(8,128)(2,1)}, bf16[8,128,512]{2,1,0:T(8,128)(2,1)}, bf16[8,512,512]{2,1,0:T(8,128)(2,1)}) custom-call(s32[1]{0:T(128)} %bitcast.place_ref, bf16[8,128,512]{2,1,0:T(8,128)(2,1)S(1)} %all-to-all-done.msg_ref, bf16[8,128,512]{2,1,0:T(8,128)(2,1)} %left_ref.3, bf16[8,512,128]{2,1,0:T(8,128)(2,1)} %down_ref.3), custom_call_target="tpu_custom_call" | custom-call | flops 1300000000 | bytes 9437184 | tf_op jit(solution)/shard_map/pallas_call | solution.py:234
  38.9 1.6 %all-to-all-done.2.msg_ref = bf16[8,128,512]{2,1,0:T(8,128)(2,1)S(1)} async-done(((bf16[8,128,512]{2,1,0:T(8,128)(2,1)}), bf16[8,128,512]{2,1,0:T(8,128)(2,1)S(1)}, u32[]{:S(2)}, u32[]{:S(2)}) %all-to-all-start.2) | async-done | bytes 1048608 | tf_op jit(solution)/shard_map/all_to_all | solution.py:286
  40.5 4.8 %all-to-all-start.1 = ((bf16[8,128,512]{2,1,0:T(8,128)(2,1)}), bf16[8,128,512]{2,1,0:T(8,128)(2,1)S(1)}, u32[]{:S(2)}, u32[]{:S(2)}) async-start(bf16[8,128,512]{2,1,0:T(8,128)(2,1)} %get-tuple-element.17), calls=%async_computation.1 | async-start | bytes 2097152 | tf_op jit(solution)/shard_map/all_to_all | solution.py:286
  45.3 9.5 %shard_map.97 = (bf16[8,128,512]{2,1,0:T(8,128)(2,1)}, bf16[64,4096]{1,0:T(8,128)(2,1)}, f32[64,4096]{1,0:T(8,128)}) custom-call(bf16[8,128,512]{2,1,0:T(8,128)(2,1)S(1)} %all-to-all-done.2.msg_ref, bf16[8,128,512]{2,1,0:T(8,128)(2,1)} %get-tuple-element.19.saved_ref, bf16[8,512,512]{2,1,0:T(8,128)(2,1)} %get-tuple-element.20.slope_ref, ...), custom_call_target="tpu_custom_call" | custom-call | flops 1800000000 | bytes 11534336 | tf_op jit(solution)/shard_map/pallas_call | solution.py:248
  54.8 5.0 %collective-permute-start = (bf16[64,4096]{1,0:T(8,128)(2,1)}, bf16[64,4096]{1,0:T(8,128)(2,1)S(1)}, u32[]{:S(2)}, u32[]{:S(2)}) collective-permute-start(bf16[64,4096]{1,0:T(8,128)(2,1)} %get-tuple-element.22), channel_id=1, source_target_pairs={{0,32},{32,0},{1,33},{33,1},{2,34},{34,2},{3,35},{35,3},{4,36},{36... | collective-permute-start | bytes 1572872 | tf_op jit(solution)/shard_map/ppermute | solution.py:316
  59.8 0.0 all-to-all-done.1.msg_ref
  59.8 5.7 %all-to-all-start.3 = ((bf16[8,128,512]{2,1,0:T(8,128)(2,1)}), bf16[8,128,512]{2,1,0:T(8,128)(2,1)S(1)}, u32[]{:S(2)}, u32[]{:S(2)}) async-start(bf16[8,128,512]{2,1,0:T(8,128)(2,1)} %get-tuple-element.25), calls=%async_computation.3 | async-start | bytes 2097152 | tf_op jit(solution)/shard_map/all_to_all | solution.py:286
  65.6 0.0 copy-start
  65.6 3.9 %shard_map.95 = (bf16[512,1024]{1,0:T(8,128)(2,1)}, bf16[64,1024]{1,0:T(8,128)(2,1)S(1)}, f32[64,1024]{1,0:T(8,128)S(1)}) custom-call(s32[1]{0:T(128)} %bitcast.place_ref, bf16[8,128,512]{2,1,0:T(8,128)(2,1)S(1)} %all-to-all-done.1.msg_ref, bf16[8,128,128]{2,1,0:T(8,128)(2,1)} %w_hbm.3, bf16[512,1024]{1,0:T(8,128)(2,1)} %x_hbm.3), custom_call_target="tpu_custom_call" | custom-call | flops 3000000000 | bytes 16777216 | tf_op jit(solution)/shard_map/pallas_call | solution.py:262
  69.5 1.9 %collective-permute-start.2 = (bf16[64,1024]{1,0:T(8,128)(2,1)S(1)}, bf16[64,1024]{1,0:T(8,128)(2,1)S(1)}, u32[]{:S(2)}, u32[]{:S(2)}) collective-permute-start(bf16[64,1024]{1,0:T(8,128)(2,1)S(1)} %get-tuple-element.24), channel_id=1, source_target_pairs={{0,8},{8,0},{1,9},{9,1},{2,10},{10,2},{3,11},{11,3},{4,12},{12,4},... | collective-permute-start | bytes 393224 | tf_op jit(solution)/shard_map/ppermute | solution.py:316
  71.5 0.1 collective-permute-done
  71.6 0.0 copy-done
  71.6 0.1 convert_add_fusion
  71.7 2.3 %collective-permute-start.1 = (bf16[32,4096]{1,0:T(8,128)(2,1)S(1)}, bf16[32,4096]{1,0:T(8,128)(2,1)S(1)}, u32[]{:S(2)}, u32[]{:S(2)}) collective-permute-start(bf16[32,4096]{1,0:T(8,128)(2,1)S(1)} %slice.24), channel_id=1, source_target_pairs={{0,8},{8,0},{1,9},{9,1},{2,10},{10,2},{3,11},{11,3},{4,12},{12,4},... | collective-permute-start | bytes 786440 | tf_op jit(solution)/shard_map/ppermute | solution.py:316
  74.0 0.0 collective-permute-done.2
  74.1 3.4 %collective-permute-start.3 = (bf16[32,1024]{1,0:T(8,128)(2,1)S(1)}, bf16[32,1024]{1,0:T(8,128)(2,1)S(1)}, u32[]{:S(2)}, u32[]{:S(2)}) collective-permute-start(bf16[32,1024]{1,0:T(8,128)(2,1)S(1)} %slice.25), channel_id=1, source_target_pairs={{0,32},{32,0},{1,33},{33,1},{2,34},{34,2},{3,35},{35,3},{4,36},{36... | collective-permute-start | bytes 196616 | tf_op jit(solution)/shard_map/ppermute | solution.py:316
  77.6 0.0 collective-permute-done.1.up_far_ref
  77.6 2.7 %collective-permute-done.3.down_far_ref = bf16[32,1024]{1,0:T(8,128)(2,1)S(1)} collective-permute-done((bf16[32,1024]{1,0:T(8,128)(2,1)S(1)}, bf16[32,1024]{1,0:T(8,128)(2,1)S(1)}, u32[]{:S(2)}, u32[]{:S(2)}) %collective-permute-start.3) | collective-permute-done | bytes 65568 | tf_op jit(solution)/shard_map/ppermute | solution.py:316
  80.2 0.8 shard_map.98
  81.1 0.0 all-to-all-done.3.msg_ref
  81.1 17.0 %all-to-all-start.4 = ((bf16[16,2,5120]{2,1,0:T(2,128)(2,1)}), bf16[16,2,5120]{2,1,0:T(2,128)(2,1)S(1)}, u32[]{:S(2)}, u32[]{:S(2)}) async-start(bf16[16,2,5120]{2,1,0:T(2,128)(2,1)} %shard_map.98), calls=%async_computation.4 | async-start | bytes 655360 | tf_op jit(solution)/shard_map/all_to_all | solution.py:359
  98.1 2.5 %shard_map.99 = bf16[512,1024]{1,0:T(8,128)(2,1)} custom-call(bf16[8,128,512]{2,1,0:T(8,128)(2,1)S(1)} %all-to-all-done.3.msg_ref, bf16[8,128,128]{2,1,0:T(8,128)(2,1)} %right_hbm.1), custom_call_target="tpu_custom_call" | custom-call | flops 300000000 | bytes 3145728 | tf_op jit(solution)/shard_map/pallas_call | solution.py:274
  100.6 21.4 %all-to-all-done.4.in_ref = bf16[16,2,5120]{2,1,0:T(2,128)(2,1)S(1)} async-done(((bf16[16,2,5120]{2,1,0:T(2,128)(2,1)}), bf16[16,2,5120]{2,1,0:T(2,128)(2,1)S(1)}, u32[]{:S(2)}, u32[]{:S(2)}) %all-to-all-start.4) | async-done | bytes 327712 | tf_op jit(solution)/shard_map/all_to_all | solution.py:359
  122.0 0.7 shard_map.100
  (5 shorter events, 0.1 us)
Async XLA Ops:
  3.6 19.5 %all-to-all-start = ((bf16[8,128,512]{2,1,0:T(8,128)(2,1)}), bf16[8,128,512]{2,1,0:T(8,128)(2,1)S(1)}, u32[]{:S(2)}, u32[]{:S(2)}) async-start(bf16[8,128,512]{2,1,0:T(8,128)(2,1)} %shard_map.93), calls=%async_computation | async-start | bytes 2097152 | tf_op jit(solution)/shard_map/all_to_all | solution.py:286
  23.1 17.4 %all-to-all-start.2 = ((bf16[8,128,512]{2,1,0:T(8,128)(2,1)}), bf16[8,128,512]{2,1,0:T(8,128)(2,1)S(1)}, u32[]{:S(2)}, u32[]{:S(2)}) async-start(bf16[8,128,512]{2,1,0:T(8,128)(2,1)} %shard_map.96), calls=%async_computation.2 | async-start | bytes 2097152 | tf_op jit(solution)/shard_map/all_to_all | solution.py:286
  40.5 19.3 %all-to-all-start.1 = ((bf16[8,128,512]{2,1,0:T(8,128)(2,1)}), bf16[8,128,512]{2,1,0:T(8,128)(2,1)S(1)}, u32[]{:S(2)}, u32[]{:S(2)}) async-start(bf16[8,128,512]{2,1,0:T(8,128)(2,1)} %get-tuple-element.17), calls=%async_computation.1 | async-start | bytes 2097152 | tf_op jit(solution)/shard_map/all_to_all | solution.py:286
  54.8 16.8 %collective-permute-start = (bf16[64,4096]{1,0:T(8,128)(2,1)}, bf16[64,4096]{1,0:T(8,128)(2,1)S(1)}, u32[]{:S(2)}, u32[]{:S(2)}) collective-permute-start(bf16[64,4096]{1,0:T(8,128)(2,1)} %get-tuple-element.22), channel_id=1, source_target_pairs={{0,32},{32,0},{1,33},{33,1},{2,34},{34,2},{3,35},{35,3},{4,36},{36... | collective-permute-start | bytes 1572872 | tf_op jit(solution)/shard_map/ppermute | solution.py:316
  59.8 21.2 %all-to-all-start.3 = ((bf16[8,128,512]{2,1,0:T(8,128)(2,1)}), bf16[8,128,512]{2,1,0:T(8,128)(2,1)S(1)}, u32[]{:S(2)}, u32[]{:S(2)}) async-start(bf16[8,128,512]{2,1,0:T(8,128)(2,1)} %get-tuple-element.25), calls=%async_computation.3 | async-start | bytes 2097152 | tf_op jit(solution)/shard_map/all_to_all | solution.py:286
  65.6 6.0 %copy-start = (f32[64,4096]{1,0:T(8,128)S(1)}, f32[64,4096]{1,0:T(8,128)}, u32[]{:S(2)}) copy-start(f32[64,4096]{1,0:T(8,128)} %get-tuple-element.21) | copy-start | bytes 3145732
  69.5 4.5 %collective-permute-start.2 = (bf16[64,1024]{1,0:T(8,128)(2,1)S(1)}, bf16[64,1024]{1,0:T(8,128)(2,1)S(1)}, u32[]{:S(2)}, u32[]{:S(2)}) collective-permute-start(bf16[64,1024]{1,0:T(8,128)(2,1)S(1)} %get-tuple-element.24), channel_id=1, source_target_pairs={{0,8},{8,0},{1,9},{9,1},{2,10},{10,2},{3,11},{11,3},{4,12},{12,4},... | collective-permute-start | bytes 393224 | tf_op jit(solution)/shard_map/ppermute | solution.py:316
  71.7 5.8 %collective-permute-start.1 = (bf16[32,4096]{1,0:T(8,128)(2,1)S(1)}, bf16[32,4096]{1,0:T(8,128)(2,1)S(1)}, u32[]{:S(2)}, u32[]{:S(2)}) collective-permute-start(bf16[32,4096]{1,0:T(8,128)(2,1)S(1)} %slice.24), channel_id=1, source_target_pairs={{0,8},{8,0},{1,9},{9,1},{2,10},{10,2},{3,11},{11,3},{4,12},{12,4},... | collective-permute-start | bytes 786440 | tf_op jit(solution)/shard_map/ppermute | solution.py:316
  74.1 6.2 %collective-permute-start.3 = (bf16[32,1024]{1,0:T(8,128)(2,1)S(1)}, bf16[32,1024]{1,0:T(8,128)(2,1)S(1)}, u32[]{:S(2)}, u32[]{:S(2)}) collective-permute-start(bf16[32,1024]{1,0:T(8,128)(2,1)S(1)} %slice.25), channel_id=1, source_target_pairs={{0,32},{32,0},{1,33},{33,1},{2,34},{34,2},{3,35},{35,3},{4,36},{36... | collective-permute-start | bytes 196616 | tf_op jit(solution)/shard_map/ppermute | solution.py:316
  81.1 41.0 %all-to-all-start.4 = ((bf16[16,2,5120]{2,1,0:T(2,128)(2,1)}), bf16[16,2,5120]{2,1,0:T(2,128)(2,1)S(1)}, u32[]{:S(2)}, u32[]{:S(2)}) async-start(bf16[16,2,5120]{2,1,0:T(2,128)(2,1)} %shard_map.98), calls=%async_computation.4 | async-start | bytes 655360 | tf_op jit(solution)/shard_map/all_to_all | solution.py:359

commit v7 on v6

--- a/solution.py
+++ b/solution.py
@@ -129,26 +129,27 @@
     keep_ref[...] = part[BIN // 2 :]
 
 
-def out_kernel(
-    place_ref, msg_ref, left_hbm, cot_hbm, out_hbm, send_ref, keep_ref,
-    held_ref, left_ref, cot_ref, out_ref, left_sem, in_sem, out_sem,
-):
-    wide = PAIR * BIN
+def down_kernel(place_ref, msg_ref, cot_hbm, send_ref, keep_ref, held_ref, cot_ref, in_sem):
     cot_copy = fetch(cot_hbm, cot_ref, in_sem)
-    left_copy = fetch(left_hbm, left_ref, left_sem)
     shard = shard_matrix(DOWN_STEPS, place_ref[0])
     gather_rows(msg_ref, held_ref)
+    cot_copy.wait()
+    for k in range(OWNED):
+        cols = slice(k * BIN, (k + 1) * BIN)
+        part = dot(dot(shard, held_ref[k], NN).astype(BF16), cot_ref[:, cols], NN)
+        send_ref[:, cols] = part[: BIN // 2].astype(BF16)
+        keep_ref[:, cols] = part[BIN // 2 :]
+
+
+def out_kernel(msg_ref, left_hbm, out_hbm, held_ref, left_ref, out_ref, left_sem, out_sem):
+    wide = PAIR * BIN
+    left_copy = fetch(left_hbm, left_ref, left_sem)
+    gather_rows(msg_ref, held_ref)
     left_copy.wait()
-    cot_copy.wait()
     out_copies = []
     for p in range(OWNED // PAIR):
         for k in range(p * PAIR, (p + 1) * PAIR):
-            cols = slice(k * BIN, (k + 1) * BIN)
-            w = held_ref[k]
-            out_ref[:, cols] = dot(w, left_ref[k], TN).astype(BF16)
-            part = dot(dot(shard, w, NN).astype(BF16), cot_ref[:, cols], NN)
-            send_ref[:, cols] = part[: BIN // 2].astype(BF16)
-            keep_ref[:, cols] = part[BIN // 2 :]
+            out_ref[:, k * BIN : (k + 1) * BIN] = dot(held_ref[k], left_ref[k], TN).astype(BF16)
         cols = pl.ds(p * wide, wide)
         out_copies.append(fetch(out_ref.at[:, cols], out_hbm.at[:, cols], out_sem.at[p]))
     for copy in out_copies:
@@ -257,17 +258,29 @@
     )(msg, stay(saved), stay(slope), stay(left), stay(down))
 
 
-def out(place, msg, left, cot):
+def down(place, msg, cot):
     half = (BIN // 2, OWNED * BIN)
     return pl.pallas_call(
-        out_kernel,
-        out_shape=[far((ROWS, OWNED * BIN), BF16), shape(half, BF16), shape(half, F32)],
-        in_specs=[SMEM, VMEM, ANY, ANY],
-        out_specs=[ANY, VMEM, VMEM],
-        scratch_shapes=[HELD, SQUARES, FLAT, FLAT, ONE, ONE, SEMS],
+        down_kernel,
+        out_shape=[shape(half, BF16), shape(half, F32)],
+        in_specs=[SMEM, VMEM, ANY],
+        out_specs=[VMEM, VMEM],
+        scratch_shapes=[HELD, FLAT, ONE],
         compiler_params=params(20),
         cost_estimate=cost(3000, 16),
-    )(place, msg, stay(left), stay(cot))
+    )(place, msg, stay(cot))
+
+
+def out(msg, left):
+    return pl.pallas_call(
+        out_kernel,
+        out_shape=far((ROWS, OWNED * BIN), BF16),
+        in_specs=[VMEM, ANY],
+        out_specs=ANY,
+        scratch_shapes=[HELD, SQUARES, FLAT, ONE, SEMS],
+        compiler_params=params(20),
+        cost_estimate=cost(134, 3),
+    )(msg, stay(left))
 
 
 def into(msg, rightw):
@@ -346,7 +359,7 @@
     )(pieces_in)
 
 
-def sum_over_dp(up_half, down_half, grad_u, factor):
+def sum_over_dp(up_half, down_half, grad_u, layer_out, factor):
     for bit in UP_STEPS[:-1]:
         up_half = halve(*up_half, bit)
     for bit in DOWN_STEPS[:-1]:
@@ -355,9 +368,9 @@
     down_send, down_keep = down_half
     up_far, down_far = swap_halves(up_send, UP_STEPS[-1]), swap_halves(down_send, DOWN_STEPS[-1])
     total = join(up_keep, up_far, down_keep, down_far)
-    total, grad_u = lax.optimization_barrier((total, grad_u))
+    total, grad_u, layer_out = lax.optimization_barrier((total, grad_u, layer_out))
     total = lax.all_to_all(total, tuple(axis_of(bit) for bit in SHARED), 0, 0, tiled=True)
-    return (*finish(total, factor), grad_u)
+    return (*finish(total, factor), grad_u, layer_out)
 
 
 def on_device(tokens, up_right, up_left, down_right, down_left, cotangent):
@@ -369,8 +382,11 @@
     w = exchange(z)
     grad_v, up_send, up_keep = back(grad_z, saved, slope, up_left, down_right)
     grad_u = exchange(grad_v)
-    layer_out, down_send, down_keep = out(place, w, down_left, cotangent)
-    up_grad, down_grad, grad_u = sum_over_dp((up_send, up_keep), (down_send, down_keep), grad_u, factor)
+    down_half = down(place, w, cotangent)
+    layer_out = out(w, down_left)
+    up_grad, down_grad, grad_u, layer_out = sum_over_dp(
+        (up_send, up_keep), down_half, grad_u, layer_out, factor
+    )
     input_grad = into(grad_u, up_right)
     return (layer_out, input_grad, up_grad, down_grad)
 

time: 124 us -> 124 us (level)
  Pallas kernels: 34.3 us -> 35.8 us
  waiting for transfers between devices: 33.1 us -> 31.7 us
    ppermute x4, waiting for transfers between devices: 2.81 us -> 1.22 us  [swap_halves(): return lax.ppermute(send, axis_of(bit), [(0, 1), (1, 0)])]
    pallas_call x1 -> x2, Pallas kernels: 3.94 us -> 5.52 us  [the longest x1 3.04 us: down(): pl.pallas_call(down_kernel, out_shape=[shape(half, BF16), shape(half, F32...]
  transfers between devices with their start and end apart: 9 -> 9, of which waited for: 5 -> 5; matrix products, arithmetic and copies ran while one was open for 0% -> 0% of each run, Pallas kernels for 25% -> 26%
where the time goes in v7:
time: 124 us; the launch traced here: 123 us
  starting transfers between devices  54.3 us (44%)
  Pallas kernels  35.8 us (29%)
  waiting for transfers between devices  31.7 us (26%)
    all_to_all x4, starting transfers between devices, exchange(): return lax.all_to_all(msg, 'blk', split_axis=0, concat_axis=0, tiled=True)  24.6 us
    all_to_all x1, waiting for transfers between devices, sum_over_dp(): lax.all_to_all(total, tuple((axis_of(bit) for bit in SHARED)), 0, 0, tile...  21.5 us
    all_to_all x1, starting transfers between devices, sum_over_dp(): lax.all_to_all(total, tuple((axis_of(bit) for bit in SHARED)), 0, 0, tile...  17.2 us
    ppermute x4, starting transfers between devices, swap_halves(): return lax.ppermute(send, axis_of(bit), [(0, 1), (1, 0)])  12.5 us
    pallas_call x1, Pallas kernels, up(): pl.pallas_call(up_kernel, grid=(OWNED,), out_shape=[far(MSG, BF16), far((...  10.9 us
    pallas_call x1, Pallas kernels, back(): pl.pallas_call(back_kernel, grid=(OWNED,), out_shape=[far(MSG, BF16), far...  9.5 us
    all_to_all x4, waiting for transfers between devices, exchange(): return lax.all_to_all(msg, 'blk', split_axis=0, concat_axis=0, tiled=True)  8.91 us
    pallas_call x2, Pallas kernels, right(): pl.pallas_call(functools.partial(right_kernel, dims), out_shape=far(MSG,...  5.9 us
  transfers between devices with their start and end apart: 9, of which 5 were waited for; matrix products, arithmetic and copies ran while one was open for 0% of the time, Pallas kernels for 26%

profile of v7, /device:TPU:8, one launch (start us, length us, event | category | flops | bytes accessed | tf_op | source)
XLA Modules:
  0.0 122.8 jit_solution(4246153504861117689)
XLA Ops:
  0.6 3.0 %shard_map.94 = bf16[8,128,512]{2,1,0:T(8,128)(2,1)} custom-call(bf16[512,1024]{1,0:T(8,128)(2,1)} %x_hbm.3, bf16[8,128,128]{2,1,0:T(8,128)(2,1)} %right_hbm.1), custom_call_target="tpu_custom_call" | custom-call | flops 134000000 | bytes 3145728 | tf_op jit(solution)/shard_map/pallas_call | solution.py:223
  3.6 9.3 %all-to-all-start.1 = ((bf16[8,128,512]{2,1,0:T(8,128)(2,1)}), bf16[8,128,512]{2,1,0:T(8,128)(2,1)S(1)}, u32[]{:S(2)}, u32[]{:S(2)}) async-start(bf16[8,128,512]{2,1,0:T(8,128)(2,1)} %shard_map.94), calls=%async_computation.1 | async-start | bytes 2097152 | tf_op jit(solution)/shard_map/all_to_all | solution.py:299
  12.9 2.9 %shard_map.93 = bf16[8,128,512]{2,1,0:T(8,128)(2,1)} custom-call(bf16[512,1024]{1,0:T(8,128)(2,1)} %cot_hbm.1, bf16[8,128,128]{2,1,0:T(8,128)(2,1)} %left_hbm.1), custom_call_target="tpu_custom_call" | custom-call | flops 134000000 | bytes 3145728 | tf_op jit(solution)/shard_map/pallas_call | solution.py:223
  15.8 7.3 %all-to-all-done.1.msg_ref = bf16[8,128,512]{2,1,0:T(8,128)(2,1)S(1)} async-done(((bf16[8,128,512]{2,1,0:T(8,128)(2,1)}), bf16[8,128,512]{2,1,0:T(8,128)(2,1)S(1)}, u32[]{:S(2)}, u32[]{:S(2)}) %all-to-all-start.1) | async-done | bytes 1048608 | tf_op jit(solution)/shard_map/all_to_all | solution.py:299
  23.1 4.8 %all-to-all-start = ((bf16[8,128,512]{2,1,0:T(8,128)(2,1)}), bf16[8,128,512]{2,1,0:T(8,128)(2,1)S(1)}, u32[]{:S(2)}, u32[]{:S(2)}) async-start(bf16[8,128,512]{2,1,0:T(8,128)(2,1)} %shard_map.93), calls=%async_computation | async-start | bytes 2097152 | tf_op jit(solution)/shard_map/all_to_all | solution.py:299
  27.9 10.9 %shard_map.95 = (bf16[8,128,512]{2,1,0:T(8,128)(2,1)}, bf16[8,128,512]{2,1,0:T(8,128)(2,1)}, bf16[8,512,512]{2,1,0:T(8,128)(2,1)}) custom-call(s32[1]{0:T(128)} %bitcast.place_ref, bf16[8,128,512]{2,1,0:T(8,128)(2,1)S(1)} %all-to-all-done.1.msg_ref, bf16[8,128,512]{2,1,0:T(8,128)(2,1)} %left_ref.3, bf16[8,512,128]{2,1,0:T(8,128)(2,1)} %down_ref.3), custom_call_target="tpu_custom_call" | custom-call | flops 1300000000 | bytes 9437184 | tf_op jit(solution)/shard_map/pallas_call | solution.py:235
  38.9 1.6 %all-to-all-done.msg_ref = bf16[8,128,512]{2,1,0:T(8,128)(2,1)S(1)} async-done(((bf16[8,128,512]{2,1,0:T(8,128)(2,1)}), bf16[8,128,512]{2,1,0:T(8,128)(2,1)S(1)}, u32[]{:S(2)}, u32[]{:S(2)}) %all-to-all-start) | async-done | bytes 1048608 | tf_op jit(solution)/shard_map/all_to_all | solution.py:299
  40.5 4.8 %all-to-all-start.2 = ((bf16[8,128,512]{2,1,0:T(8,128)(2,1)}), bf16[8,128,512]{2,1,0:T(8,128)(2,1)S(1)}, u32[]{:S(2)}, u32[]{:S(2)}) async-start(bf16[8,128,512]{2,1,0:T(8,128)(2,1)} %get-tuple-element.21), calls=%async_computation.2 | async-start | bytes 2097152 | tf_op jit(solution)/shard_map/all_to_all | solution.py:299
  45.3 9.5 %shard_map.96 = (bf16[8,128,512]{2,1,0:T(8,128)(2,1)}, bf16[64,4096]{1,0:T(8,128)(2,1)}, f32[64,4096]{1,0:T(8,128)}) custom-call(bf16[8,128,512]{2,1,0:T(8,128)(2,1)S(1)} %all-to-all-done.msg_ref, bf16[8,128,512]{2,1,0:T(8,128)(2,1)} %get-tuple-element.17.saved_ref, bf16[8,512,512]{2,1,0:T(8,128)(2,1)} %get-tuple-element.18.slope_ref, ...), custom_call_target="tpu_custom_call" | custom-call | flops 1800000000 | bytes 11534336 | tf_op jit(solution)/shard_map/pallas_call | solution.py:249
  54.8 5.0 %collective-permute-start = (bf16[64,4096]{1,0:T(8,128)(2,1)}, bf16[64,4096]{1,0:T(8,128)(2,1)S(1)}, u32[]{:S(2)}, u32[]{:S(2)}) collective-permute-start(bf16[64,4096]{1,0:T(8,128)(2,1)} %get-tuple-element.20), channel_id=1, source_target_pairs={{0,32},{32,0},{1,33},{33,1},{2,34},{34,2},{3,35},{35,3},{4,36},{36... | collective-permute-start | bytes 1572872 | tf_op jit(solution)/shard_map/ppermute | solution.py:329
  59.8 0.0 all-to-all-done.2.msg_ref
  59.8 5.7 %all-to-all-start.3 = ((bf16[8,128,512]{2,1,0:T(8,128)(2,1)}), bf16[8,128,512]{2,1,0:T(8,128)(2,1)S(1)}, u32[]{:S(2)}, u32[]{:S(2)}) async-start(bf16[8,128,512]{2,1,0:T(8,128)(2,1)} %get-tuple-element.24), calls=%async_computation.3 | async-start | bytes 2097152 | tf_op jit(solution)/shard_map/all_to_all | solution.py:299
  65.6 0.0 copy-start
  65.6 3.0 %shard_map.97 = (bf16[64,1024]{1,0:T(8,128)(2,1)S(1)}, f32[64,1024]{1,0:T(8,128)S(1)}) custom-call(s32[1]{0:T(128)} %bitcast.place_ref, bf16[8,128,512]{2,1,0:T(8,128)(2,1)S(1)} %all-to-all-done.2.msg_ref, bf16[512,1024]{1,0:T(8,128)(2,1)} %cot_hbm.1), custom_call_target="tpu_custom_call" | custom-call | flops 3000000000 | bytes 16777216 | tf_op jit(solution)/shard_map/pallas_call | solution.py:263
  68.6 1.9 %collective-permute-start.2 = (bf16[64,1024]{1,0:T(8,128)(2,1)S(1)}, bf16[64,1024]{1,0:T(8,128)(2,1)S(1)}, u32[]{:S(2)}, u32[]{:S(2)}) collective-permute-start(bf16[64,1024]{1,0:T(8,128)(2,1)S(1)} %get-tuple-element.23), channel_id=1, source_target_pairs={{0,8},{8,0},{1,9},{9,1},{2,10},{10,2},{3,11},{11,3},{4,12},{12,4},... | collective-permute-start | bytes 393224 | tf_op jit(solution)/shard_map/ppermute | solution.py:329
  70.6 1.0 collective-permute-done
  71.6 0.0 copy-done
  71.6 0.1 convert_add_fusion
  71.7 1.9 %collective-permute-start.1 = (bf16[32,4096]{1,0:T(8,128)(2,1)S(1)}, bf16[32,4096]{1,0:T(8,128)(2,1)S(1)}, u32[]{:S(2)}, u32[]{:S(2)}) collective-permute-start(bf16[32,4096]{1,0:T(8,128)(2,1)S(1)} %slice.24), channel_id=1, source_target_pairs={{0,8},{8,0},{1,9},{9,1},{2,10},{10,2},{3,11},{11,3},{4,12},{12,4},... | collective-permute-start | bytes 786440 | tf_op jit(solution)/shard_map/ppermute | solution.py:329
  73.7 0.0 collective-permute-done.2
  73.7 3.6 %collective-permute-start.3 = (bf16[32,1024]{1,0:T(8,128)(2,1)S(1)}, bf16[32,1024]{1,0:T(8,128)(2,1)S(1)}, u32[]{:S(2)}, u32[]{:S(2)}) collective-permute-start(bf16[32,1024]{1,0:T(8,128)(2,1)S(1)} %slice.25), channel_id=1, source_target_pairs={{0,32},{32,0},{1,33},{33,1},{2,34},{34,2},{3,35},{35,3},{4,36},{36... | collective-permute-start | bytes 196616 | tf_op jit(solution)/shard_map/ppermute | solution.py:329
  77.4 2.5 %shard_map.99 = bf16[512,1024]{1,0:T(8,128)(2,1)} custom-call(bf16[8,128,512]{2,1,0:T(8,128)(2,1)S(1)} %all-to-all-done.2.msg_ref, bf16[8,128,128]{2,1,0:T(8,128)(2,1)} %left_hbm.1), custom_call_target="tpu_custom_call" | custom-call | flops 134000000 | bytes 3145728 | tf_op jit(solution)/shard_map/pallas_call | solution.py:275
  79.9 0.0 collective-permute-done.1.up_far_ref
  79.9 0.2 collective-permute-done.3.down_far_ref
  80.1 0.8 shard_map.98
  80.9 0.0 all-to-all-done.3.msg_ref
  80.9 17.2 %all-to-all-start.4 = ((bf16[16,2,5120]{2,1,0:T(2,128)(2,1)}), bf16[16,2,5120]{2,1,0:T(2,128)(2,1)S(1)}, u32[]{:S(2)}, u32[]{:S(2)}) async-start(bf16[16,2,5120]{2,1,0:T(2,128)(2,1)} %shard_map.98), calls=%async_computation.4 | async-start | bytes 655360 | tf_op jit(solution)/shard_map/all_to_all | solution.py:372
  98.1 2.5 %shard_map.100 = bf16[512,1024]{1,0:T(8,128)(2,1)} custom-call(bf16[8,128,512]{2,1,0:T(8,128)(2,1)S(1)} %all-to-all-done.3.msg_ref, bf16[8,128,128]{2,1,0:T(8,128)(2,1)} %right_hbm.1), custom_call_target="tpu_custom_call" | custom-call | flops 300000000 | bytes 3145728 | tf_op jit(solution)/shard_map/pallas_call | solution.py:287
  100.6 21.5 %all-to-all-done.4.in_ref = bf16[16,2,5120]{2,1,0:T(2,128)(2,1)S(1)} async-done(((bf16[16,2,5120]{2,1,0:T(2,128)(2,1)}), bf16[16,2,5120]{2,1,0:T(2,128)(2,1)S(1)}, u32[]{:S(2)}, u32[]{:S(2)}) %all-to-all-start.4) | async-done | bytes 327712 | tf_op jit(solution)/shard_map/all_to_all | solution.py:372
  122.2 0.7 shard_map.101
  (5 shorter events, 0.1 us)
Async XLA Ops:
  3.6 19.5 %all-to-all-start.1 = ((bf16[8,128,512]{2,1,0:T(8,128)(2,1)}), bf16[8,128,512]{2,1,0:T(8,128)(2,1)S(1)}, u32[]{:S(2)}, u32[]{:S(2)}) async-start(bf16[8,128,512]{2,1,0:T(8,128)(2,1)} %shard_map.94), calls=%async_computation.1 | async-start | bytes 2097152 | tf_op jit(solution)/shard_map/all_to_all | solution.py:299
  23.1 17.4 %all-to-all-start = ((bf16[8,128,512]{2,1,0:T(8,128)(2,1)}), bf16[8,128,512]{2,1,0:T(8,128)(2,1)S(1)}, u32[]{:S(2)}, u32[]{:S(2)}) async-start(bf16[8,128,512]{2,1,0:T(8,128)(2,1)} %shard_map.93), calls=%async_computation | async-start | bytes 2097152 | tf_op jit(solution)/shard_map/all_to_all | solution.py:299
  40.5 19.3 %all-to-all-start.2 = ((bf16[8,128,512]{2,1,0:T(8,128)(2,1)}), bf16[8,128,512]{2,1,0:T(8,128)(2,1)S(1)}, u32[]{:S(2)}, u32[]{:S(2)}) async-start(bf16[8,128,512]{2,1,0:T(8,128)(2,1)} %get-tuple-element.21), calls=%async_computation.2 | async-start | bytes 2097152 | tf_op jit(solution)/shard_map/all_to_all | solution.py:299
  54.8 16.8 %collective-permute-start = (bf16[64,4096]{1,0:T(8,128)(2,1)}, bf16[64,4096]{1,0:T(8,128)(2,1)S(1)}, u32[]{:S(2)}, u32[]{:S(2)}) collective-permute-start(bf16[64,4096]{1,0:T(8,128)(2,1)} %get-tuple-element.20), channel_id=1, source_target_pairs={{0,32},{32,0},{1,33},{33,1},{2,34},{34,2},{3,35},{35,3},{4,36},{36... | collective-permute-start | bytes 1572872 | tf_op jit(solution)/shard_map/ppermute | solution.py:329
  59.8 21.1 %all-to-all-start.3 = ((bf16[8,128,512]{2,1,0:T(8,128)(2,1)}), bf16[8,128,512]{2,1,0:T(8,128)(2,1)S(1)}, u32[]{:S(2)}, u32[]{:S(2)}) async-start(bf16[8,128,512]{2,1,0:T(8,128)(2,1)} %get-tuple-element.24), calls=%async_computation.3 | async-start | bytes 2097152 | tf_op jit(solution)/shard_map/all_to_all | solution.py:299
  65.6 6.0 %copy-start = (f32[64,4096]{1,0:T(8,128)S(1)}, f32[64,4096]{1,0:T(8,128)}, u32[]{:S(2)}) copy-start(f32[64,4096]{1,0:T(8,128)} %get-tuple-element.19) | copy-start | bytes 3145732
  68.6 5.0 %collective-permute-start.2 = (bf16[64,1024]{1,0:T(8,128)(2,1)S(1)}, bf16[64,1024]{1,0:T(8,128)(2,1)S(1)}, u32[]{:S(2)}, u32[]{:S(2)}) collective-permute-start(bf16[64,1024]{1,0:T(8,128)(2,1)S(1)} %get-tuple-element.23), channel_id=1, source_target_pairs={{0,8},{8,0},{1,9},{9,1},{2,10},{10,2},{3,11},{11,3},{4,12},{12,4},... | collective-permute-start | bytes 393224 | tf_op jit(solution)/shard_map/ppermute | solution.py:329
  71.7 8.2 %collective-permute-start.1 = (bf16[32,4096]{1,0:T(8,128)(2,1)S(1)}, bf16[32,4096]{1,0:T(8,128)(2,1)S(1)}, u32[]{:S(2)}, u32[]{:S(2)}) collective-permute-start(bf16[32,4096]{1,0:T(8,128)(2,1)S(1)} %slice.24), channel_id=1, source_target_pairs={{0,8},{8,0},{1,9},{9,1},{2,10},{10,2},{3,11},{11,3},{4,12},{12,4},... | collective-permute-start | bytes 786440 | tf_op jit(solution)/shard_map/ppermute | solution.py:329
  73.7 6.4 %collective-permute-start.3 = (bf16[32,1024]{1,0:T(8,128)(2,1)S(1)}, bf16[32,1024]{1,0:T(8,128)(2,1)S(1)}, u32[]{:S(2)}, u32[]{:S(2)}) collective-permute-start(bf16[32,1024]{1,0:T(8,128)(2,1)S(1)} %slice.25), channel_id=1, source_target_pairs={{0,32},{32,0},{1,33},{33,1},{2,34},{34,2},{3,35},{35,3},{4,36},{36... | collective-permute-start | bytes 196616 | tf_op jit(solution)/shard_map/ppermute | solution.py:329
  80.9 41.2 %all-to-all-start.4 = ((bf16[16,2,5120]{2,1,0:T(2,128)(2,1)}), bf16[16,2,5120]{2,1,0:T(2,128)(2,1)S(1)}, u32[]{:S(2)}, u32[]{:S(2)}) async-start(bf16[16,2,5120]{2,1,0:T(2,128)(2,1)} %shard_map.98), calls=%async_computation.4 | async-start | bytes 655360 | tf_op jit(solution)/shard_map/all_to_all | solution.py:372

commit v8 on v7

--- a/solution.py
+++ b/solution.py
@@ -16,7 +16,7 @@
 PIECE = 16
 PAIR = 2
 UP_STEPS = (2, 0)
-DOWN_STEPS = (0, 2)
+DOWN_STEPS = (2, 0)
 SHARED = (5, 4, 3, 1)
 DP = ("z8", "z4", "z2", "z1", "far", "core")
 MIB = 1 << 20

time: 124 us -> 125 us (level)
  waiting for transfers between devices: 31.7 us -> 33.8 us
    all_to_all x1, waiting for transfers between devices: 21.5 us -> 23.5 us  [sum_over_dp(): lax.all_to_all(total, tuple((axis_of(bit) for bit in SHARED)), 0, 0, tile...]
  transfers between devices with their start and end apart: 9 -> 9, of which waited for: 5 -> 4; matrix products, arithmetic and copies ran while one was open for 0% -> 0% of each run, Pallas kernels for 26% -> 26%
where the time goes in v8:
time: 125 us; the launch traced here: 124 us
  starting transfers between devices  53.8 us (43%)
  Pallas kernels  35.8 us (29%)
  waiting for transfers between devices  33.8 us (27%)
    all_to_all x4, starting transfers between devices, exchange(): return lax.all_to_all(msg, 'blk', split_axis=0, concat_axis=0, tiled=True)  24.6 us
    all_to_all x1, waiting for transfers between devices, sum_over_dp(): lax.all_to_all(total, tuple((axis_of(bit) for bit in SHARED)), 0, 0, tile...  23.5 us
    all_to_all x1, starting transfers between devices, sum_over_dp(): lax.all_to_all(total, tuple((axis_of(bit) for bit in SHARED)), 0, 0, tile...  16.9 us
    ppermute x4, starting transfers between devices, swap_halves(): return lax.ppermute(send, axis_of(bit), [(0, 1), (1, 0)])  12.3 us
    pallas_call x1, Pallas kernels, up(): pl.pallas_call(up_kernel, grid=(OWNED,), out_shape=[far(MSG, BF16), far((...  10.9 us
    pallas_call x1, Pallas kernels, back(): pl.pallas_call(back_kernel, grid=(OWNED,), out_shape=[far(MSG, BF16), far...  9.5 us
    all_to_all x4, waiting for transfers between devices, exchange(): return lax.all_to_all(msg, 'blk', split_axis=0, concat_axis=0, tiled=True)  8.91 us
    pallas_call x2, Pallas kernels, right(): pl.pallas_call(functools.partial(right_kernel, dims), out_shape=far(MSG,...  5.9 us
  transfers between devices with their start and end apart: 9, of which 4 were waited for; matrix products, arithmetic and copies ran while one was open for 0% of the time, Pallas kernels for 26%

profile of v8, /device:TPU:8, one launch (start us, length us, event | category | flops | bytes accessed | tf_op | source)
XLA Modules:
  0.0 124.4 jit_solution(5507857505194802323)
XLA Ops:
  0.6 3.0 %shard_map.94 = bf16[8,128,512]{2,1,0:T(8,128)(2,1)} custom-call(bf16[512,1024]{1,0:T(8,128)(2,1)} %x_hbm.3, bf16[8,128,128]{2,1,0:T(8,128)(2,1)} %right_hbm.1), custom_call_target="tpu_custom_call" | custom-call | flops 134000000 | bytes 3145728 | tf_op jit(solution)/shard_map/pallas_call | solution.py:223
  3.6 9.3 %all-to-all-start.1 = ((bf16[8,128,512]{2,1,0:T(8,128)(2,1)}), bf16[8,128,512]{2,1,0:T(8,128)(2,1)S(1)}, u32[]{:S(2)}, u32[]{:S(2)}) async-start(bf16[8,128,512]{2,1,0:T(8,128)(2,1)} %shard_map.94), calls=%async_computation.1 | async-start | bytes 2097152 | tf_op jit(solution)/shard_map/all_to_all | solution.py:299
  12.9 2.9 %shard_map.93 = bf16[8,128,512]{2,1,0:T(8,128)(2,1)} custom-call(bf16[512,1024]{1,0:T(8,128)(2,1)} %cot_hbm.1, bf16[8,128,128]{2,1,0:T(8,128)(2,1)} %left_hbm.1), custom_call_target="tpu_custom_call" | custom-call | flops 134000000 | bytes 3145728 | tf_op jit(solution)/shard_map/pallas_call | solution.py:223
  15.8 7.3 %all-to-all-done.1.msg_ref = bf16[8,128,512]{2,1,0:T(8,128)(2,1)S(1)} async-done(((bf16[8,128,512]{2,1,0:T(8,128)(2,1)}), bf16[8,128,512]{2,1,0:T(8,128)(2,1)S(1)}, u32[]{:S(2)}, u32[]{:S(2)}) %all-to-all-start.1) | async-done | bytes 1048608 | tf_op jit(solution)/shard_map/all_to_all | solution.py:299
  23.1 4.8 %all-to-all-start = ((bf16[8,128,512]{2,1,0:T(8,128)(2,1)}), bf16[8,128,512]{2,1,0:T(8,128)(2,1)S(1)}, u32[]{:S(2)}, u32[]{:S(2)}) async-start(bf16[8,128,512]{2,1,0:T(8,128)(2,1)} %shard_map.93), calls=%async_computation | async-start | bytes 2097152 | tf_op jit(solution)/shard_map/all_to_all | solution.py:299
  27.9 10.9 %shard_map.95 = (bf16[8,128,512]{2,1,0:T(8,128)(2,1)}, bf16[8,128,512]{2,1,0:T(8,128)(2,1)}, bf16[8,512,512]{2,1,0:T(8,128)(2,1)}) custom-call(s32[1]{0:T(128)} %bitcast.place_ref, bf16[8,128,512]{2,1,0:T(8,128)(2,1)S(1)} %all-to-all-done.1.msg_ref, bf16[8,128,512]{2,1,0:T(8,128)(2,1)} %left_ref.3, bf16[8,512,128]{2,1,0:T(8,128)(2,1)} %down_ref.3), custom_call_target="tpu_custom_call" | custom-call | flops 1300000000 | bytes 9437184 | tf_op jit(solution)/shard_map/pallas_call | solution.py:235
  38.9 1.6 %all-to-all-done.msg_ref = bf16[8,128,512]{2,1,0:T(8,128)(2,1)S(1)} async-done(((bf16[8,128,512]{2,1,0:T(8,128)(2,1)}), bf16[8,128,512]{2,1,0:T(8,128)(2,1)S(1)}, u32[]{:S(2)}, u32[]{:S(2)}) %all-to-all-start) | async-done | bytes 1048608 | tf_op jit(solution)/shard_map/all_to_all | solution.py:299
  40.5 4.8 %all-to-all-start.2 = ((bf16[8,128,512]{2,1,0:T(8,128)(2,1)}), bf16[8,128,512]{2,1,0:T(8,128)(2,1)S(1)}, u32[]{:S(2)}, u32[]{:S(2)}) async-start(bf16[8,128,512]{2,1,0:T(8,128)(2,1)} %get-tuple-element.21), calls=%async_computation.2 | async-start | bytes 2097152 | tf_op jit(solution)/shard_map/all_to_all | solution.py:299
  45.3 9.5 %shard_map.96 = (bf16[8,128,512]{2,1,0:T(8,128)(2,1)}, bf16[64,4096]{1,0:T(8,128)(2,1)}, f32[64,4096]{1,0:T(8,128)}) custom-call(bf16[8,128,512]{2,1,0:T(8,128)(2,1)S(1)} %all-to-all-done.msg_ref, bf16[8,128,512]{2,1,0:T(8,128)(2,1)} %get-tuple-element.17.saved_ref, bf16[8,512,512]{2,1,0:T(8,128)(2,1)} %get-tuple-element.18.slope_ref, ...), custom_call_target="tpu_custom_call" | custom-call | flops 1800000000 | bytes 11534336 | tf_op jit(solution)/shard_map/pallas_call | solution.py:249
  54.8 5.0 %collective-permute-start = (bf16[64,4096]{1,0:T(8,128)(2,1)}, bf16[64,4096]{1,0:T(8,128)(2,1)S(1)}, u32[]{:S(2)}, u32[]{:S(2)}) collective-permute-start(bf16[64,4096]{1,0:T(8,128)(2,1)} %get-tuple-element.20), channel_id=1, source_target_pairs={{0,32},{32,0},{1,33},{33,1},{2,34},{34,2},{3,35},{35,3},{4,36},{36... | collective-permute-start | bytes 1572872 | tf_op jit(solution)/shard_map/ppermute | solution.py:329
  59.8 0.0 all-to-all-done.2.msg_ref
  59.8 5.7 %all-to-all-start.3 = ((bf16[8,128,512]{2,1,0:T(8,128)(2,1)}), bf16[8,128,512]{2,1,0:T(8,128)(2,1)S(1)}, u32[]{:S(2)}, u32[]{:S(2)}) async-start(bf16[8,128,512]{2,1,0:T(8,128)(2,1)} %get-tuple-element.24), calls=%async_computation.3 | async-start | bytes 2097152 | tf_op jit(solution)/shard_map/all_to_all | solution.py:299
  65.6 0.0 copy-start
  65.6 3.0 %shard_map.97 = (bf16[64,1024]{1,0:T(8,128)(2,1)S(1)}, f32[64,1024]{1,0:T(8,128)S(1)}) custom-call(s32[1]{0:T(128)} %bitcast.place_ref, bf16[8,128,512]{2,1,0:T(8,128)(2,1)S(1)} %all-to-all-done.2.msg_ref, bf16[512,1024]{1,0:T(8,128)(2,1)} %cot_hbm.1), custom_call_target="tpu_custom_call" | custom-call | flops 3000000000 | bytes 16777216 | tf_op jit(solution)/shard_map/pallas_call | solution.py:263
  68.6 3.4 %collective-permute-start.2 = (bf16[64,1024]{1,0:T(8,128)(2,1)S(1)}, bf16[64,1024]{1,0:T(8,128)(2,1)S(1)}, u32[]{:S(2)}, u32[]{:S(2)}) collective-permute-start(bf16[64,1024]{1,0:T(8,128)(2,1)S(1)} %get-tuple-element.23), channel_id=1, source_target_pairs={{0,32},{32,0},{1,33},{33,1},{2,34},{34,2},{3,35},{35,3},{4,36},{36... | collective-permute-start | bytes 393224 | tf_op jit(solution)/shard_map/ppermute | solution.py:329
  72.0 0.0 collective-permute-done
  72.0 0.0 copy-done
  72.1 0.1 convert_add_fusion
  72.2 1.9 %collective-permute-start.1 = (bf16[32,4096]{1,0:T(8,128)(2,1)S(1)}, bf16[32,4096]{1,0:T(8,128)(2,1)S(1)}, u32[]{:S(2)}, u32[]{:S(2)}) collective-permute-start(bf16[32,4096]{1,0:T(8,128)(2,1)S(1)} %slice.24), channel_id=1, source_target_pairs={{0,8},{8,0},{1,9},{9,1},{2,10},{10,2},{3,11},{11,3},{4,12},{12,4},... | collective-permute-start | bytes 786440 | tf_op jit(solution)/shard_map/ppermute | solution.py:329
  74.1 1.4 %collective-permute-done.2 = bf16[64,1024]{1,0:T(8,128)(2,1)S(1)} collective-permute-done((bf16[64,1024]{1,0:T(8,128)(2,1)S(1)}, bf16[64,1024]{1,0:T(8,128)(2,1)S(1)}, u32[]{:S(2)}, u32[]{:S(2)}) %collective-permute-start.2) | collective-permute-done | bytes 131104 | tf_op jit(solution)/shard_map/ppermute | solution.py:329
  75.5 1.9 %collective-permute-start.3 = (bf16[32,1024]{1,0:T(8,128)(2,1)S(1)}, bf16[32,1024]{1,0:T(8,128)(2,1)S(1)}, u32[]{:S(2)}, u32[]{:S(2)}) collective-permute-start(bf16[32,1024]{1,0:T(8,128)(2,1)S(1)} %slice.25), channel_id=1, source_target_pairs={{0,8},{8,0},{1,9},{9,1},{2,10},{10,2},{3,11},{11,3},{4,12},{12,4},... | collective-permute-start | bytes 196616 | tf_op jit(solution)/shard_map/ppermute | solution.py:329
  77.5 2.5 %shard_map.99 = bf16[512,1024]{1,0:T(8,128)(2,1)} custom-call(bf16[8,128,512]{2,1,0:T(8,128)(2,1)S(1)} %all-to-all-done.2.msg_ref, bf16[8,128,128]{2,1,0:T(8,128)(2,1)} %left_hbm.1), custom_call_target="tpu_custom_call" | custom-call | flops 134000000 | bytes 3145728 | tf_op jit(solution)/shard_map/pallas_call | solution.py:275
  80.0 0.0 collective-permute-done.1.up_far_ref
  80.0 0.0 collective-permute-done.3.down_far_ref
  80.0 0.8 shard_map.98
  80.9 0.0 all-to-all-done.3.msg_ref
  80.9 16.9 %all-to-all-start.4 = ((bf16[16,2,5120]{2,1,0:T(2,128)(2,1)}), bf16[16,2,5120]{2,1,0:T(2,128)(2,1)S(1)}, u32[]{:S(2)}, u32[]{:S(2)}) async-start(bf16[16,2,5120]{2,1,0:T(2,128)(2,1)} %shard_map.98), calls=%async_computation.4 | async-start | bytes 655360 | tf_op jit(solution)/shard_map/all_to_all | solution.py:372
  97.8 2.5 %shard_map.100 = bf16[512,1024]{1,0:T(8,128)(2,1)} custom-call(bf16[8,128,512]{2,1,0:T(8,128)(2,1)S(1)} %all-to-all-done.3.msg_ref, bf16[8,128,128]{2,1,0:T(8,128)(2,1)} %right_hbm.1), custom_call_target="tpu_custom_call" | custom-call | flops 300000000 | bytes 3145728 | tf_op jit(solution)/shard_map/pallas_call | solution.py:287
  100.3 23.5 %all-to-all-done.4.in_ref = bf16[16,2,5120]{2,1,0:T(2,128)(2,1)S(1)} async-done(((bf16[16,2,5120]{2,1,0:T(2,128)(2,1)}), bf16[16,2,5120]{2,1,0:T(2,128)(2,1)S(1)}, u32[]{:S(2)}, u32[]{:S(2)}) %all-to-all-start.4) | async-done | bytes 327712 | tf_op jit(solution)/shard_map/all_to_all | solution.py:372
  123.8 0.7 shard_map.101
  (5 shorter events, 0.1 us)
Async XLA Ops:
  3.6 19.5 %all-to-all-start.1 = ((bf16[8,128,512]{2,1,0:T(8,128)(2,1)}), bf16[8,128,512]{2,1,0:T(8,128)(2,1)S(1)}, u32[]{:S(2)}, u32[]{:S(2)}) async-start(bf16[8,128,512]{2,1,0:T(8,128)(2,1)} %shard_map.94), calls=%async_computation.1 | async-start | bytes 2097152 | tf_op jit(solution)/shard_map/all_to_all | solution.py:299
  23.1 17.4 %all-to-all-start = ((bf16[8,128,512]{2,1,0:T(8,128)(2,1)}), bf16[8,128,512]{2,1,0:T(8,128)(2,1)S(1)}, u32[]{:S(2)}, u32[]{:S(2)}) async-start(bf16[8,128,512]{2,1,0:T(8,128)(2,1)} %shard_map.93), calls=%async_computation | async-start | bytes 2097152 | tf_op jit(solution)/shard_map/all_to_all | solution.py:299
  40.5 19.3 %all-to-all-start.2 = ((bf16[8,128,512]{2,1,0:T(8,128)(2,1)}), bf16[8,128,512]{2,1,0:T(8,128)(2,1)S(1)}, u32[]{:S(2)}, u32[]{:S(2)}) async-start(bf16[8,128,512]{2,1,0:T(8,128)(2,1)} %get-tuple-element.21), calls=%async_computation.2 | async-start | bytes 2097152 | tf_op jit(solution)/shard_map/all_to_all | solution.py:299
  54.8 17.2 %collective-permute-start = (bf16[64,4096]{1,0:T(8,128)(2,1)}, bf16[64,4096]{1,0:T(8,128)(2,1)S(1)}, u32[]{:S(2)}, u32[]{:S(2)}) collective-permute-start(bf16[64,4096]{1,0:T(8,128)(2,1)} %get-tuple-element.20), channel_id=1, source_target_pairs={{0,32},{32,0},{1,33},{33,1},{2,34},{34,2},{3,35},{35,3},{4,36},{36... | collective-permute-start | bytes 1572872 | tf_op jit(solution)/shard_map/ppermute | solution.py:329
  59.8 21.0 %all-to-all-start.3 = ((bf16[8,128,512]{2,1,0:T(8,128)(2,1)}), bf16[8,128,512]{2,1,0:T(8,128)(2,1)S(1)}, u32[]{:S(2)}, u32[]{:S(2)}) async-start(bf16[8,128,512]{2,1,0:T(8,128)(2,1)} %get-tuple-element.24), calls=%async_computation.3 | async-start | bytes 2097152 | tf_op jit(solution)/shard_map/all_to_all | solution.py:299
  65.6 6.5 %copy-start = (f32[64,4096]{1,0:T(8,128)S(1)}, f32[64,4096]{1,0:T(8,128)}, u32[]{:S(2)}) copy-start(f32[64,4096]{1,0:T(8,128)} %get-tuple-element.19) | copy-start | bytes 3145732
  68.6 6.9 %collective-permute-start.2 = (bf16[64,1024]{1,0:T(8,128)(2,1)S(1)}, bf16[64,1024]{1,0:T(8,128)(2,1)S(1)}, u32[]{:S(2)}, u32[]{:S(2)}) collective-permute-start(bf16[64,1024]{1,0:T(8,128)(2,1)S(1)} %get-tuple-element.23), channel_id=1, source_target_pairs={{0,32},{32,0},{1,33},{33,1},{2,34},{34,2},{3,35},{35,3},{4,36},{36... | collective-permute-start | bytes 393224 | tf_op jit(solution)/shard_map/ppermute | solution.py:329
  72.2 7.8 %collective-permute-start.1 = (bf16[32,4096]{1,0:T(8,128)(2,1)S(1)}, bf16[32,4096]{1,0:T(8,128)(2,1)S(1)}, u32[]{:S(2)}, u32[]{:S(2)}) collective-permute-start(bf16[32,4096]{1,0:T(8,128)(2,1)S(1)} %slice.24), channel_id=1, source_target_pairs={{0,8},{8,0},{1,9},{9,1},{2,10},{10,2},{3,11},{11,3},{4,12},{12,4},... | collective-permute-start | bytes 786440 | tf_op jit(solution)/shard_map/ppermute | solution.py:329
  75.5 4.5 %collective-permute-start.3 = (bf16[32,1024]{1,0:T(8,128)(2,1)S(1)}, bf16[32,1024]{1,0:T(8,128)(2,1)S(1)}, u32[]{:S(2)}, u32[]{:S(2)}) collective-permute-start(bf16[32,1024]{1,0:T(8,128)(2,1)S(1)} %slice.25), channel_id=1, source_target_pairs={{0,8},{8,0},{1,9},{9,1},{2,10},{10,2},{3,11},{11,3},{4,12},{12,4},... | collective-permute-start | bytes 196616 | tf_op jit(solution)/shard_map/ppermute | solution.py:329
  80.9 42.9 %all-to-all-start.4 = ((bf16[16,2,5120]{2,1,0:T(2,128)(2,1)}), bf16[16,2,5120]{2,1,0:T(2,128)(2,1)S(1)}, u32[]{:S(2)}, u32[]{:S(2)}) async-start(bf16[16,2,5120]{2,1,0:T(2,128)(2,1)} %shard_map.98), calls=%async_computation.4 | async-start | bytes 655360 | tf_op jit(solution)/shard_map/all_to_all | solution.py:372
